TPU v7x, 256 devices: a whole 4x4x8 slice. The times are simulated.
256 devices in a mesh: ctx: 16 (over z_hi, y, core), head: 16 (over z_lo, x).
Axes of the slice: x: 4, y: 4, z: 8 (z_hi: 2, z_lo: 4; z = z_hi * 4 + z_lo), core: 2. Of those that a mesh axis runs over, the one named last changes fastest.
Arguments:
- queries: bfloat16 [32768, 2048], P(('ctx', 'head')), may hold values from -10 to 10
- keys: bfloat16 [32768, 2048], P(('ctx', 'head')), may hold values from -10 to 10
- values: bfloat16 [32768, 2048], P(('ctx', 'head')), may hold values from -6 to 6
- out_grad: bfloat16 [32768, 2048], P(('ctx', 'head')), may hold values from -6 to 6
- key_lists: int32 [256, 4], replicated, may hold values from 0 to 255, as said below
Outputs:
- attended: bfloat16 [32768, 2048], P(('ctx', 'head'))
- query_grad: bfloat16 [32768, 2048], P(('ctx', 'head'))
- key_grad: bfloat16 [32768, 2048], P(('ctx', 'head'))
- value_grad: bfloat16 [32768, 2048], P(('ctx', 'head'))
Inputs may be any that keep to these rules, and one draw needn't show every extreme that they name: `key_lists`: row n lists block n in slot 0 and block (n - 1) mod 256 in slot 1; slots 2 and 3 name blocks of slabs other than n's own slab of 16 blocks. Over the 32 entries in slots 2 and 3 of one slab's rows, each other slab is named floor or ceil of 2 * 16 / 15 times, some slab exactly 3 times.
All inputs are finite; a program needn't handle non-finite values.
Results may differ from a plain program's by a relative error of at most 0.029.
Values may be sent and summed in bfloat16 or wider, within the bound.
No kernel may reach another device: no remote copies, remote signals or barrier semaphores. Data moves between devices by JAX's collectives and lax.ppermute only.
A program may use at most 128 MiB of HBM per device.

v0:
```python
import jax
import jax.numpy as jnp
from jax import lax
from jax.sharding import PartitionSpec as P

HEAD_DIM = 128
BLOCK = 128
SLOTS = 4


def from_behind(array, axis, by):
    size = lax.axis_size(axis)
    return lax.ppermute(array, axis, [(i, (i + by) % size) for i in range(size)])


def select_blocks(local_blocks, edge_block, far_blocks, pool_index, block_shape):
    pool = jnp.concatenate(
        [local_blocks, edge_block[None], far_blocks.reshape((-1,) + local_blocks.shape[1:])], axis=0
    )
    chosen = pool[pool_index]
    return chosen.reshape(
        block_shape[0], pool_index.shape[1] * BLOCK, block_shape[2], block_shape[3]
    )


def block_scores(query_blocks, listed_keys, score_scale):
    return (
        jnp.einsum("qbhd,qkhd->qhbk", query_blocks, listed_keys, preferred_element_type=jnp.float32)
        * score_scale
    )


def body(queries, keys, values, out_grad, key_lists):
    ctx_count = lax.axis_size("ctx")
    ctx_rank = lax.axis_index("ctx")
    score_scale = HEAD_DIM ** (-0.5)
    highest = lax.Precision.HIGHEST
    q_slab, k_slab, v_slab, g_slab = (
        lax.all_to_all(queries, "head", split_axis=1, concat_axis=0, tiled=True),
        lax.all_to_all(keys, "head", split_axis=1, concat_axis=0, tiled=True),
        lax.all_to_all(values, "head", split_axis=1, concat_axis=0, tiled=True),
        lax.all_to_all(out_grad, "head", split_axis=1, concat_axis=0, tiled=True),
    )
    slab_len, features = q_slab.shape
    heads_dev = features // HEAD_DIM
    blocks = slab_len // BLOCK
    requests = 2 * blocks
    capacity = (requests + ctx_count - 2) // (ctx_count - 1)
    block_shape = (blocks, BLOCK, heads_dev, HEAD_DIM)
    q_blocks = q_slab.reshape(block_shape)
    g_blocks = g_slab.reshape(block_shape)
    k_local = k_slab.reshape(blocks, BLOCK, features)
    v_local = v_slab.reshape(blocks, BLOCK, features)
    far_all = key_lists[:, 2:].reshape(ctx_count, requests)
    wanted = far_all // blocks == ctx_rank
    slot_rank = jnp.cumsum(wanted.astype(jnp.int32), axis=1) - 1
    chosen = wanted[:, None, :] & (
        slot_rank[:, None, :] == jnp.arange(capacity, dtype=jnp.int32)[None, :, None]
    )
    send_index = jnp.sum(jnp.where(chosen, far_all[:, None, :] % blocks, 0), axis=2).reshape(-1)
    send_valid = jnp.any(chosen, axis=2).reshape(-1)
    own_lists = lax.dynamic_slice_in_dim(key_lists, ctx_rank * blocks, blocks, 0)
    my_far = own_lists[:, 2:].reshape(requests)
    my_source = my_far // blocks
    owner_hot = (my_source[:, None] == jnp.arange(ctx_count, dtype=jnp.int32)[None, :]).astype(
        jnp.int32
    )
    my_rank = jnp.sum((jnp.cumsum(owner_hot, axis=0) - 1) * owner_hot, axis=1)
    my_slot = my_source * capacity + my_rank
    block_ids = jnp.arange(blocks, dtype=jnp.int32)
    before = jnp.where(block_ids > 0, block_ids - 1, blocks)
    pool_index = jnp.concatenate(
        [block_ids[:, None], before[:, None], (blocks + 1 + my_slot).reshape(blocks, 2)], axis=1
    )
    landing = ((send_index[None, :] == block_ids[:, None]) & send_valid[None, :]).astype(
        jnp.float32
    )
    edge_k, edge_v = from_behind((k_local[blocks - 1], v_local[blocks - 1]), "ctx", 1)
    send_k = k_local[send_index].reshape(ctx_count, capacity, BLOCK, features)
    send_v = v_local[send_index].reshape(ctx_count, capacity, BLOCK, features)
    got_k, got_v = (
        lax.all_to_all(send_k, "ctx", split_axis=0, concat_axis=0, tiled=True),
        lax.all_to_all(send_v, "ctx", split_axis=0, concat_axis=0, tiled=True),
    )
    listed_keys = select_blocks(k_local, edge_k, got_k, pool_index, block_shape)
    listed_values = select_blocks(v_local, edge_v, got_v, pool_index, block_shape)
    scores = block_scores(q_blocks, listed_keys, score_scale)
    row_max = jnp.max(scores, axis=-1, keepdims=True)
    weights = jnp.exp(scores - row_max)
    row_sum = jnp.sum(weights, axis=-1, keepdims=True)
    probs = weights / row_sum
    probs_low = probs.astype(jnp.bfloat16)
    attended = jnp.einsum(
        "qhbk,qkhd->qbhd", probs_low, listed_values, preferred_element_type=jnp.float32
    ).astype(jnp.bfloat16)
    row_delta = jnp.sum(
        g_blocks.astype(jnp.float32) * attended.astype(jnp.float32), axis=-1
    ).transpose(0, 2, 1)
    again_k, again_v = (
        lax.all_to_all(send_k, "ctx", split_axis=0, concat_axis=0, tiled=True),
        lax.all_to_all(send_v, "ctx", split_axis=0, concat_axis=0, tiled=True),
    )
    listed_keys = select_blocks(k_local, edge_k, again_k, pool_index, block_shape)
    listed_values = select_blocks(v_local, edge_v, again_v, pool_index, block_shape)
    probs = jnp.exp(block_scores(q_blocks, listed_keys, score_scale) - row_max) / row_sum
    probs_low = probs.astype(jnp.bfloat16)
    used_slots = SLOTS
    dprob = jnp.einsum(
        "qbhd,qkhd->qhbk", g_blocks, listed_values, preferred_element_type=jnp.float32
    )
    dscore = (probs * (dprob - row_delta[..., None]) * score_scale).astype(jnp.bfloat16)
    query_total = jnp.einsum(
        "qhbk,qkhd->qbhd", dscore, listed_keys, preferred_element_type=jnp.float32
    ).reshape(blocks, BLOCK, features)
    key_slots = jnp.einsum(
        "qhbk,qbhd->qkhd", dscore, q_blocks, preferred_element_type=jnp.float32
    ).reshape(blocks, used_slots, BLOCK, features)
    value_slots = jnp.einsum(
        "qhbk,qbhd->qkhd", probs_low, g_blocks, preferred_element_type=jnp.float32
    ).reshape(blocks, used_slots, BLOCK, features)
    key_sum = key_slots[:, 0] + jnp.concatenate(
        [key_slots[1:, 1], jnp.zeros_like(key_slots[:1, 1])], axis=0
    )
    value_sum = value_slots[:, 0] + jnp.concatenate(
        [value_slots[1:, 1], jnp.zeros_like(value_slots[:1, 1])], axis=0
    )
    back_k, back_v = (
        from_behind(key_slots[0, 1].astype(jnp.bfloat16), "ctx", -1).astype(jnp.float32),
        from_behind(value_slots[0, 1].astype(jnp.bfloat16), "ctx", -1).astype(jnp.float32),
    )
    key_sum = key_sum.at[blocks - 1].add(back_k)
    value_sum = value_sum.at[blocks - 1].add(back_v)
    slot_total = ctx_count * capacity
    empty = jnp.zeros((slot_total, BLOCK, features), jnp.float32)
    grad_keys = (
        empty.at[my_slot]
        .set(key_slots[:, 2:].reshape(requests, BLOCK, features))
        .reshape(ctx_count, capacity, BLOCK, features)
    )
    grad_values = (
        empty.at[my_slot]
        .set(value_slots[:, 2:].reshape(requests, BLOCK, features))
        .reshape(ctx_count, capacity, BLOCK, features)
    )
    home_k, home_v = (
        lax.all_to_all(
            grad_keys.astype(jnp.bfloat16), "ctx", split_axis=0, concat_axis=0, tiled=True
        ).astype(grad_keys.dtype),
        lax.all_to_all(
            grad_values.astype(jnp.bfloat16), "ctx", split_axis=0, concat_axis=0, tiled=True
        ).astype(grad_values.dtype),
    )
    key_sum = key_sum + jnp.dot(
        landing,
        home_k.reshape(slot_total, BLOCK * features),
        precision=highest,
        preferred_element_type=jnp.float32,
    ).reshape(blocks, BLOCK, features)
    value_sum = value_sum + jnp.dot(
        landing,
        home_v.reshape(slot_total, BLOCK * features),
        precision=highest,
        preferred_element_type=jnp.float32,
    ).reshape(blocks, BLOCK, features)
    results = (
        attended.reshape(slab_len, features),
        query_total.astype(jnp.bfloat16).reshape(slab_len, features),
        key_sum.astype(jnp.bfloat16).reshape(slab_len, features),
        value_sum.astype(jnp.bfloat16).reshape(slab_len, features),
    )
    return (
        lax.all_to_all(results[0], "head", split_axis=0, concat_axis=1, tiled=True),
        lax.all_to_all(results[1], "head", split_axis=0, concat_axis=1, tiled=True),
        lax.all_to_all(results[2], "head", split_axis=0, concat_axis=1, tiled=True),
        lax.all_to_all(results[3], "head", split_axis=0, concat_axis=1, tiled=True),
    )


def solution(mesh):
    placed = (
        P(("ctx", "head"), None),
        P(("ctx", "head"), None),
        P(("ctx", "head"), None),
        P(("ctx", "head"), None),
        P(),
    )
    return jax.shard_map(
        body,
        mesh=mesh,
        in_specs=placed,
        out_specs=(
            P(("ctx", "head"), None),
            P(("ctx", "head"), None),
            P(("ctx", "head"), None),
            P(("ctx", "head"), None),
        ),
        check_vma=False,
    )
```

profile of v0, /device:TPU:56, one launch (start us, length us, event | category | flops | bytes accessed | tf_op | source)
XLA Modules:
  0.0 366.1 jit_solution(5046689353949950767)
XLA Ops:
  3.0 8.6 %all-to-all-start = ((bf16[128,16,128]{2,0,1:T(8,128)(2,1)}), bf16[128,16,128]{2,0,1:T(8,128)(2,1)S(1)}, u32[]{:S(2)}, u32[]{:S(2)}) async-start(bf16[128,16,128]{2,0,1:T(8,128)(2,1)} %copy.148), calls=%async_computation | async-start | bytes 1048576 | tf_op jit(solution)/shard_map/all_to_all | solution.py:41
  12.9 13.5 %all-to-all-done = bf16[128,16,128]{2,0,1:T(8,128)(2,1)S(1)} async-done(((bf16[128,16,128]{2,0,1:T(8,128)(2,1)}), bf16[128,16,128]{2,0,1:T(8,128)(2,1)S(1)}, u32[]{:S(2)}, u32[]{:S(2)}) %all-to-all-start) | async-done | bytes 524320 | tf_op jit(solution)/shard_map/all_to_all | solution.py:41
  26.4 5.1 %all-to-all-start.2 = ((bf16[128,16,128]{2,0,1:T(8,128)(2,1)}), bf16[128,16,128]{2,0,1:T(8,128)(2,1)S(1)}, u32[]{:S(2)}, u32[]{:S(2)}) async-start(bf16[128,16,128]{2,0,1:T(8,128)(2,1)} %copy.156), calls=%async_computation.2 | async-start | bytes 1048576 | tf_op jit(solution)/shard_map/all_to_all | solution.py:40
  34.4 11.1 %all-to-all-done.2 = bf16[128,16,128]{2,0,1:T(8,128)(2,1)S(1)} async-done(((bf16[128,16,128]{2,0,1:T(8,128)(2,1)}), bf16[128,16,128]{2,0,1:T(8,128)(2,1)S(1)}, u32[]{:S(2)}, u32[]{:S(2)}) %all-to-all-start.2) | async-done | bytes 524320 | tf_op jit(solution)/shard_map/all_to_all | solution.py:40
  45.5 8.6 %all-to-all-start.1 = ((bf16[16,3,128,128]{3,2,1,0:T(8,128)(2,1)}), bf16[16,3,128,128]{3,2,1,0:T(8,128)(2,1)S(1)}, u32[]{:S(2)}, u32[]{:S(2)}) async-start(bf16[16,3,128,128]{3,2,1,0:T(8,128)(2,1)} %bitcast.203), calls=%async_computation.1 | async-start | bytes 3145728 | tf_op jit(solution)/shard_map/all_to_all | solution.py:83
  56.1 39.9 %all-to-all-done.1 = bf16[16,3,128,128]{3,2,1,0:T(8,128)(2,1)S(1)} async-done(((bf16[16,3,128,128]{3,2,1,0:T(8,128)(2,1)}), bf16[16,3,128,128]{3,2,1,0:T(8,128)(2,1)S(1)}, u32[]{:S(2)}, u32[]{:S(2)}) %all-to-all-start.1) | async-done | bytes 1572896 | tf_op jit(solution)/shard_map/all_to_all | solution.py:83
  96.0 5.3 %all-to-all-start.3 = ((bf16[16,3,128,128]{3,2,1,0:T(8,128)(2,1)}), bf16[16,3,128,128]{3,2,1,0:T(8,128)(2,1)}, u32[]{:S(2)}, u32[]{:S(2)}) async-start(bf16[16,3,128,128]{3,2,1,0:T(8,128)(2,1)} %bitcast.201), calls=%async_computation.3 | async-start | bytes 3145728 | tf_op jit(solution)/shard_map/all_to_all | solution.py:82
  105.5 36.2 %all-to-all-done.3 = bf16[16,3,128,128]{3,2,1,0:T(8,128)(2,1)} async-done(((bf16[16,3,128,128]{3,2,1,0:T(8,128)(2,1)}), bf16[16,3,128,128]{3,2,1,0:T(8,128)(2,1)}, u32[]{:S(2)}, u32[]{:S(2)}) %all-to-all-start.3) | async-done | bytes 1572896 | tf_op jit(solution)/shard_map/all_to_all | solution.py:82
  141.7 4.7 %all-to-all-start.4 = ((bf16[128,16,128]{2,0,1:T(8,128)(2,1)}), bf16[128,16,128]{2,0,1:T(8,128)(2,1)}, u32[]{:S(2)}, u32[]{:S(2)}) async-start(bf16[128,16,128]{2,0,1:T(8,128)(2,1)} %copy.158), calls=%async_computation.4 | async-start | bytes 1048576 | tf_op jit(solution)/shard_map/all_to_all | solution.py:39
  163.1 5.1 %all-to-all-start.6 = ((bf16[128,16,128]{0,2,1:T(8,128)(2,1)}), bf16[128,16,128]{0,2,1:T(8,128)(2,1)S(1)}, u32[]{:S(2)}, u32[]{:S(2)}) async-start(bf16[128,16,128]{0,2,1:T(8,128)(2,1)} %bitcast.26), calls=%async_computation.6 | async-start | bytes 1048576 | tf_op jit(solution)/shard_map/all_to_all | solution.py:42
  175.1 5.5 %all-to-all-done.6 = bf16[128,16,128]{0,2,1:T(8,128)(2,1)S(1)} async-done(((bf16[128,16,128]{0,2,1:T(8,128)(2,1)}), bf16[128,16,128]{0,2,1:T(8,128)(2,1)S(1)}, u32[]{:S(2)}, u32[]{:S(2)}) %all-to-all-start.6) | async-done | bytes 524320 | tf_op jit(solution)/shard_map/all_to_all | solution.py:42
  184.0 7.4 %all-to-all-start.5 = ((bf16[16,128,128]{1,2,0:T(8,128)(2,1)}), bf16[16,128,128]{1,2,0:T(8,128)(2,1)S(1)}, u32[]{:S(2)}, u32[]{:S(2)}) async-start(bf16[16,128,128]{1,2,0:T(8,128)(2,1)} %bitcast.23), calls=%async_computation.5 | async-start | bytes 1048576 | tf_op jit(solution)/shard_map/all_to_all | solution.py:172
  196.9 10.3 %all-to-all-done.5 = bf16[16,128,128]{1,2,0:T(8,128)(2,1)S(1)} async-done(((bf16[16,128,128]{1,2,0:T(8,128)(2,1)}), bf16[16,128,128]{1,2,0:T(8,128)(2,1)S(1)}, u32[]{:S(2)}, u32[]{:S(2)}) %all-to-all-start.5) | async-done | bytes 524320 | tf_op jit(solution)/shard_map/all_to_all | solution.py:172
  207.2 5.2 %all-to-all-start.7 = ((bf16[16,128,128]{1,2,0:T(8,128)(2,1)}), bf16[16,128,128]{1,2,0:T(8,128)(2,1)}, u32[]{:S(2)}, u32[]{:S(2)}) async-start(bf16[16,128,128]{1,2,0:T(8,128)(2,1)} %fusion.28), calls=%async_computation.7 | async-start | bytes 1048576 | tf_op jit(solution)/shard_map/all_to_all | solution.py:173
  222.7 4.8 %all-to-all-done.7 = bf16[16,128,128]{1,2,0:T(8,128)(2,1)} async-done(((bf16[16,128,128]{1,2,0:T(8,128)(2,1)}), bf16[16,128,128]{1,2,0:T(8,128)(2,1)}, u32[]{:S(2)}, u32[]{:S(2)}) %all-to-all-start.7) | async-done | bytes 524320 | tf_op jit(solution)/shard_map/all_to_all | solution.py:173
  227.5 7.1 %all-to-all-start.8 = ((bf16[16,3,128,128]{3,2,1,0:T(8,128)(2,1)}), bf16[16,3,128,128]{3,2,1,0:T(8,128)(2,1)}, u32[]{:S(2)}, u32[]{:S(2)}) async-start(bf16[16,3,128,128]{3,2,1,0:T(8,128)(2,1)} %bitcast.202), calls=%async_computation.8 | async-start | bytes 3145728 | tf_op jit(solution)/shard_map/all_to_all | solution.py:146
  243.9 32.5 %all-to-all-done.8 = bf16[16,3,128,128]{3,2,1,0:T(8,128)(2,1)} async-done(((bf16[16,3,128,128]{3,2,1,0:T(8,128)(2,1)}), bf16[16,3,128,128]{3,2,1,0:T(8,128)(2,1)}, u32[]{:S(2)}, u32[]{:S(2)}) %all-to-all-start.8) | async-done | bytes 1572896 | tf_op jit(solution)/shard_map/all_to_all | solution.py:146
  276.4 4.9 %all-to-all-start.10 = ((bf16[16,3,128,128]{3,2,1,0:T(8,128)(2,1)}), bf16[16,3,128,128]{3,2,1,0:T(8,128)(2,1)S(1)}, u32[]{:S(2)}, u32[]{:S(2)}) async-start(bf16[16,3,128,128]{3,2,1,0:T(8,128)(2,1)} %bitcast.200), calls=%async_computation.10 | async-start | bytes 3145728 | tf_op jit(solution)/shard_map/all_to_all | solution.py:149
  286.5 4.6 %collective-permute-done.2 = bf16[128,128]{1,0:T(8,128)(2,1)S(1)} collective-permute-done((bf16[128,128]{1,0:T(8,128)(2,1)S(1)}, bf16[128,128]{1,0:T(8,128)(2,1)S(1)}, u32[]{:S(2)}, u32[]{:S(2)}) %collective-permute-start.2) | collective-permute-done | bytes 32800 | tf_op jit(solution)/shard_map/ppermute | solution.py:13
  295.9 28.0 %all-to-all-done.10 = bf16[16,3,128,128]{3,2,1,0:T(8,128)(2,1)S(1)} async-done(((bf16[16,3,128,128]{3,2,1,0:T(8,128)(2,1)}), bf16[16,3,128,128]{3,2,1,0:T(8,128)(2,1)S(1)}, u32[]{:S(2)}, u32[]{:S(2)}) %all-to-all-start.10) | async-done | bytes 1572896 | tf_op jit(solution)/shard_map/all_to_all | solution.py:149
  323.9 5.9 %all-to-all-start.9 = ((bf16[16,128,128]{2,1,0:T(8,128)(2,1)}), bf16[16,128,128]{2,1,0:T(8,128)(2,1)}, u32[]{:S(2)}, u32[]{:S(2)}) async-start(bf16[16,128,128]{2,1,0:T(8,128)(2,1)} %copy.171), calls=%async_computation.9 | async-start | bytes 1048576 | tf_op jit(solution)/shard_map/all_to_all | solution.py:174
  337.4 6.9 %all-to-all-done.9 = bf16[16,128,128]{2,1,0:T(8,128)(2,1)} async-done(((bf16[16,128,128]{2,1,0:T(8,128)(2,1)}), bf16[16,128,128]{2,1,0:T(8,128)(2,1)}, u32[]{:S(2)}, u32[]{:S(2)}) %all-to-all-start.9) | async-done | bytes 524320 | tf_op jit(solution)/shard_map/all_to_all | solution.py:174
  344.3 6.0 %all-to-all-start.11 = ((bf16[16,128,128]{2,1,0:T(8,128)(2,1)}), bf16[16,128,128]{2,1,0:T(8,128)(2,1)S(1)}, u32[]{:S(2)}, u32[]{:S(2)}) async-start(bf16[16,128,128]{2,1,0:T(8,128)(2,1)} %copy.178), calls=%async_computation.11 | async-start | bytes 1048576 | tf_op jit(solution)/shard_map/all_to_all | solution.py:175
  355.7 9.0 %all-to-all-done.11 = bf16[16,128,128]{2,1,0:T(8,128)(2,1)S(1)} async-done(((bf16[16,128,128]{2,1,0:T(8,128)(2,1)}), bf16[16,128,128]{2,1,0:T(8,128)(2,1)S(1)}, u32[]{:S(2)}, u32[]{:S(2)}) %all-to-all-start.11) | async-done | bytes 524320 | tf_op jit(solution)/shard_map/all_to_all | solution.py:175
  (129 shorter events, 88.6 us)
Async XLA Ops:
  0.6 11.0 %copy-start.12 = (bf16[128,2048]{1,0:T(8,128)(2,1)S(1)}, bf16[128,2048]{1,0:T(8,128)(2,1)}, u32[]{:S(2)}) copy-start(bf16[128,2048]{1,0:T(8,128)(2,1)} %param.10) | copy-start | bytes 1572868
  3.0 28.5 %copy-start.14 = (s32[256,4]{0,1:T(4,128)S(1)}, s32[256,4]{0,1:T(4,128)}, u32[]{:S(2)}) copy-start(s32[256,4]{0,1:T(4,128)} %param.13) | copy-start | bytes 12292
  3.0 23.4 %all-to-all-start = ((bf16[128,16,128]{2,0,1:T(8,128)(2,1)}), bf16[128,16,128]{2,0,1:T(8,128)(2,1)S(1)}, u32[]{:S(2)}, u32[]{:S(2)}) async-start(bf16[128,16,128]{2,0,1:T(8,128)(2,1)} %copy.148), calls=%async_computation | async-start | bytes 1048576 | tf_op jit(solution)/shard_map/all_to_all | solution.py:41
  26.4 19.1 %all-to-all-start.2 = ((bf16[128,16,128]{2,0,1:T(8,128)(2,1)}), bf16[128,16,128]{2,0,1:T(8,128)(2,1)S(1)}, u32[]{:S(2)}, u32[]{:S(2)}) async-start(bf16[128,16,128]{2,0,1:T(8,128)(2,1)} %copy.156), calls=%async_computation.2 | async-start | bytes 1048576 | tf_op jit(solution)/shard_map/all_to_all | solution.py:40
  45.5 50.5 %all-to-all-start.1 = ((bf16[16,3,128,128]{3,2,1,0:T(8,128)(2,1)}), bf16[16,3,128,128]{3,2,1,0:T(8,128)(2,1)S(1)}, u32[]{:S(2)}, u32[]{:S(2)}) async-start(bf16[16,3,128,128]{3,2,1,0:T(8,128)(2,1)} %bitcast.203), calls=%async_computation.1 | async-start | bytes 3145728 | tf_op jit(solution)/shard_map/all_to_all | solution.py:83
  56.1 45.3 %copy-start.13 = (bf16[128,2048]{1,0:T(8,128)(2,1)S(1)}, bf16[128,2048]{1,0:T(8,128)(2,1)}, u32[]{:S(2)}) copy-start(bf16[128,2048]{1,0:T(8,128)(2,1)} %param.12) | copy-start | bytes 1572868
  96.0 45.7 %all-to-all-start.3 = ((bf16[16,3,128,128]{3,2,1,0:T(8,128)(2,1)}), bf16[16,3,128,128]{3,2,1,0:T(8,128)(2,1)}, u32[]{:S(2)}, u32[]{:S(2)}) async-start(bf16[16,3,128,128]{3,2,1,0:T(8,128)(2,1)} %bitcast.201), calls=%async_computation.3 | async-start | bytes 3145728 | tf_op jit(solution)/shard_map/all_to_all | solution.py:82
  141.7 21.4 %all-to-all-start.4 = ((bf16[128,16,128]{2,0,1:T(8,128)(2,1)}), bf16[128,16,128]{2,0,1:T(8,128)(2,1)}, u32[]{:S(2)}, u32[]{:S(2)}) async-start(bf16[128,16,128]{2,0,1:T(8,128)(2,1)} %copy.158), calls=%async_computation.4 | async-start | bytes 1048576 | tf_op jit(solution)/shard_map/all_to_all | solution.py:39
  146.6 3.4 collective-permute-start
  146.7 7.1 %collective-permute-start.1 = (bf16[128,128]{1,0:T(8,128)(2,1)S(1)}, bf16[128,128]{1,0:T(8,128)(2,1)S(1)}, u32[]{:S(2)}, u32[]{:S(2)}) collective-permute-start(bf16[128,128]{1,0:T(8,128)(2,1)S(1)} %slice_bitcast_fusion.4), channel_id=1, source_target_pairs={{0,16},{16,32},{32,48},{48,64},{64,80},{80,96},{96,112},{112,128},... | collective-permute-start | bytes 98312 | tf_op jit(solution)/shard_map/ppermute | solution.py:13
  159.2 10.7 %copy-start.2 = (bf16[64,128,128]{2,1,0:T(8,128)(2,1)}, bf16[64,128,128]{2,1,0:T(8,128)(2,1)S(1)}, u32[]{:S(2)}) copy-start(bf16[64,128,128]{2,1,0:T(8,128)(2,1)S(1)} %gather_fusion.3) | copy-start | bytes 6291460
  163.1 17.4 %all-to-all-start.6 = ((bf16[128,16,128]{0,2,1:T(8,128)(2,1)}), bf16[128,16,128]{0,2,1:T(8,128)(2,1)S(1)}, u32[]{:S(2)}, u32[]{:S(2)}) async-start(bf16[128,16,128]{0,2,1:T(8,128)(2,1)} %bitcast.26), calls=%async_computation.6 | async-start | bytes 1048576 | tf_op jit(solution)/shard_map/all_to_all | solution.py:42
  180.6 10.9 %copy-start.8 = (bf16[128,16,128]{0,2,1:T(8,128)(2,1)}, bf16[128,16,128]{0,2,1:T(8,128)(2,1)S(1)}, u32[]{:S(2)}) copy-start(bf16[128,16,128]{0,2,1:T(8,128)(2,1)S(1)} %all-to-all-done.6) | copy-start | bytes 1572868
  184.0 23.2 %all-to-all-start.5 = ((bf16[16,128,128]{1,2,0:T(8,128)(2,1)}), bf16[16,128,128]{1,2,0:T(8,128)(2,1)S(1)}, u32[]{:S(2)}, u32[]{:S(2)}) async-start(bf16[16,128,128]{1,2,0:T(8,128)(2,1)} %bitcast.23), calls=%async_computation.5 | async-start | bytes 1048576 | tf_op jit(solution)/shard_map/all_to_all | solution.py:172
  207.2 20.3 %all-to-all-start.7 = ((bf16[16,128,128]{1,2,0:T(8,128)(2,1)}), bf16[16,128,128]{1,2,0:T(8,128)(2,1)}, u32[]{:S(2)}, u32[]{:S(2)}) async-start(bf16[16,128,128]{1,2,0:T(8,128)(2,1)} %fusion.28), calls=%async_computation.7 | async-start | bytes 1048576 | tf_op jit(solution)/shard_map/all_to_all | solution.py:173
  222.7 12.0 %copy-start.1 = (bf16[16,128,512]{1,2,0:T(8,128)(2,1)S(1)}, bf16[16,128,512]{1,2,0:T(8,128)(2,1)}, u32[]{:S(2)}) copy-start(bf16[16,128,512]{1,2,0:T(8,128)(2,1)} %copy-done) | copy-start | bytes 6291460
  222.7 12.0 %copy-start.9 = (bf16[128,16,128]{0,2,1:T(8,128)(2,1)S(1)}, bf16[128,16,128]{0,2,1:T(8,128)(2,1)}, u32[]{:S(2)}) copy-start(bf16[128,16,128]{0,2,1:T(8,128)(2,1)} %copy-done.8) | copy-start | bytes 1572868
  227.5 48.9 %all-to-all-start.8 = ((bf16[16,3,128,128]{3,2,1,0:T(8,128)(2,1)}), bf16[16,3,128,128]{3,2,1,0:T(8,128)(2,1)}, u32[]{:S(2)}, u32[]{:S(2)}) async-start(bf16[16,3,128,128]{3,2,1,0:T(8,128)(2,1)} %bitcast.202), calls=%async_computation.8 | async-start | bytes 3145728 | tf_op jit(solution)/shard_map/all_to_all | solution.py:146
  276.4 47.5 %all-to-all-start.10 = ((bf16[16,3,128,128]{3,2,1,0:T(8,128)(2,1)}), bf16[16,3,128,128]{3,2,1,0:T(8,128)(2,1)S(1)}, u32[]{:S(2)}, u32[]{:S(2)}) async-start(bf16[16,3,128,128]{3,2,1,0:T(8,128)(2,1)} %bitcast.200), calls=%async_computation.10 | async-start | bytes 3145728 | tf_op jit(solution)/shard_map/all_to_all | solution.py:149
  282.6 8.4 %collective-permute-start.2 = (bf16[128,128]{1,0:T(8,128)(2,1)S(1)}, bf16[128,128]{1,0:T(8,128)(2,1)S(1)}, u32[]{:S(2)}, u32[]{:S(2)}) collective-permute-start(bf16[128,128]{1,0:T(8,128)(2,1)S(1)} %fusion.39), channel_id=1, source_target_pairs={{0,240},{16,0},{32,16},{48,32},{64,48},{80,64},{96,80},{112,96},{1... | collective-permute-start | bytes 98312 | tf_op jit(solution)/shard_map/ppermute | solution.py:13
  323.9 20.4 %all-to-all-start.9 = ((bf16[16,128,128]{2,1,0:T(8,128)(2,1)}), bf16[16,128,128]{2,1,0:T(8,128)(2,1)}, u32[]{:S(2)}, u32[]{:S(2)}) async-start(bf16[16,128,128]{2,1,0:T(8,128)(2,1)} %copy.171), calls=%async_computation.9 | async-start | bytes 1048576 | tf_op jit(solution)/shard_map/all_to_all | solution.py:174
  330.6 3.3 collective-permute-start.3
  335.4 14.9 %copy-start.11 = (bf16[16,128,128]{1,2,0:T(8,128)(2,1)S(1)}, bf16[16,128,128]{1,2,0:T(8,128)(2,1)}, u32[]{:S(2)}) copy-start(bf16[16,128,128]{1,2,0:T(8,128)(2,1)} %copy-done.10) | copy-start | bytes 1572868
  344.3 20.5 %all-to-all-start.11 = ((bf16[16,128,128]{2,1,0:T(8,128)(2,1)}), bf16[16,128,128]{2,1,0:T(8,128)(2,1)S(1)}, u32[]{:S(2)}, u32[]{:S(2)}) async-start(bf16[16,128,128]{2,1,0:T(8,128)(2,1)} %copy.178), calls=%async_computation.11 | async-start | bytes 1048576 | tf_op jit(solution)/shard_map/all_to_all | solution.py:175
  (7 other events, 33.4 us)
where the time goes:
time: 371 us; the launch traced here: 366 us
  waiting for transfers between devices  209 us (56%)
  starting transfers between devices  75.4 us (20%)
  local copies, waits for them, and re-layouts  49.9 us (13%)
  matrix products  16.4 us (4%)
  other arithmetic  14.4 us (4%)
    all_to_all x1, waiting for transfers between devices, body(): lax.all_to_all(send_v, 'ctx', split_axis=0, concat_axis=0, tiled=True)  39.9 us
    all_to_all x1, waiting for transfers between devices, body(): lax.all_to_all(send_k, 'ctx', split_axis=0, concat_axis=0, tiled=True)  36.2 us
    all_to_all x1, waiting for transfers between devices, body(): lax.all_to_all(grad_keys.astype(jnp.bfloat16), 'ctx', split_axis=0, conca...  32.5 us
    all_to_all x1, waiting for transfers between devices, body(): lax.all_to_all(grad_values.astype(jnp.bfloat16), 'ctx', split_axis=0, con...  28 us
    all_to_all x1, waiting for transfers between devices, body(): lax.all_to_all(values, 'head', split_axis=1, concat_axis=0, tiled=True)  13.5 us
    unnamed x39, local copies, waits for them, and re-layouts  13.1 us
    all_to_all x1, waiting for transfers between devices, body(): lax.all_to_all(keys, 'head', split_axis=1, concat_axis=0, tiled=True)  11.1 us
    all_to_all x1, waiting for transfers between devices, body(): lax.all_to_all(results[0], 'head', split_axis=0, concat_axis=1, tiled=True)  10.3 us
  transfers between devices with their start and end apart: 16, of which 14 were waited for; matrix products, arithmetic and copies ran while one was open for 19% of the time, Pallas kernels for 0%

commit v1 on v0

v1 whole, which is shorter than its diff:
```python
import functools

import jax
import jax.numpy as jnp
from jax import lax
from jax.experimental import pallas as pl
from jax.experimental.pallas import tpu as pltpu
from jax.sharding import PartitionSpec as P

HEAD_DIM = 128
BLOCK = 128
VMEM_LIMIT = 48 * 1024 * 1024
ANY = pl.BlockSpec(memory_space=pl.ANY)
VMEM = pl.BlockSpec(memory_space=pltpu.VMEM)
SMEM = pl.BlockSpec(memory_space=pltpu.SMEM)


def params():
    return pltpu.CompilerParams(vmem_limit_bytes=VMEM_LIMIT)


def cost(flops, nbytes):
    return pl.CostEstimate(flops=flops, bytes_accessed=nbytes, transcendentals=0)


def split_kernel(heads, first_ref, second_ref, out_ref, sems):
    copies = []
    for which, ref in enumerate((first_ref, second_ref)):
        for head in range(heads):
            copies.append(
                pltpu.make_async_copy(
                    ref.at[:, pl.ds(head * HEAD_DIM, HEAD_DIM)],
                    out_ref.at[head, which],
                    sems.at[which * heads + head],
                )
            )
    for copy in copies:
        copy.start()
    for copy in copies:
        copy.wait()


def split_heads(first, second):
    rows, features = first.shape
    heads = features // HEAD_DIM
    return pl.pallas_call(
        functools.partial(split_kernel, heads),
        out_shape=jax.ShapeDtypeStruct((heads, 2, rows, HEAD_DIM), first.dtype),
        in_specs=[ANY, ANY],
        out_specs=ANY,
        scratch_shapes=[pltpu.SemaphoreType.DMA((2 * heads,))],
        compiler_params=params(),
        cost_estimate=cost(0, 4 * first.size * 2),
        name="split_heads",
    )(first, second)


def join_kernel(heads, in_ref, first_ref, second_ref, sems):
    copies = []
    for which, ref in enumerate((first_ref, second_ref)):
        for head in range(heads):
            copies.append(
                pltpu.make_async_copy(
                    in_ref.at[head, which],
                    ref.at[:, pl.ds(head * HEAD_DIM, HEAD_DIM)],
                    sems.at[which * heads + head],
                )
            )
    for copy in copies:
        copy.start()
    for copy in copies:
        copy.wait()


def join_heads(both):
    heads, _, rows, depth = both.shape
    shape = jax.ShapeDtypeStruct((rows, heads * depth), both.dtype)
    return pl.pallas_call(
        functools.partial(join_kernel, heads),
        out_shape=(shape, shape),
        in_specs=[ANY],
        out_specs=(ANY, ANY),
        scratch_shapes=[pltpu.SemaphoreType.DMA((2 * heads,))],
        compiler_params=params(),
        cost_estimate=cost(0, 2 * both.size * 2),
        name="join_heads",
    )(both)


def pick_kernel(slots, index_ref, in_ref, out_ref, sems):
    copies = [
        pltpu.make_async_copy(in_ref.at[index_ref[slot]], out_ref.at[slot], sems.at[slot])
        for slot in range(slots)
    ]
    for copy in copies:
        copy.start()
    for copy in copies:
        copy.wait()


def pick_blocks(index, blocks):
    slots = index.shape[0]
    return pl.pallas_call(
        functools.partial(pick_kernel, slots),
        out_shape=jax.ShapeDtypeStruct((slots,) + blocks.shape[1:], blocks.dtype),
        in_specs=[SMEM, VMEM],
        out_specs=ANY,
        scratch_shapes=[pltpu.SemaphoreType.DMA((slots,))],
        compiler_params=params(),
        cost_estimate=cost(0, 2 * slots * blocks[0].size * 2),
        name="pick_blocks",
    )(index, blocks)


def attend_kernel(blocks, slot_ref, qg_ref, kv_ref, edge_ref, far_ref, out_ref, far_out_ref, edge_out_ref, sum_ref):
    scale = HEAD_DIM ** (-0.5)
    f32, bf16 = jnp.float32, jnp.bfloat16

    def dot(a, b, dims):
        return lax.dot_general(a, b, (dims, ((), ())), preferred_element_type=f32)

    def one(n, first):
        q, g = qg_ref[n, 0], qg_ref[n, 1]
        s2, s3 = slot_ref[2 * n], slot_ref[2 * n + 1]
        if first:
            prev_k, prev_v = edge_ref[0], edge_ref[1]
        else:
            prev_k, prev_v = kv_ref[n - 1, 0], kv_ref[n - 1, 1]
        k = jnp.concatenate([kv_ref[n, 0], prev_k, far_ref[s2, 0], far_ref[s3, 0]], axis=0)
        v = jnp.concatenate([kv_ref[n, 1], prev_v, far_ref[s2, 1], far_ref[s3, 1]], axis=0)
        s = dot(k, q, ((1,), (1,))) * scale
        dp = dot(v, g, ((1,), (1,)))
        w = jnp.exp(s - jnp.max(s, axis=0, keepdims=True))
        p = w * (1.0 / jnp.sum(w, axis=0, keepdims=True))
        p_low = p.astype(bf16)
        delta = jnp.sum(p_low.astype(f32) * dp, axis=0, keepdims=True)
        ds = (p * (dp - delta) * scale).astype(bf16)
        out_ref[n, 0] = dot(p_low, v, ((0,), (0,))).astype(bf16)
        out_ref[n, 1] = dot(ds, k, ((0,), (0,))).astype(bf16)
        dk = dot(ds, q, ((1,), (0,)))
        dv = dot(p_low, g, ((1,), (0,)))
        for which, d in enumerate((dk, dv)):
            sum_ref[n, which] = d[:BLOCK]
            if first:
                edge_out_ref[which] = d[BLOCK : 2 * BLOCK].astype(bf16)
            else:
                sum_ref[n - 1, which] += d[BLOCK : 2 * BLOCK]
            far_out_ref[s2, which] = d[2 * BLOCK : 3 * BLOCK].astype(bf16)
            far_out_ref[s3, which] = d[3 * BLOCK :].astype(bf16)

    far_out_ref[...] = jnp.zeros_like(far_out_ref)
    one(0, True)
    lax.fori_loop(1, blocks, lambda n, _: one(n, False), None)


def attend(slot, qg, kv, edge, far):
    blocks = qg.shape[0]
    bf16 = jnp.bfloat16
    return pl.pallas_call(
        functools.partial(attend_kernel, blocks),
        out_shape=(
            jax.ShapeDtypeStruct(qg.shape, bf16),
            jax.ShapeDtypeStruct(far.shape, bf16),
            jax.ShapeDtypeStruct(edge.shape, bf16),
            jax.ShapeDtypeStruct(kv.shape, jnp.float32),
        ),
        in_specs=[SMEM, VMEM, VMEM, VMEM, VMEM],
        out_specs=(VMEM, VMEM, VMEM, VMEM),
        compiler_params=params(),
        cost_estimate=cost(
            5 * 2 * blocks * 4 * BLOCK * BLOCK * HEAD_DIM, 2 * (2 * qg.size + 3 * kv.size + 2 * far.size)
        ),
        name="attend",
    )(slot, qg, kv, edge, far)


def land_kernel(slots, blocks, index_ref, valid_ref, sum_ref, back_ref, home_ref, out_ref, total):
    total[...] = sum_ref[...]
    total[blocks - 1] += back_ref[...].astype(jnp.float32)

    def one(slot, _):
        @pl.when(valid_ref[slot] != 0)
        def _():
            total[index_ref[slot]] += home_ref[slot].astype(jnp.float32)

    lax.fori_loop(0, slots, one, None)
    out_ref[...] = total[...].astype(out_ref.dtype)


def land(index, valid, sums, back, home):
    slots = index.shape[0]
    blocks = sums.shape[0]
    return pl.pallas_call(
        functools.partial(land_kernel, slots, blocks),
        out_shape=jax.ShapeDtypeStruct(sums.shape, jnp.bfloat16),
        in_specs=[SMEM, SMEM, VMEM, VMEM, VMEM],
        out_specs=VMEM,
        scratch_shapes=[pltpu.VMEM(sums.shape, jnp.float32)],
        compiler_params=params(),
        cost_estimate=cost(sums.size * 4, 6 * sums.size + 2 * home.size),
        name="land",
    )(index, valid, sums, back, home)


def body(queries, keys, values, out_grad, key_lists):
    ctx_count = lax.axis_size("ctx")
    ctx_rank = lax.axis_index("ctx")
    blocks = lax.axis_size("head")
    requests = 2 * blocks
    capacity = (requests + ctx_count - 2) // (ctx_count - 1)

    far_all = key_lists[:, 2:].reshape(ctx_count, requests)
    source = far_all // blocks
    earlier = jnp.arange(requests)[None, :] < jnp.arange(requests)[:, None]
    rank = jnp.sum(
        ((source[:, None, :] == source[:, :, None]) & earlier[None]).astype(jnp.int32), axis=2
    )
    slot_of = source * capacity + rank
    is_mine = jnp.arange(ctx_count) == ctx_rank
    my_slot = jnp.sum(jnp.where(is_mine[:, None], slot_of, 0), axis=0)
    wanted = (
        slot_of[:, None, :] == ctx_rank * capacity + jnp.arange(capacity, dtype=jnp.int32)[None, :, None]
    )
    send_index = jnp.sum(jnp.where(wanted, far_all[:, None, :] % blocks, 0), axis=2).reshape(-1)
    send_valid = jnp.sum(wanted.astype(jnp.int32), axis=2).reshape(-1)

    def head_exchange(array):
        return lax.all_to_all(array, "head", split_axis=0, concat_axis=0, tiled=True)

    def ctx_exchange(array):
        return lax.all_to_all(array, "ctx", split_axis=0, concat_axis=0, tiled=True)

    def shift(array, by):
        return lax.ppermute(
            array, "ctx", [(i, (i + by) % ctx_count) for i in range(ctx_count)]
        )

    kv = head_exchange(split_heads(keys, values))
    qg = head_exchange(split_heads(queries, out_grad))
    edge = shift(kv[blocks - 1], 1)
    far = ctx_exchange(pick_blocks(send_index, kv))
    out, far_grad, edge_grad, sums = attend(my_slot, qg, kv, edge, far)
    home = ctx_exchange(far_grad)
    back = shift(edge_grad, -1)
    attended, query_grad = join_heads(head_exchange(out))
    key_grad, value_grad = join_heads(head_exchange(land(send_index, send_valid, sums, back, home)))
    return attended, query_grad, key_grad, value_grad


def solution(mesh):
    tokens = P(("ctx", "head"), None)
    return jax.shard_map(
        body,
        mesh=mesh,
        in_specs=(tokens, tokens, tokens, tokens, P()),
        out_specs=(tokens, tokens, tokens, tokens),
        check_vma=False,
    )
```

time: 371 us -> 316 us (0.85)
  blocking collectives: 0 us -> 74.5 us
  local copies, waits for them, and re-layouts: 49.9 us -> 2.71 us
  starting transfers between devices: 75.4 us -> 33.6 us
  waiting for transfers between devices: 209 us -> 174 us
  Pallas kernels: 0 us -> 27.6 us
  matrix products: 16.4 us -> 0 us
  other arithmetic: 14.4 us -> 0.83 us
    all_to_all x0 -> x1, blocking collectives: none -> 74.5 us  [ctx_exchange(): return lax.all_to_all(array, 'ctx', split_axis=0, concat_axis=0, tiled=True)]
    all_to_all x12 -> x5, waiting for transfers between devices: 202 us -> 151 us  [the longest x4 90.5 us: head_exchange(): lax.all_to_all(array, 'head', split_axis=0, concat_axis=0, tiled=True)]
    all_to_all x12 -> x5, starting transfers between devices: 74.1 us -> 33.3 us  [the longest x4 24.7 us: head_exchange(): lax.all_to_all(array, 'head', split_axis=0, concat_axis=0, tiled=True)]
    pallas_call x0 -> x7, Pallas kernels: none -> 27.6 us  [the longest x1 15.9 us: attend(): pl.pallas_call(functools.partial(attend_kernel, blocks), out_shape=(jax.S...]
    dot_general x8 -> x0, matrix products: 16.4 us -> none  [the longest x1 3.86 us: body(): jnp.einsum('qbhd,qkhd->qhbk', g_blocks, listed_values, preferred_element_...]
    ppermute x4 -> x2, waiting for transfers between devices: 7.29 us -> 23.2 us  [shift(): lax.ppermute(array, 'ctx', [(i, (i + by) % ctx_count) for i in range(ctx_...]
    unnamed x39 -> x16, local copies, waits for them, and re-layouts: 13.1 us -> 2.1 us
    gather x4 -> x0, local copies, waits for them, and re-layouts: 8.66 us -> none  [the longest x2 4.72 us: select_blocks(): chosen = pool[pool_index]]
  transfers between devices with their start and end apart: 16 -> 7, of which waited for: 14 -> 7; matrix products, arithmetic and copies ran while one was open for 19% -> 0% of each run, Pallas kernels for 0% -> 3%
where the time goes in v1:
time: 316 us; the launch traced here: 314 us
  waiting for transfers between devices  174 us (55%)
  blocking collectives  74.5 us (24%)
  starting transfers between devices  33.6 us (11%)
  Pallas kernels  27.6 us (9%)
    all_to_all x4, waiting for transfers between devices, head_exchange(): lax.all_to_all(array, 'head', split_axis=0, concat_axis=0, tiled=True)  90.5 us
    all_to_all x1, blocking collectives, ctx_exchange(): return lax.all_to_all(array, 'ctx', split_axis=0, concat_axis=0, tiled=True)  74.5 us
    all_to_all x1, waiting for transfers between devices, ctx_exchange(): return lax.all_to_all(array, 'ctx', split_axis=0, concat_axis=0, tiled=True)  60.3 us
    all_to_all x4, starting transfers between devices, head_exchange(): lax.all_to_all(array, 'head', split_axis=0, concat_axis=0, tiled=True)  24.7 us
    ppermute x2, waiting for transfers between devices, shift(): lax.ppermute(array, 'ctx', [(i, (i + by) % ctx_count) for i in range(ctx_...  23.2 us
    pallas_call x1, Pallas kernels, attend(): pl.pallas_call(functools.partial(attend_kernel, blocks), out_shape=(jax.S...  15.9 us
    all_to_all x1, starting transfers between devices, ctx_exchange(): return lax.all_to_all(array, 'ctx', split_axis=0, concat_axis=0, tiled=True)  8.64 us
  transfers between devices with their start and end apart: 7, of which 7 were waited for; matrix products, arithmetic and copies ran while one was open for 0% of the time, Pallas kernels for 3%

profile of v1, /device:TPU:56, one launch (start us, length us, event | category | flops | bytes accessed | tf_op | source)
XLA Modules:
  0.0 314.1 jit_solution(15159180384542652241)
XLA Ops:
  0.6 1.0 copy-done.3
  1.7 1.0 copy-done.4
  2.7 1.3 split_heads.3
  4.0 8.5 %all-to-all-start.1 = ((bf16[16,2,128,128]{3,2,1,0:T(8,128)(2,1)}), bf16[16,2,128,128]{3,2,1,0:T(8,128)(2,1)S(1)}, u32[]{:S(2)}, u32[]{:S(2)}) async-start(bf16[16,2,128,128]{3,2,1,0:T(8,128)(2,1)} %split_heads.3), calls=%async_computation.1 | async-start | bytes 2097152 | tf_op jit(solution)/shard_map/all_to_all | solution.py:228
  12.5 1.3 split_heads.2
  13.8 24.4 %all-to-all-done.1.in_ref.kv_ref = bf16[16,2,128,128]{3,2,1,0:T(8,128)(2,1)S(1)} async-done(((bf16[16,2,128,128]{3,2,1,0:T(8,128)(2,1)}), bf16[16,2,128,128]{3,2,1,0:T(8,128)(2,1)S(1)}, u32[]{:S(2)}, u32[]{:S(2)}) %all-to-all-start.1) | async-done | bytes 1048608 | tf_op jit(solution)/shard_map/all_to_all | solution.py:228
  38.2 5.2 %all-to-all-start = ((bf16[16,2,128,128]{3,2,1,0:T(8,128)(2,1)}), bf16[16,2,128,128]{3,2,1,0:T(8,128)(2,1)S(1)}, u32[]{:S(2)}, u32[]{:S(2)}) async-start(bf16[16,2,128,128]{3,2,1,0:T(8,128)(2,1)} %split_heads.2), calls=%async_computation | async-start | bytes 2097152 | tf_op jit(solution)/shard_map/all_to_all | solution.py:228
  43.7 0.5 convert_reduce_fusion
  44.3 0.3 fusion.1
  44.7 2.6 pick_blocks.1
  47.3 20.8 %all-to-all-done.qg_ref = bf16[16,2,128,128]{3,2,1,0:T(8,128)(2,1)S(1)} async-done(((bf16[16,2,128,128]{3,2,1,0:T(8,128)(2,1)}), bf16[16,2,128,128]{3,2,1,0:T(8,128)(2,1)S(1)}, u32[]{:S(2)}, u32[]{:S(2)}) %all-to-all-start) | async-done | bytes 1048608 | tf_op jit(solution)/shard_map/all_to_all | solution.py:228
  68.1 8.6 %all-to-all-start.2 = ((bf16[48,2,128,128]{3,2,1,0:T(8,128)(2,1)}), bf16[48,2,128,128]{3,2,1,0:T(8,128)(2,1)}, u32[]{:S(2)}, u32[]{:S(2)}) async-start(bf16[48,2,128,128]{3,2,1,0:T(8,128)(2,1)} %pick_blocks.1), calls=%async_computation.2 | async-start | bytes 6291456 | tf_op jit(solution)/shard_map/all_to_all | solution.py:231
  77.0 21.5 %collective-permute-done.edge_ref = bf16[2,128,128]{2,1,0:T(8,128)(2,1)S(1)} collective-permute-done((bf16[2,128,128]{2,1,0:T(8,128)(2,1)S(1)}, bf16[2,128,128]{2,1,0:T(8,128)(2,1)S(1)}, u32[]{:S(2)}, u32[]{:S(2)}) %collective-permute-start) | collective-permute-done | bytes 65568 | tf_op jit(solution)/shard_map/ppermute | solution.py:234
  98.5 60.3 %all-to-all-done.2.far_ref = bf16[48,2,128,128]{3,2,1,0:T(8,128)(2,1)} async-done(((bf16[48,2,128,128]{3,2,1,0:T(8,128)(2,1)}), bf16[48,2,128,128]{3,2,1,0:T(8,128)(2,1)}, u32[]{:S(2)}, u32[]{:S(2)}) %all-to-all-start.2) | async-done | bytes 3145760 | tf_op jit(solution)/shard_map/all_to_all | solution.py:231
  158.8 15.9 %attend.1 = (bf16[16,2,128,128]{3,2,1,0:T(8,128)(2,1)S(1)}, bf16[48,2,128,128]{3,2,1,0:T(8,128)(2,1)}, bf16[2,128,128]{2,1,0:T(8,128)(2,1)S(1)}, f32[16,2,128,128]{3,2,1,0:T(8,128)S(1)}) custom-call(s32[32]{0:T(128)S(1)} %get-tuple-element.22.slot_ref, bf16[16,2,128,128]{3,2,1,0:T(8,128)(2,1)S(1)} %all-to-all-done.qg_ref, ...), custom_call_target="tpu_custom_call" | custom-call | flops 1342177280 | bytes 11534336 | tf_op jit(solution)/shard_map/attend/pallas_call | solution.py:159
  174.7 74.5 %all_to_all.30.home_ref = bf16[48,2,128,128]{3,2,1,0:T(8,128)(2,1)} all-to-all(bf16[48,2,128,128]{3,2,1,0:T(8,128)(2,1)} %get-tuple-element.17), channel_id=1, replica_groups=mesh['ctx'=16,'head'=16] {'ctx'}, dimensions={0} | all-to-all | bytes 6291456 | tf_op jit(solution)/shard_map/all_to_all | solution.py:231
  249.3 5.9 %all-to-all-start.3 = ((bf16[16,2,128,128]{3,2,1,0:T(8,128)(2,1)}), bf16[16,2,128,128]{3,2,1,0:T(8,128)(2,1)S(1)}, u32[]{:S(2)}, u32[]{:S(2)}) async-start(bf16[16,2,128,128]{3,2,1,0:T(8,128)(2,1)} %copy-done.2), calls=%async_computation.3 | async-start | bytes 2097152 | tf_op jit(solution)/shard_map/all_to_all | solution.py:228
  255.3 1.7 collective-permute-done.1.back_ref
  257.1 4.1 %land.1 = bf16[16,2,128,128]{3,2,1,0:T(8,128)(2,1)} custom-call(s32[48]{0:T(128)S(1)} %reshape.136.index_ref, s32[48]{0:T(128)S(1)} %reshape.137.valid_ref, f32[16,2,128,128]{3,2,1,0:T(8,128)S(1)} %copy-done.1, bf16[2,128,128]{2,1,0:T(8,128)(2,1)S(1)} %collective-permute-done.1.back_ref, bf16[48,2,128,128]{3,2,1,0:T(8,128)(2,1)} %all_to_all.30.home_ref), custom_call_target="tpu_custom_call" | custom-call | flops 2097152 | bytes 6291456 | tf_op jit(solution)/shard_map/land/pallas_call | solution.py:193
  261.2 19.9 %all-to-all-done.3.in_ref = bf16[16,2,128,128]{3,2,1,0:T(8,128)(2,1)S(1)} async-done(((bf16[16,2,128,128]{3,2,1,0:T(8,128)(2,1)}), bf16[16,2,128,128]{3,2,1,0:T(8,128)(2,1)S(1)}, u32[]{:S(2)}, u32[]{:S(2)}) %all-to-all-start.3) | async-done | bytes 1048608 | tf_op jit(solution)/shard_map/all_to_all | solution.py:228
  281.1 5.2 %all-to-all-start.5 = ((bf16[16,2,128,128]{3,2,1,0:T(8,128)(2,1)}), bf16[16,2,128,128]{3,2,1,0:T(8,128)(2,1)S(1)}, u32[]{:S(2)}, u32[]{:S(2)}) async-start(bf16[16,2,128,128]{3,2,1,0:T(8,128)(2,1)} %land.1), calls=%async_computation.5 | async-start | bytes 2097152 | tf_op jit(solution)/shard_map/all_to_all | solution.py:228
  286.3 1.2 join_heads.2
  287.5 25.3 %all-to-all-done.5.in_ref = bf16[16,2,128,128]{3,2,1,0:T(8,128)(2,1)S(1)} async-done(((bf16[16,2,128,128]{3,2,1,0:T(8,128)(2,1)}), bf16[16,2,128,128]{3,2,1,0:T(8,128)(2,1)S(1)}, u32[]{:S(2)}, u32[]{:S(2)}) %all-to-all-start.5) | async-done | bytes 1048608 | tf_op jit(solution)/shard_map/all_to_all | solution.py:228
  312.9 1.2 join_heads.3
  (29 shorter events, 1.0 us)
Async XLA Ops:
  0.6 1.0 copy-start.3
  1.7 1.0 copy-start.4
  2.7 9.8 %copy-start.5 = (bf16[128,2048]{1,0:T(8,128)(2,1)S(1)}, bf16[128,2048]{1,0:T(8,128)(2,1)}, u32[]{:S(2)}) copy-start(bf16[128,2048]{1,0:T(8,128)(2,1)} %first_ref.2) | copy-start | bytes 1572868
  2.7 9.8 %copy-start.6 = (bf16[128,2048]{1,0:T(8,128)(2,1)S(1)}, bf16[128,2048]{1,0:T(8,128)(2,1)}, u32[]{:S(2)}) copy-start(bf16[128,2048]{1,0:T(8,128)(2,1)} %second_ref.2) | copy-start | bytes 1572868
  4.0 39.4 %copy-start.7 = (s32[256,4]{0,1:T(4,128)S(1)}, s32[256,4]{0,1:T(4,128)}, u32[]{:S(2)}) copy-start(s32[256,4]{0,1:T(4,128)} %param.9) | copy-start | bytes 12292
  4.0 34.2 %all-to-all-start.1 = ((bf16[16,2,128,128]{3,2,1,0:T(8,128)(2,1)}), bf16[16,2,128,128]{3,2,1,0:T(8,128)(2,1)S(1)}, u32[]{:S(2)}, u32[]{:S(2)}) async-start(bf16[16,2,128,128]{3,2,1,0:T(8,128)(2,1)} %split_heads.3), calls=%async_computation.1 | async-start | bytes 2097152 | tf_op jit(solution)/shard_map/all_to_all | solution.py:228
  38.2 29.9 %all-to-all-start = ((bf16[16,2,128,128]{3,2,1,0:T(8,128)(2,1)}), bf16[16,2,128,128]{3,2,1,0:T(8,128)(2,1)S(1)}, u32[]{:S(2)}, u32[]{:S(2)}) async-start(bf16[16,2,128,128]{3,2,1,0:T(8,128)(2,1)} %split_heads.2), calls=%async_computation | async-start | bytes 2097152 | tf_op jit(solution)/shard_map/all_to_all | solution.py:228
  68.1 90.7 %all-to-all-start.2 = ((bf16[48,2,128,128]{3,2,1,0:T(8,128)(2,1)}), bf16[48,2,128,128]{3,2,1,0:T(8,128)(2,1)}, u32[]{:S(2)}, u32[]{:S(2)}) async-start(bf16[48,2,128,128]{3,2,1,0:T(8,128)(2,1)} %pick_blocks.1), calls=%async_computation.2 | async-start | bytes 6291456 | tf_op jit(solution)/shard_map/all_to_all | solution.py:231
  76.8 21.7 %collective-permute-start = (bf16[2,128,128]{2,1,0:T(8,128)(2,1)S(1)}, bf16[2,128,128]{2,1,0:T(8,128)(2,1)S(1)}, u32[]{:S(2)}, u32[]{:S(2)}) collective-permute-start(bf16[2,128,128]{2,1,0:T(8,128)(2,1)S(1)} %slice_bitcast_fusion), channel_id=1, source_target_pairs={{0,16},{16,32},{32,48},{48,64},{64,80},{80,96},{96,112},{112,128},... | collective-permute-start | bytes 196616 | tf_op jit(solution)/shard_map/ppermute | solution.py:234
  174.7 74.5 %copy-start = (f32[16,2,128,128]{3,2,1,0:T(8,128)}, f32[16,2,128,128]{3,2,1,0:T(8,128)S(1)}, u32[]{:S(2)}) copy-start(f32[16,2,128,128]{3,2,1,0:T(8,128)S(1)} %get-tuple-element.15.sum_ref) | copy-start | bytes 6291460
  174.7 74.5 %copy-start.2 = (bf16[16,2,128,128]{3,2,1,0:T(8,128)(2,1)}, bf16[16,2,128,128]{3,2,1,0:T(8,128)(2,1)S(1)}, u32[]{:S(2)}) copy-start(bf16[16,2,128,128]{3,2,1,0:T(8,128)(2,1)S(1)} %get-tuple-element.12) | copy-start | bytes 3145732
  249.3 7.8 %copy-start.1 = (f32[16,2,128,128]{3,2,1,0:T(8,128)S(1)}, f32[16,2,128,128]{3,2,1,0:T(8,128)}, u32[]{:S(2)}) copy-start(f32[16,2,128,128]{3,2,1,0:T(8,128)} %copy-done) | copy-start | bytes 6291460
  249.3 31.9 %all-to-all-start.3 = ((bf16[16,2,128,128]{3,2,1,0:T(8,128)(2,1)}), bf16[16,2,128,128]{3,2,1,0:T(8,128)(2,1)S(1)}, u32[]{:S(2)}, u32[]{:S(2)}) async-start(bf16[16,2,128,128]{3,2,1,0:T(8,128)(2,1)} %copy-done.2), calls=%async_computation.3 | async-start | bytes 2097152 | tf_op jit(solution)/shard_map/all_to_all | solution.py:228
  255.1 1.9 collective-permute-start.1
  281.1 31.7 %all-to-all-start.5 = ((bf16[16,2,128,128]{3,2,1,0:T(8,128)(2,1)}), bf16[16,2,128,128]{3,2,1,0:T(8,128)(2,1)S(1)}, u32[]{:S(2)}, u32[]{:S(2)}) async-start(bf16[16,2,128,128]{3,2,1,0:T(8,128)(2,1)} %land.1), calls=%async_computation.5 | async-start | bytes 2097152 | tf_op jit(solution)/shard_map/all_to_all | solution.py:228

commit v2 on v1

v2 whole, which is shorter than its diff:
```python
import functools

import jax
import jax.numpy as jnp
from jax import lax
from jax.experimental import pallas as pl
from jax.experimental.pallas import tpu as pltpu
from jax.sharding import PartitionSpec as P

HEAD_DIM = 128
BLOCK = 128
VMEM_LIMIT = 48 * 1024 * 1024
ANY = pl.BlockSpec(memory_space=pl.ANY)
HBM = pl.BlockSpec(memory_space=pltpu.HBM)
VMEM = pl.BlockSpec(memory_space=pltpu.VMEM)
SMEM = pl.BlockSpec(memory_space=pltpu.SMEM)


def params():
    return pltpu.CompilerParams(vmem_limit_bytes=VMEM_LIMIT)


def cost(flops, nbytes):
    return pl.CostEstimate(flops=flops, bytes_accessed=nbytes, transcendentals=0)


def split_kernel(heads, first_ref, second_ref, out_ref, sems):
    copies = []
    for which, ref in enumerate((first_ref, second_ref)):
        for head in range(heads):
            copies.append(
                pltpu.make_async_copy(
                    ref.at[:, pl.ds(head * HEAD_DIM, HEAD_DIM)],
                    out_ref.at[head, which],
                    sems.at[which * heads + head],
                )
            )
    for copy in copies:
        copy.start()
    for copy in copies:
        copy.wait()


def split_heads(first, second):
    rows, features = first.shape
    heads = features // HEAD_DIM
    return pl.pallas_call(
        functools.partial(split_kernel, heads),
        out_shape=jax.ShapeDtypeStruct((heads, 2, rows, HEAD_DIM), first.dtype),
        in_specs=[HBM, HBM],
        out_specs=ANY,
        scratch_shapes=[pltpu.SemaphoreType.DMA((2 * heads,))],
        compiler_params=params(),
        cost_estimate=cost(0, 4 * first.size * 2),
        name="split_heads",
    )(first, second)


def join_kernel(heads, in_ref, first_ref, second_ref, sems):
    copies = []
    for which, ref in enumerate((first_ref, second_ref)):
        for head in range(heads):
            copies.append(
                pltpu.make_async_copy(
                    in_ref.at[head, which],
                    ref.at[:, pl.ds(head * HEAD_DIM, HEAD_DIM)],
                    sems.at[which * heads + head],
                )
            )
    for copy in copies:
        copy.start()
    for copy in copies:
        copy.wait()


def join_heads(both):
    heads, _, rows, depth = both.shape
    shape = jax.ShapeDtypeStruct((rows, heads * depth), both.dtype)
    return pl.pallas_call(
        functools.partial(join_kernel, heads),
        out_shape=(shape, shape),
        in_specs=[ANY],
        out_specs=(ANY, ANY),
        scratch_shapes=[pltpu.SemaphoreType.DMA((2 * heads,))],
        compiler_params=params(),
        cost_estimate=cost(0, 2 * both.size * 2),
        name="join_heads",
    )(both)


def start_all(copies):
    for copy in copies:
        copy.start()


def wait_all(copies):
    for copy in copies:
        copy.wait()


def pick_kernel(slots, index_ref, in_ref, out_ref, sems):
    copies = [
        pltpu.make_async_copy(in_ref.at[index_ref[slot]], out_ref.at[slot], sems.at[slot])
        for slot in range(slots)
    ]
    start_all(copies)
    wait_all(copies)


def pick_blocks(index, blocks):
    slots = index.shape[0]
    return pl.pallas_call(
        functools.partial(pick_kernel, slots),
        out_shape=jax.ShapeDtypeStruct((slots,) + blocks.shape[1:], blocks.dtype),
        in_specs=[SMEM, VMEM],
        out_specs=ANY,
        scratch_shapes=[pltpu.SemaphoreType.DMA((slots,))],
        compiler_params=params(),
        cost_estimate=cost(0, 2 * slots * blocks[0].size * 2),
        name="pick_blocks",
    )(index, blocks)


def pick_third_kernel(lanes, index_ref, in_ref, *refs):
    outs, sems = refs[:lanes], refs[lanes]
    copies = [
        pltpu.make_async_copy(
            in_ref.at[index_ref[2 * step + half]], outs[step].at[half], sems.at[2 * step + half]
        )
        for step in range(lanes)
        for half in range(2)
    ]
    start_all(copies)
    wait_all(copies)


def pick_third(index, blocks):
    lanes = index.shape[0] // 2
    shape = jax.ShapeDtypeStruct((2,) + blocks.shape[1:], blocks.dtype)
    return pl.pallas_call(
        functools.partial(pick_third_kernel, lanes),
        out_shape=(shape,) * lanes,
        in_specs=[SMEM, VMEM],
        out_specs=(ANY,) * lanes,
        scratch_shapes=[pltpu.SemaphoreType.DMA((2 * lanes,))],
        compiler_params=params(),
        cost_estimate=cost(0, 4 * lanes * blocks[0].size * 2),
        name="pick_third",
    )(index, blocks)


def pick_cross_kernel(lanes, step_ref, *refs):
    ins, out_ref, sems = refs[:lanes], refs[lanes], refs[lanes + 1]
    for j in range(2):
        for step in range(lanes):

            @pl.when(step_ref[j] == step)
            def _():
                pltpu.make_async_copy(ins[step].at[1], out_ref.at[j], sems.at[j]).start()

    for j in range(2):

        @pl.when(step_ref[j] >= 0)
        def _():
            pltpu.make_async_copy(ins[0].at[1], out_ref.at[j], sems.at[j]).wait()


def pick_cross(steps, thirds):
    lanes = len(thirds)
    return pl.pallas_call(
        functools.partial(pick_cross_kernel, lanes),
        out_shape=jax.ShapeDtypeStruct(thirds[0].shape, thirds[0].dtype),
        in_specs=[SMEM] + [ANY] * lanes,
        out_specs=ANY,
        scratch_shapes=[pltpu.SemaphoreType.DMA((2,))],
        compiler_params=params(),
        cost_estimate=cost(0, 4 * thirds[0].size),
        name="pick_cross",
    )(steps, *thirds)


def pick_back_kernel(lanes, near_ref, cross_ref, own_in, cross_in, *refs):
    outs, sems = refs[:lanes], refs[lanes]
    plan = ((near_ref, own_in, 0), (cross_ref, cross_in, 1))
    for step_ref, ref, half in plan:
        for j in range(2):
            for step in range(lanes):

                @pl.when(step_ref[j] == step)
                def _():
                    pltpu.make_async_copy(
                        ref.at[j], outs[step].at[half], sems.at[2 * half + j]
                    ).start()

    for step_ref, ref, half in plan:
        for j in range(2):

            @pl.when(step_ref[j] >= 0)
            def _():
                pltpu.make_async_copy(ref.at[j], outs[0].at[half], sems.at[2 * half + j]).wait()


def pick_back(near_steps, cross_steps, own, crossed, lanes):
    shape = jax.ShapeDtypeStruct(own.shape, own.dtype)
    return pl.pallas_call(
        functools.partial(pick_back_kernel, lanes),
        out_shape=(shape,) * lanes,
        in_specs=[SMEM, SMEM, ANY, ANY],
        out_specs=(ANY,) * lanes,
        scratch_shapes=[pltpu.SemaphoreType.DMA((4,))],
        compiler_params=params(),
        cost_estimate=cost(0, 8 * own.size),
        name="pick_back",
    )(near_steps, cross_steps, own, crossed)


def attend_kernel(
    blocks, lanes, slot_ref, third_ref, near_ref, qg_ref, kv_ref, edge_ref, main_ref, cross_ref, *refs
):
    thirds = refs[:lanes]
    out_ref, main_out, third_out, edge_out, sum_ref = refs[lanes : lanes + 5]
    far, far_out, sems, out_sems, third_sems = refs[lanes + 5 :]
    requests = 2 * blocks
    scale = HEAD_DIM ** (-0.5)
    f32, bf16 = jnp.float32, jnp.bfloat16

    def dot(a, b, dims):
        return lax.dot_general(a, b, (dims, ((), ())), preferred_element_type=f32)

    def arrive(r):
        return pltpu.make_async_copy(main_ref.at[0], far.at[r], sems.at[r])

    def leave(r, slot):
        return pltpu.make_async_copy(far_out.at[r], main_out.at[slot], out_sems.at[r])

    def load(r, _):
        @pl.when(slot_ref[r] >= 0)
        def _():
            pltpu.make_async_copy(main_ref.at[slot_ref[r]], far.at[r], sems.at[r]).start()

    lax.fori_loop(0, requests, load, None)
    for j in range(2):
        r = third_ref[j]
        for step in range(1, lanes):

            @pl.when(near_ref[j] == step)
            def _():
                pltpu.make_async_copy(thirds[step].at[0], far.at[r], sems.at[r]).start()

        @pl.when(near_ref[j] < 0)
        def _():
            pltpu.make_async_copy(cross_ref.at[j], far.at[r], sems.at[r]).start()

    def one(n, first):
        q, g = qg_ref[n, 0], qg_ref[n, 1]
        r2, r3 = 2 * n, 2 * n + 1
        if first:
            prev_k, prev_v = edge_ref[0], edge_ref[1]
        else:
            prev_k, prev_v = kv_ref[n - 1, 0], kv_ref[n - 1, 1]
        arrive(r2).wait()
        arrive(r3).wait()
        k = jnp.concatenate([kv_ref[n, 0], prev_k, far[r2, 0], far[r3, 0]], axis=0)
        v = jnp.concatenate([kv_ref[n, 1], prev_v, far[r2, 1], far[r3, 1]], axis=0)
        s = dot(k, q, ((1,), (1,))) * scale
        dp = dot(v, g, ((1,), (1,)))
        w = jnp.exp(s - jnp.max(s, axis=0, keepdims=True))
        p = w * (1.0 / jnp.sum(w, axis=0, keepdims=True))
        p_low = p.astype(bf16)
        delta = jnp.sum(p_low.astype(f32) * dp, axis=0, keepdims=True)
        ds = (p * (dp - delta) * scale).astype(bf16)
        out_ref[n, 0] = dot(p_low, v, ((0,), (0,))).astype(bf16)
        out_ref[n, 1] = dot(ds, k, ((0,), (0,))).astype(bf16)
        dk = dot(ds, q, ((1,), (0,)))
        dv = dot(p_low, g, ((1,), (0,)))
        for which, d in enumerate((dk, dv)):
            sum_ref[n, which] = d[:BLOCK]
            if first:
                edge_out[which] = d[BLOCK : 2 * BLOCK].astype(bf16)
            else:
                sum_ref[n - 1, which] += d[BLOCK : 2 * BLOCK]
            far_out[r2, which] = d[2 * BLOCK : 3 * BLOCK].astype(bf16)
            far_out[r3, which] = d[3 * BLOCK :].astype(bf16)
        for r in (r2, r3):

            @pl.when(slot_ref[r] >= 0)
            def _():
                leave(r, slot_ref[r]).start()

    one(0, True)
    lax.fori_loop(1, blocks, lambda n, _: one(n, False), None)
    lasts = [
        pltpu.make_async_copy(far_out.at[third_ref[j]], third_out.at[j], third_sems.at[j])
        for j in range(2)
    ]
    start_all(lasts)

    def finish(r, _):
        @pl.when(slot_ref[r] >= 0)
        def _():
            leave(r, 0).wait()

    lax.fori_loop(0, requests, finish, None)
    wait_all(lasts)


def attend(slot, third, near, qg, kv, edge, main, cross, thirds):
    blocks = qg.shape[0]
    lanes = len(thirds)
    bf16 = jnp.bfloat16
    far = pltpu.VMEM((2 * blocks,) + kv.shape[1:], bf16)
    return pl.pallas_call(
        functools.partial(attend_kernel, blocks, lanes),
        out_shape=(
            jax.ShapeDtypeStruct(qg.shape, bf16),
            jax.ShapeDtypeStruct(main.shape, bf16),
            jax.ShapeDtypeStruct(cross.shape, bf16),
            jax.ShapeDtypeStruct(edge.shape, bf16),
            jax.ShapeDtypeStruct(kv.shape, jnp.float32),
        ),
        in_specs=[SMEM, SMEM, SMEM, VMEM, VMEM, VMEM] + [ANY] * (2 + lanes),
        out_specs=(VMEM, ANY, ANY, VMEM, VMEM),
        scratch_shapes=[
            far,
            far,
            pltpu.SemaphoreType.DMA((2 * blocks,)),
            pltpu.SemaphoreType.DMA((2 * blocks,)),
            pltpu.SemaphoreType.DMA((2,)),
        ],
        compiler_params=params(),
        cost_estimate=cost(
            5 * 2 * blocks * 4 * BLOCK * BLOCK * HEAD_DIM, 2 * (2 * qg.size + 3 * kv.size + 2 * main.size)
        ),
        name="attend",
    )(slot, third, near, qg, kv, edge, main, cross, *thirds)


def land_kernel(
    slots, blocks, lanes, rank_ref, index_ref, third_ref, sum_ref, back_ref, home_ref, *refs
):
    thirds, out_ref = refs[:lanes], refs[lanes]
    total, late, sems = refs[lanes + 1 :]
    f32 = jnp.float32

    def arrive(at):
        step, half = divmod(at, 2)
        return pltpu.make_async_copy(thirds[step].at[half], late.at[at], sems.at[at])

    for at in range(1, 2 * lanes):

        @pl.when(third_ref[at] >= 0)
        def _():
            arrive(at).start()

    total[...] = sum_ref[...]
    total[blocks - 1] += back_ref[...].astype(f32)

    def one(slot, _):
        @pl.when(slot // 2 != rank_ref[0])
        def _():
            total[index_ref[slot]] += home_ref[slot].astype(f32)

    lax.fori_loop(0, slots, one, None)
    for at in range(1, 2 * lanes):

        @pl.when(third_ref[at] >= 0)
        def _():
            arrive(at).wait()
            total[third_ref[at]] += late[at].astype(f32)

    out_ref[...] = total[...].astype(out_ref.dtype)


def land(rank, index, third_index, sums, back, home, thirds):
    slots = index.shape[0]
    blocks = sums.shape[0]
    lanes = len(thirds)
    return pl.pallas_call(
        functools.partial(land_kernel, slots, blocks, lanes),
        out_shape=jax.ShapeDtypeStruct(sums.shape, jnp.bfloat16),
        in_specs=[SMEM, SMEM, SMEM, VMEM, VMEM, VMEM] + [ANY] * lanes,
        out_specs=VMEM,
        scratch_shapes=[
            pltpu.VMEM(sums.shape, jnp.float32),
            pltpu.VMEM((2 * lanes,) + home.shape[1:], home.dtype),
            pltpu.SemaphoreType.DMA((2 * lanes,)),
        ],
        compiler_params=params(),
        cost_estimate=cost(sums.size * 4, 6 * sums.size + 2 * home.size),
        name="land",
    )(rank, index, third_index, sums, back, home, *thirds)


def plan(key_lists, blocks, ctx_count, lanes):
    i32 = jnp.int32
    me = lax.axis_index("ctx")
    half, lane = me // lanes, me % lanes
    requests = 2 * blocks
    far_all = key_lists[:, 2:].reshape(ctx_count, requests)
    source, inside = far_all // blocks, far_all % blocks
    earlier = (jnp.arange(requests)[None, :] < jnp.arange(requests)[:, None])[None]
    rank = jnp.sum(((source[:, None, :] == source[:, :, None]) & earlier).astype(i32), axis=2)
    is_third = rank == 2
    order = jnp.sum((is_third[:, None, :] & earlier).astype(i32), axis=2)

    pair = jnp.arange(2, dtype=i32)[None, :, None]
    wanted = (source[:, None, :] == me) & (rank[:, None, :] == pair)
    send_main = jnp.sum(jnp.where(wanted, inside[:, None, :], 0), axis=2).reshape(-1)

    from_me = is_third & (source == me)
    third_of = jnp.sum(jnp.where(from_me, inside + 1, 0), axis=1) - 1
    step = jnp.arange(lanes, dtype=i32)[:, None]
    side = jnp.arange(2, dtype=i32)[None, :]
    asker = jnp.where(side == 0, half, 1 - half) * lanes + (lane + step) % lanes
    hit = asker[:, :, None] == jnp.arange(ctx_count, dtype=i32)[None, None, :]
    third_index = jnp.sum(jnp.where(hit, third_of[None, None, :], 0), axis=2).reshape(-1)

    def row(of, array):
        at = jnp.arange(ctx_count, dtype=i32)[:, None] == of
        return jnp.sum(jnp.where(at, array, 0), axis=0)

    slot_of = jnp.where(is_third, -1, source * 2 + rank)
    my_slot = row(me, slot_of)
    is_jth = (is_third[:, None, :] & (order[:, None, :] == pair)).astype(i32)
    third_source = jnp.sum(is_jth * source[:, None, :], axis=2)
    third_request = jnp.sum(is_jth * jnp.arange(requests, dtype=i32), axis=2)

    def steps(of):
        slab = row(of, third_source)
        return jnp.where(slab // lanes == half, (lane - slab % lanes + lanes) % lanes, -1)

    partner = (me + lanes) % ctx_count
    return (
        send_main,
        third_index,
        my_slot,
        row(me, third_request),
        steps(me),
        steps(partner),
    )


def body(queries, keys, values, out_grad, key_lists):
    ctx_count = lax.axis_size("ctx")
    blocks = lax.axis_size("head")
    lanes = ctx_count // 2
    send_main, third_index, my_slot, my_third, near_steps, cross_steps = plan(
        key_lists, blocks, ctx_count, lanes
    )

    def head_exchange(array):
        return lax.all_to_all(array, "head", split_axis=0, concat_axis=0, tiled=True)

    def ctx_exchange(array):
        return lax.all_to_all(array, "ctx", split_axis=0, concat_axis=0, tiled=True)

    def move(array, target):
        return lax.ppermute(array, "ctx", [(i, target(i)) for i in range(ctx_count)])

    def across(array):
        return move(array, lambda i: (i + lanes) % ctx_count)

    def along(arrays, sign):
        def target(step):
            return lambda i: i // lanes * lanes + (i + sign * step) % lanes

        return [arrays[0]] + [move(arrays[s], target(s)) for s in range(1, lanes)]

    kv = head_exchange(split_heads(keys, values))
    qg = head_exchange(split_heads(queries, out_grad))
    thirds = along(pick_third(jnp.maximum(third_index, 0), kv), 1)
    edge = move(kv[blocks - 1], lambda i: (i + 1) % ctx_count)
    to_send, qg, edge, thirds = lax.optimization_barrier(
        (pick_blocks(send_main, kv), qg, edge, thirds)
    )
    main = ctx_exchange(to_send)
    cross = across(pick_cross(cross_steps, thirds))
    out, main_grad, third_grad, edge_grad, sums = attend(
        my_slot, my_third, near_steps, qg, kv, edge, main, cross, thirds
    )
    cross_grad = across(third_grad)
    home = ctx_exchange(main_grad)
    back = move(edge_grad, lambda i: (i - 1) % ctx_count)
    late = along(pick_back(near_steps, cross_steps, third_grad, cross_grad, lanes), -1)
    out, home, back, late = lax.optimization_barrier((out, home, back, late))
    rank = lax.axis_index("ctx").reshape(1)
    attended, query_grad = join_heads(head_exchange(out))
    key_grad, value_grad = join_heads(
        head_exchange(land(rank, send_main, third_index, sums, back, home, late))
    )
    return attended, query_grad, key_grad, value_grad


def solution(mesh):
    tokens = P(("ctx", "head"), None)
    return jax.shard_map(
        body,
        mesh=mesh,
        in_specs=(tokens, tokens, tokens, tokens, P()),
        out_specs=(tokens, tokens, tokens, tokens),
        check_vma=False,
    )
```

time: 316 us -> 300 us (0.949)
  blocking collectives: 74.5 us -> 0 us
  starting transfers between devices: 33.6 us -> 72.8 us
  local copies, waits for them, and re-layouts: 2.71 us -> 13.7 us
  Pallas kernels: 27.6 us -> 31.5 us
    ppermute x2 -> x18, waiting for transfers between devices: 23.2 us -> 112 us  [move(): lax.ppermute(array, 'ctx', [(i, target(i)) for i in range(ctx_count)])]
    all_to_all x1 -> x0, blocking collectives: 74.5 us -> none  [ctx_exchange(): return lax.all_to_all(array, 'ctx', split_axis=0, concat_axis=0, tiled=True)]
    all_to_all x1 -> x2, waiting for transfers between devices: 60.3 us -> 0.01 us  [ctx_exchange(): return lax.all_to_all(array, 'ctx', split_axis=0, concat_axis=0, tiled=True)]
    ppermute x2 -> x18, starting transfers between devices: 0.23 us -> 36.6 us  [move(): lax.ppermute(array, 'ctx', [(i, target(i)) for i in range(ctx_count)])]
    all_to_all x4, waiting for transfers between devices: 90.5 us -> 64.9 us  [head_exchange(): lax.all_to_all(array, 'head', split_axis=0, concat_axis=0, tiled=True)]
    unnamed x16 -> x43, local copies, waits for them, and re-layouts: 2.1 us -> 13 us
    all_to_all x1 -> x2, starting transfers between devices: 8.64 us -> 13.4 us  [ctx_exchange(): return lax.all_to_all(array, 'ctx', split_axis=0, concat_axis=0, tiled=True)]
    pallas_call x2 -> x5, Pallas kernels: 20 us -> 24.3 us  [the longest x1 16.4 us: attend(): pl.pallas_call(functools.partial(attend_kernel, blocks, lanes), out_shape...]
  transfers between devices with their start and end apart: 7 -> 24, of which waited for: 7 -> 10; matrix products, arithmetic and copies ran while one was open for 0% -> 1% of each run, Pallas kernels for 3% -> 4%
where the time goes in v2:
time: 300 us; the launch traced here: 298 us
  waiting for transfers between devices  177 us (59%)
  starting transfers between devices  72.8 us (24%)
  Pallas kernels  31.5 us (10%)
  local copies, waits for them, and re-layouts  13.7 us (5%)
    ppermute x18, waiting for transfers between devices, move(): lax.ppermute(array, 'ctx', [(i, target(i)) for i in range(ctx_count)])  112 us
    all_to_all x4, waiting for transfers between devices, head_exchange(): lax.all_to_all(array, 'head', split_axis=0, concat_axis=0, tiled=True)  64.9 us
    ppermute x18, starting transfers between devices, move(): lax.ppermute(array, 'ctx', [(i, target(i)) for i in range(ctx_count)])  36.6 us
    all_to_all x4, starting transfers between devices, head_exchange(): lax.all_to_all(array, 'head', split_axis=0, concat_axis=0, tiled=True)  22.8 us
    pallas_call x1, Pallas kernels, attend(): pl.pallas_call(functools.partial(attend_kernel, blocks, lanes), out_shape...  16.4 us
    all_to_all x2, starting transfers between devices, ctx_exchange(): return lax.all_to_all(array, 'ctx', split_axis=0, concat_axis=0, tiled=True)  13.4 us
    unnamed x43, local copies, waits for them, and re-layouts  13 us
  transfers between devices with their start and end apart: 24, of which 10 were waited for; matrix products, arithmetic and copies ran while one was open for 1% of the time, Pallas kernels for 4%

profile of v2, /device:TPU:56, one launch (start us, length us, event | category | flops | bytes accessed | tf_op | source)
XLA Modules:
  0.0 298.1 jit_solution(1848666480884018828)
XLA Ops:
  4.0 8.5 %all-to-all-start = ((bf16[16,2,128,128]{3,2,1,0:T(8,128)(2,1)}), bf16[16,2,128,128]{3,2,1,0:T(8,128)(2,1)S(1)}, u32[]{:S(2)}, u32[]{:S(2)}) async-start(bf16[16,2,128,128]{3,2,1,0:T(8,128)(2,1)} %split_heads.2), calls=%async_computation | async-start | bytes 2097152 | tf_op jit(solution)/shard_map/all_to_all | solution.py:452
  14.5 23.6 %all-to-all-done.in_ref.kv_ref = bf16[16,2,128,128]{3,2,1,0:T(8,128)(2,1)S(1)} async-done(((bf16[16,2,128,128]{3,2,1,0:T(8,128)(2,1)}), bf16[16,2,128,128]{3,2,1,0:T(8,128)(2,1)S(1)}, u32[]{:S(2)}, u32[]{:S(2)}) %all-to-all-start) | async-done | bytes 1048608 | tf_op jit(solution)/shard_map/all_to_all | solution.py:452
  38.2 5.2 %all-to-all-start.1 = ((bf16[16,2,128,128]{3,2,1,0:T(8,128)(2,1)}), bf16[16,2,128,128]{3,2,1,0:T(8,128)(2,1)S(1)}, u32[]{:S(2)}, u32[]{:S(2)}) async-start(bf16[16,2,128,128]{3,2,1,0:T(8,128)(2,1)} %split_heads.3), calls=%async_computation.1 | async-start | bytes 2097152 | tf_op jit(solution)/shard_map/all_to_all | solution.py:452
  46.5 4.3 %collective-permute-start.1 = (bf16[2,2,128,128]{3,2,1,0:T(8,128)(2,1)S(1)}, bf16[2,2,128,128]{3,2,1,0:T(8,128)(2,1)S(1)}, u32[]{:S(2)}, u32[]{:S(2)}) collective-permute-start(bf16[2,2,128,128]{3,2,1,0:T(8,128)(2,1)S(1)} %get-tuple-element.52), channel_id=1, source_target_pairs={{0,16},{16,32},{32,48},{48,64},{64,80},{80,96},{96,112},{112,0},{1... | collective-permute-start | bytes 393224 | tf_op jit(solution)/shard_map/ppermute | solution.py:458
  50.8 3.4 %collective-permute-start.4 = (bf16[2,2,128,128]{3,2,1,0:T(8,128)(2,1)}, bf16[2,2,128,128]{3,2,1,0:T(8,128)(2,1)S(1)}, u32[]{:S(2)}, u32[]{:S(2)}) collective-permute-start(bf16[2,2,128,128]{3,2,1,0:T(8,128)(2,1)} %get-tuple-element.55), channel_id=1, source_target_pairs={{0,64},{16,80},{32,96},{48,112},{64,0},{80,16},{96,32},{112,48},{1... | collective-permute-start | bytes 393224 | tf_op jit(solution)/shard_map/ppermute | solution.py:458
  57.1 6.5 %collective-permute-start.7 = (bf16[2,2,128,128]{3,2,1,0:T(8,128)(2,1)S(1)}, bf16[2,2,128,128]{3,2,1,0:T(8,128)(2,1)S(1)}, u32[]{:S(2)}, u32[]{:S(2)}) collective-permute-start(bf16[2,2,128,128]{3,2,1,0:T(8,128)(2,1)S(1)} %get-tuple-element.58), channel_id=1, source_target_pairs={{0,112},{16,0},{32,16},{48,32},{64,48},{80,64},{96,80},{112,96},{1... | collective-permute-start | bytes 393224 | tf_op jit(solution)/shard_map/ppermute | solution.py:458
  64.3 2.1 pick_blocks.1
  66.5 3.0 %all-to-all-done.1.qg_ref = bf16[16,2,128,128]{3,2,1,0:T(8,128)(2,1)S(1)} async-done(((bf16[16,2,128,128]{3,2,1,0:T(8,128)(2,1)}), bf16[16,2,128,128]{3,2,1,0:T(8,128)(2,1)S(1)}, u32[]{:S(2)}, u32[]{:S(2)}) %all-to-all-start.1) | async-done | bytes 1048608 | tf_op jit(solution)/shard_map/all_to_all | solution.py:452
  69.5 8.5 %all-to-all-start.2 = ((bf16[32,2,128,128]{3,2,1,0:T(8,128)(2,1)}), bf16[32,2,128,128]{3,2,1,0:T(8,128)(2,1)}, u32[]{:S(2)}, u32[]{:S(2)}) async-start(bf16[32,2,128,128]{3,2,1,0:T(8,128)(2,1)} %pick_blocks.1), calls=%async_computation.2 | async-start | bytes 4194304 | tf_op jit(solution)/shard_map/all_to_all | solution.py:455
  79.0 5.5 %collective-permute-start.8 = (bf16[2,2,128,128]{3,2,1,0:T(8,128)(2,1)S(1)}, bf16[2,2,128,128]{3,2,1,0:T(8,128)(2,1)S(1)}, u32[]{:S(2)}, u32[]{:S(2)}) collective-permute-start(bf16[2,2,128,128]{3,2,1,0:T(8,128)(2,1)S(1)} %pick_cross.1), channel_id=1, source_target_pairs={{0,128},{16,144},{32,160},{48,176},{64,192},{80,208},{96,224},{112... | collective-permute-start | bytes 393224 | tf_op jit(solution)/shard_map/ppermute | solution.py:458
  84.6 50.7 %collective-permute-done.8.cross_ref = bf16[2,2,128,128]{3,2,1,0:T(8,128)(2,1)S(1)} collective-permute-done((bf16[2,2,128,128]{3,2,1,0:T(8,128)(2,1)S(1)}, bf16[2,2,128,128]{3,2,1,0:T(8,128)(2,1)S(1)}, u32[]{:S(2)}, u32[]{:S(2)}) %collective-permute-start.8) | collective-permute-done | bytes 131104 | tf_op jit(solution)/shard_map/ppermute | solution.py:458
  135.3 16.4 %attend.1 = (bf16[16,2,128,128]{3,2,1,0:T(8,128)(2,1)S(1)}, bf16[32,2,128,128]{3,2,1,0:T(8,128)(2,1)}, bf16[2,2,128,128]{3,2,1,0:T(8,128)(2,1)S(1)}, bf16[2,128,128]{2,1,0:T(8,128)(2,1)S(1)}, f32[16,2,128,128]{3,2,1,0:T(8,128)}) custom-call(s32[32]{0:T(128)S(1)} %select_reduce_fusion.4.slot_ref, s32[2]{0:T(128)S(1)} %get-tuple-element.102.third_ref, ...), custom_call_target="tpu_custom_call" | custom-call | flops 1342177280 | bytes 9437184 | tf_op jit(solution)/shard_map/attend/pallas_call | solution.py:312
  153.3 5.0 %all-to-all-start.3 = ((bf16[32,2,128,128]{3,2,1,0:T(8,128)(2,1)}), bf16[32,2,128,128]{3,2,1,0:T(8,128)(2,1)}, u32[]{:S(2)}, u32[]{:S(2)}) async-start(bf16[32,2,128,128]{3,2,1,0:T(8,128)(2,1)} %get-tuple-element.71), calls=%async_computation.3 | async-start | bytes 4194304 | tf_op jit(solution)/shard_map/all_to_all | solution.py:455
  158.3 5.5 %collective-permute-start.10 = (bf16[2,2,128,128]{3,2,1,0:T(8,128)(2,1)S(1)}, bf16[2,2,128,128]{3,2,1,0:T(8,128)(2,1)S(1)}, u32[]{:S(2)}, u32[]{:S(2)}) collective-permute-start(bf16[2,2,128,128]{3,2,1,0:T(8,128)(2,1)S(1)} %get-tuple-element.73.own_in), channel_id=1, source_target_pairs={{0,128},{16,144},{32,160},{48,176},{64,192},{80,208},{96,224},{112... | collective-permute-start | bytes 393224 | tf_op jit(solution)/shard_map/ppermute | solution.py:458
  163.7 51.7 %collective-permute-done.10.cross_in = bf16[2,2,128,128]{3,2,1,0:T(8,128)(2,1)S(1)} collective-permute-done((bf16[2,2,128,128]{3,2,1,0:T(8,128)(2,1)S(1)}, bf16[2,2,128,128]{3,2,1,0:T(8,128)(2,1)S(1)}, u32[]{:S(2)}, u32[]{:S(2)}) %collective-permute-start.10) | collective-permute-done | bytes 131104 | tf_op jit(solution)/shard_map/ppermute | solution.py:458
  221.9 2.5 collective-permute-done.9.back_ref
  225.1 3.1 %collective-permute-start.15 = (bf16[2,2,128,128]{3,2,1,0:T(8,128)(2,1)S(1)}, bf16[2,2,128,128]{3,2,1,0:T(8,128)(2,1)S(1)}, u32[]{:S(2)}, u32[]{:S(2)}) collective-permute-start(bf16[2,2,128,128]{3,2,1,0:T(8,128)(2,1)S(1)} %get-tuple-element.79), channel_id=1, source_target_pairs={{0,48},{16,64},{32,80},{48,96},{64,112},{80,0},{96,16},{112,32},{1... | collective-permute-start | bytes 393224 | tf_op jit(solution)/shard_map/ppermute | solution.py:458
  229.8 3.3 %collective-permute-done.14.refs_4_ = bf16[2,2,128,128]{3,2,1,0:T(8,128)(2,1)S(1)} collective-permute-done((bf16[2,2,128,128]{3,2,1,0:T(8,128)(2,1)S(1)}, bf16[2,2,128,128]{3,2,1,0:T(8,128)(2,1)S(1)}, u32[]{:S(2)}, u32[]{:S(2)}) %collective-permute-start.14) | collective-permute-done | bytes 131104 | tf_op jit(solution)/shard_map/ppermute | solution.py:458
  234.5 2.9 collective-permute-done.16.refs_6_
  238.7 3.6 %all-to-all-start.4 = ((bf16[16,2,128,128]{3,2,1,0:T(8,128)(2,1)}), bf16[16,2,128,128]{3,2,1,0:T(8,128)(2,1)S(1)}, u32[]{:S(2)}, u32[]{:S(2)}) async-start(bf16[16,2,128,128]{3,2,1,0:T(8,128)(2,1)} %copy-done.1), calls=%async_computation.4 | async-start | bytes 2097152 | tf_op jit(solution)/shard_map/all_to_all | solution.py:452
  247.6 4.1 %land.1 = bf16[16,2,128,128]{3,2,1,0:T(8,128)(2,1)} custom-call(s32[1]{0:T(128)} %bitcast.1.rank_ref, s32[32]{0:T(128)S(1)} %reshape.201.index_ref, s32[16]{0:T(128)S(1)} %reshape.202.third_ref, f32[16,2,128,128]{3,2,1,0:T(8,128)S(1)} %copy-done, bf16[2,128,128]{2,1,0:T(8,128)(2,1)S(1)} %copy-done.17, bf16[32,2,128,128]{3,2,1,0:T(8,128)(2,1)} %all-to-all-done.3.home_ref, ...), custom_call_target="tpu_custom_call" | custom-call | flops 2097152 | bytes 5242880 | tf_op jit(solution)/shard_map/land/pallas_call | solution.py:378
  251.8 14.6 %all-to-all-done.4.in_ref = bf16[16,2,128,128]{3,2,1,0:T(8,128)(2,1)S(1)} async-done(((bf16[16,2,128,128]{3,2,1,0:T(8,128)(2,1)}), bf16[16,2,128,128]{3,2,1,0:T(8,128)(2,1)S(1)}, u32[]{:S(2)}, u32[]{:S(2)}) %all-to-all-start.4) | async-done | bytes 1048608 | tf_op jit(solution)/shard_map/all_to_all | solution.py:452
  266.3 5.5 %all-to-all-start.5 = ((bf16[16,2,128,128]{3,2,1,0:T(8,128)(2,1)}), bf16[16,2,128,128]{3,2,1,0:T(8,128)(2,1)S(1)}, u32[]{:S(2)}, u32[]{:S(2)}) async-start(bf16[16,2,128,128]{3,2,1,0:T(8,128)(2,1)} %land.1), calls=%async_computation.5 | async-start | bytes 2097152 | tf_op jit(solution)/shard_map/all_to_all | solution.py:452
  273.1 23.7 %all-to-all-done.5.in_ref = bf16[16,2,128,128]{3,2,1,0:T(8,128)(2,1)S(1)} async-done(((bf16[16,2,128,128]{3,2,1,0:T(8,128)(2,1)}), bf16[16,2,128,128]{3,2,1,0:T(8,128)(2,1)S(1)}, u32[]{:S(2)}, u32[]{:S(2)}) %all-to-all-start.5) | async-done | bytes 1048608 | tf_op jit(solution)/shard_map/all_to_all | solution.py:452
  (107 shorter events, 33.9 us)
Async XLA Ops:
  4.0 34.2 %all-to-all-start = ((bf16[16,2,128,128]{3,2,1,0:T(8,128)(2,1)}), bf16[16,2,128,128]{3,2,1,0:T(8,128)(2,1)S(1)}, u32[]{:S(2)}, u32[]{:S(2)}) async-start(bf16[16,2,128,128]{3,2,1,0:T(8,128)(2,1)} %split_heads.2), calls=%async_computation | async-start | bytes 2097152 | tf_op jit(solution)/shard_map/all_to_all | solution.py:452
  38.2 31.3 %all-to-all-start.1 = ((bf16[16,2,128,128]{3,2,1,0:T(8,128)(2,1)}), bf16[16,2,128,128]{3,2,1,0:T(8,128)(2,1)S(1)}, u32[]{:S(2)}, u32[]{:S(2)}) async-start(bf16[16,2,128,128]{3,2,1,0:T(8,128)(2,1)} %split_heads.3), calls=%async_computation.1 | async-start | bytes 2097152 | tf_op jit(solution)/shard_map/all_to_all | solution.py:452
  44.4 9.8 %collective-permute-start = (bf16[2,128,128]{2,1,0:T(8,128)(2,1)S(1)}, bf16[2,128,128]{2,1,0:T(8,128)(2,1)S(1)}, u32[]{:S(2)}, u32[]{:S(2)}) collective-permute-start(bf16[2,128,128]{2,1,0:T(8,128)(2,1)S(1)} %slice_bitcast_fusion), channel_id=1, source_target_pairs={{0,16},{16,32},{32,48},{48,64},{64,80},{80,96},{96,112},{112,128},... | collective-permute-start | bytes 196616 | tf_op jit(solution)/shard_map/ppermute | solution.py:458
  46.5 7.8 %collective-permute-start.1 = (bf16[2,2,128,128]{3,2,1,0:T(8,128)(2,1)S(1)}, bf16[2,2,128,128]{3,2,1,0:T(8,128)(2,1)S(1)}, u32[]{:S(2)}, u32[]{:S(2)}) collective-permute-start(bf16[2,2,128,128]{3,2,1,0:T(8,128)(2,1)S(1)} %get-tuple-element.52), channel_id=1, source_target_pairs={{0,16},{16,32},{32,48},{48,64},{64,80},{80,96},{96,112},{112,0},{1... | collective-permute-start | bytes 393224 | tf_op jit(solution)/shard_map/ppermute | solution.py:458
  50.7 6.4 %collective-permute-start.2 = (bf16[2,2,128,128]{3,2,1,0:T(8,128)(2,1)S(1)}, bf16[2,2,128,128]{3,2,1,0:T(8,128)(2,1)S(1)}, u32[]{:S(2)}, u32[]{:S(2)}) collective-permute-start(bf16[2,2,128,128]{3,2,1,0:T(8,128)(2,1)S(1)} %get-tuple-element.53), channel_id=1, source_target_pairs={{0,32},{16,48},{32,64},{48,80},{64,96},{80,112},{96,0},{112,16},{1... | collective-permute-start | bytes 393224 | tf_op jit(solution)/shard_map/ppermute | solution.py:458
  50.8 18.8 %collective-permute-start.3 = (bf16[2,2,128,128]{3,2,1,0:T(8,128)(2,1)}, bf16[2,2,128,128]{3,2,1,0:T(8,128)(2,1)S(1)}, u32[]{:S(2)}, u32[]{:S(2)}) collective-permute-start(bf16[2,2,128,128]{3,2,1,0:T(8,128)(2,1)} %get-tuple-element.54), channel_id=1, source_target_pairs={{0,48},{16,64},{32,80},{48,96},{64,112},{80,0},{96,16},{112,32},{1... | collective-permute-start | bytes 393224 | tf_op jit(solution)/shard_map/ppermute | solution.py:458
  50.8 18.7 %collective-permute-start.4 = (bf16[2,2,128,128]{3,2,1,0:T(8,128)(2,1)}, bf16[2,2,128,128]{3,2,1,0:T(8,128)(2,1)S(1)}, u32[]{:S(2)}, u32[]{:S(2)}) collective-permute-start(bf16[2,2,128,128]{3,2,1,0:T(8,128)(2,1)} %get-tuple-element.55), channel_id=1, source_target_pairs={{0,64},{16,80},{32,96},{48,112},{64,0},{80,16},{96,32},{112,48},{1... | collective-permute-start | bytes 393224 | tf_op jit(solution)/shard_map/ppermute | solution.py:458
  54.3 15.2 %collective-permute-start.5 = (bf16[2,2,128,128]{3,2,1,0:T(8,128)(2,1)}, bf16[2,2,128,128]{3,2,1,0:T(8,128)(2,1)S(1)}, u32[]{:S(2)}, u32[]{:S(2)}) collective-permute-start(bf16[2,2,128,128]{3,2,1,0:T(8,128)(2,1)} %get-tuple-element.56), channel_id=1, source_target_pairs={{0,80},{16,96},{32,112},{48,0},{64,16},{80,32},{96,48},{112,64},{1... | collective-permute-start | bytes 393224 | tf_op jit(solution)/shard_map/ppermute | solution.py:458
  54.3 15.2 %collective-permute-start.6 = (bf16[2,2,128,128]{3,2,1,0:T(8,128)(2,1)S(1)}, bf16[2,2,128,128]{3,2,1,0:T(8,128)(2,1)S(1)}, u32[]{:S(2)}, u32[]{:S(2)}) collective-permute-start(bf16[2,2,128,128]{3,2,1,0:T(8,128)(2,1)S(1)} %get-tuple-element.57), channel_id=1, source_target_pairs={{0,96},{16,112},{32,0},{48,16},{64,32},{80,48},{96,64},{112,80},{1... | collective-permute-start | bytes 393224 | tf_op jit(solution)/shard_map/ppermute | solution.py:458
  57.1 12.4 %collective-permute-start.7 = (bf16[2,2,128,128]{3,2,1,0:T(8,128)(2,1)S(1)}, bf16[2,2,128,128]{3,2,1,0:T(8,128)(2,1)S(1)}, u32[]{:S(2)}, u32[]{:S(2)}) collective-permute-start(bf16[2,2,128,128]{3,2,1,0:T(8,128)(2,1)S(1)} %get-tuple-element.58), channel_id=1, source_target_pairs={{0,112},{16,0},{32,16},{48,32},{64,48},{80,64},{96,80},{112,96},{1... | collective-permute-start | bytes 393224 | tf_op jit(solution)/shard_map/ppermute | solution.py:458
  69.5 65.7 %all-to-all-start.2 = ((bf16[32,2,128,128]{3,2,1,0:T(8,128)(2,1)}), bf16[32,2,128,128]{3,2,1,0:T(8,128)(2,1)}, u32[]{:S(2)}, u32[]{:S(2)}) async-start(bf16[32,2,128,128]{3,2,1,0:T(8,128)(2,1)} %pick_blocks.1), calls=%async_computation.2 | async-start | bytes 4194304 | tf_op jit(solution)/shard_map/all_to_all | solution.py:455
  79.0 56.3 %collective-permute-start.8 = (bf16[2,2,128,128]{3,2,1,0:T(8,128)(2,1)S(1)}, bf16[2,2,128,128]{3,2,1,0:T(8,128)(2,1)S(1)}, u32[]{:S(2)}, u32[]{:S(2)}) collective-permute-start(bf16[2,2,128,128]{3,2,1,0:T(8,128)(2,1)S(1)} %pick_cross.1), channel_id=1, source_target_pairs={{0,128},{16,144},{32,160},{48,176},{64,192},{80,208},{96,224},{112... | collective-permute-start | bytes 393224 | tf_op jit(solution)/shard_map/ppermute | solution.py:458
  153.3 85.4 %all-to-all-start.3 = ((bf16[32,2,128,128]{3,2,1,0:T(8,128)(2,1)}), bf16[32,2,128,128]{3,2,1,0:T(8,128)(2,1)}, u32[]{:S(2)}, u32[]{:S(2)}) async-start(bf16[32,2,128,128]{3,2,1,0:T(8,128)(2,1)} %get-tuple-element.71), calls=%async_computation.3 | async-start | bytes 4194304 | tf_op jit(solution)/shard_map/all_to_all | solution.py:455
  158.3 57.1 %collective-permute-start.10 = (bf16[2,2,128,128]{3,2,1,0:T(8,128)(2,1)S(1)}, bf16[2,2,128,128]{3,2,1,0:T(8,128)(2,1)S(1)}, u32[]{:S(2)}, u32[]{:S(2)}) collective-permute-start(bf16[2,2,128,128]{3,2,1,0:T(8,128)(2,1)S(1)} %get-tuple-element.73.own_in), channel_id=1, source_target_pairs={{0,128},{16,144},{32,160},{48,176},{64,192},{80,208},{96,224},{112... | collective-permute-start | bytes 393224 | tf_op jit(solution)/shard_map/ppermute | solution.py:458
  216.4 11.7 %collective-permute-start.11 = (bf16[2,2,128,128]{3,2,1,0:T(8,128)(2,1)S(1)}, bf16[2,2,128,128]{3,2,1,0:T(8,128)(2,1)S(1)}, u32[]{:S(2)}, u32[]{:S(2)}) collective-permute-start(bf16[2,2,128,128]{3,2,1,0:T(8,128)(2,1)S(1)} %get-tuple-element.75), channel_id=1, source_target_pairs={{0,112},{16,0},{32,16},{48,32},{64,48},{80,64},{96,80},{112,96},{1... | collective-permute-start | bytes 393224 | tf_op jit(solution)/shard_map/ppermute | solution.py:458
  216.9 12.1 %collective-permute-start.12 = (bf16[2,2,128,128]{3,2,1,0:T(8,128)(2,1)S(1)}, bf16[2,2,128,128]{3,2,1,0:T(8,128)(2,1)S(1)}, u32[]{:S(2)}, u32[]{:S(2)}) collective-permute-start(bf16[2,2,128,128]{3,2,1,0:T(8,128)(2,1)S(1)} %get-tuple-element.76), channel_id=1, source_target_pairs={{0,96},{16,112},{32,0},{48,16},{64,32},{80,48},{96,64},{112,80},{1... | collective-permute-start | bytes 393224 | tf_op jit(solution)/shard_map/ppermute | solution.py:458
  218.3 6.2 %collective-permute-start.9 = (bf16[2,128,128]{2,1,0:T(8,128)(2,1)S(1)}, bf16[2,128,128]{2,1,0:T(8,128)(2,1)S(1)}, u32[]{:S(2)}, u32[]{:S(2)}) collective-permute-start(bf16[2,128,128]{2,1,0:T(8,128)(2,1)S(1)} %copy-done.19), channel_id=1, source_target_pairs={{0,240},{16,0},{32,16},{48,32},{64,48},{80,64},{96,80},{112,96},{1... | collective-permute-start | bytes 196616 | tf_op jit(solution)/shard_map/ppermute | solution.py:458
  219.0 10.2 %collective-permute-start.13 = (bf16[2,2,128,128]{3,2,1,0:T(8,128)(2,1)S(1)}, bf16[2,2,128,128]{3,2,1,0:T(8,128)(2,1)S(1)}, u32[]{:S(2)}, u32[]{:S(2)}) collective-permute-start(bf16[2,2,128,128]{3,2,1,0:T(8,128)(2,1)S(1)} %get-tuple-element.77), channel_id=1, source_target_pairs={{0,80},{16,96},{32,112},{48,0},{64,16},{80,32},{96,48},{112,64},{1... | collective-permute-start | bytes 393224 | tf_op jit(solution)/shard_map/ppermute | solution.py:458
  220.5 12.6 %collective-permute-start.14 = (bf16[2,2,128,128]{3,2,1,0:T(8,128)(2,1)S(1)}, bf16[2,2,128,128]{3,2,1,0:T(8,128)(2,1)S(1)}, u32[]{:S(2)}, u32[]{:S(2)}) collective-permute-start(bf16[2,2,128,128]{3,2,1,0:T(8,128)(2,1)S(1)} %get-tuple-element.78), channel_id=1, source_target_pairs={{0,64},{16,80},{32,96},{48,112},{64,0},{80,16},{96,32},{112,48},{1... | collective-permute-start | bytes 393224 | tf_op jit(solution)/shard_map/ppermute | solution.py:458
  225.1 8.7 %collective-permute-start.15 = (bf16[2,2,128,128]{3,2,1,0:T(8,128)(2,1)S(1)}, bf16[2,2,128,128]{3,2,1,0:T(8,128)(2,1)S(1)}, u32[]{:S(2)}, u32[]{:S(2)}) collective-permute-start(bf16[2,2,128,128]{3,2,1,0:T(8,128)(2,1)S(1)} %get-tuple-element.79), channel_id=1, source_target_pairs={{0,48},{16,64},{32,80},{48,96},{64,112},{80,0},{96,16},{112,32},{1... | collective-permute-start | bytes 393224 | tf_op jit(solution)/shard_map/ppermute | solution.py:458
  228.2 9.2 %collective-permute-start.16 = (bf16[2,2,128,128]{3,2,1,0:T(8,128)(2,1)S(1)}, bf16[2,2,128,128]{3,2,1,0:T(8,128)(2,1)S(1)}, u32[]{:S(2)}, u32[]{:S(2)}) collective-permute-start(bf16[2,2,128,128]{3,2,1,0:T(8,128)(2,1)S(1)} %get-tuple-element.80), channel_id=1, source_target_pairs={{0,32},{16,48},{32,64},{48,80},{64,96},{80,112},{96,0},{112,16},{1... | collective-permute-start | bytes 393224 | tf_op jit(solution)/shard_map/ppermute | solution.py:458
  229.0 9.0 %collective-permute-start.17 = (bf16[2,2,128,128]{3,2,1,0:T(8,128)(2,1)S(1)}, bf16[2,2,128,128]{3,2,1,0:T(8,128)(2,1)S(1)}, u32[]{:S(2)}, u32[]{:S(2)}) collective-permute-start(bf16[2,2,128,128]{3,2,1,0:T(8,128)(2,1)S(1)} %get-tuple-element.81), channel_id=1, source_target_pairs={{0,16},{16,32},{32,48},{48,64},{64,80},{80,96},{96,112},{112,0},{1... | collective-permute-start | bytes 393224 | tf_op jit(solution)/shard_map/ppermute | solution.py:458
  238.7 27.6 %all-to-all-start.4 = ((bf16[16,2,128,128]{3,2,1,0:T(8,128)(2,1)}), bf16[16,2,128,128]{3,2,1,0:T(8,128)(2,1)S(1)}, u32[]{:S(2)}, u32[]{:S(2)}) async-start(bf16[16,2,128,128]{3,2,1,0:T(8,128)(2,1)} %copy-done.1), calls=%async_computation.4 | async-start | bytes 2097152 | tf_op jit(solution)/shard_map/all_to_all | solution.py:452
  266.3 30.4 %all-to-all-start.5 = ((bf16[16,2,128,128]{3,2,1,0:T(8,128)(2,1)}), bf16[16,2,128,128]{3,2,1,0:T(8,128)(2,1)S(1)}, u32[]{:S(2)}, u32[]{:S(2)}) async-start(bf16[16,2,128,128]{3,2,1,0:T(8,128)(2,1)} %land.1), calls=%async_computation.5 | async-start | bytes 2097152 | tf_op jit(solution)/shard_map/all_to_all | solution.py:452
  (21 other events, 191.7 us)

commit v3 on v2

--- a/solution.py
+++ b/solution.py
@@ -218,8 +218,8 @@
     blocks, lanes, slot_ref, third_ref, near_ref, qg_ref, kv_ref, edge_ref, main_ref, cross_ref, *refs
 ):
     thirds = refs[:lanes]
-    out_ref, main_out, third_out, edge_out, sum_ref = refs[lanes : lanes + 5]
-    far, far_out, sems, out_sems, third_sems = refs[lanes + 5 :]
+    out, main_out, third_out, edge_out, sum_ref = refs[lanes : lanes + 5]
+    far, far_out, out_ref, sems, out_sems, third_sems, done_sems = refs[lanes + 5 :]
     requests = 2 * blocks
     scale = HEAD_DIM ** (-0.5)
     f32, bf16 = jnp.float32, jnp.bfloat16
@@ -232,6 +232,9 @@
 
     def leave(r, slot):
         return pltpu.make_async_copy(far_out.at[r], main_out.at[slot], out_sems.at[r])
+
+    def finished(n):
+        return pltpu.make_async_copy(out_ref.at[n], out.at[n], done_sems.at[n])
 
     def load(r, _):
         @pl.when(slot_ref[r] >= 0)
@@ -281,6 +284,7 @@
                 sum_ref[n - 1, which] += d[BLOCK : 2 * BLOCK]
             far_out[r2, which] = d[2 * BLOCK : 3 * BLOCK].astype(bf16)
             far_out[r3, which] = d[3 * BLOCK :].astype(bf16)
+        finished(n).start()
         for r in (r2, r3):
 
             @pl.when(slot_ref[r] >= 0)
@@ -301,6 +305,7 @@
             leave(r, 0).wait()
 
     lax.fori_loop(0, requests, finish, None)
+    lax.fori_loop(0, blocks, lambda n, _: finished(n).wait(), None)
     wait_all(lasts)
 
 
@@ -319,13 +324,15 @@
             jax.ShapeDtypeStruct(kv.shape, jnp.float32),
         ),
         in_specs=[SMEM, SMEM, SMEM, VMEM, VMEM, VMEM] + [ANY] * (2 + lanes),
-        out_specs=(VMEM, ANY, ANY, VMEM, VMEM),
+        out_specs=(ANY, ANY, ANY, VMEM, VMEM),
         scratch_shapes=[
             far,
             far,
+            pltpu.VMEM(qg.shape, bf16),
             pltpu.SemaphoreType.DMA((2 * blocks,)),
             pltpu.SemaphoreType.DMA((2 * blocks,)),
             pltpu.SemaphoreType.DMA((2,)),
+            pltpu.SemaphoreType.DMA((blocks,)),
         ],
         compiler_params=params(),
         cost_estimate=cost(
@@ -335,11 +342,9 @@
     )(slot, third, near, qg, kv, edge, main, cross, *thirds)
 
 
-def land_kernel(
-    slots, blocks, lanes, rank_ref, index_ref, third_ref, sum_ref, back_ref, home_ref, *refs
-):
-    thirds, out_ref = refs[:lanes], refs[lanes]
-    total, late, sems = refs[lanes + 1 :]
+def land_thirds_kernel(blocks, lanes, third_ref, sum_ref, back_ref, *refs):
+    thirds, total = refs[:lanes], refs[lanes]
+    late, sems = refs[lanes + 1 :]
     f32 = jnp.float32
 
     def arrive(at):
@@ -354,13 +359,6 @@
 
     total[...] = sum_ref[...]
     total[blocks - 1] += back_ref[...].astype(f32)
-
-    def one(slot, _):
-        @pl.when(slot // 2 != rank_ref[0])
-        def _():
-            total[index_ref[slot]] += home_ref[slot].astype(f32)
-
-    lax.fori_loop(0, slots, one, None)
     for at in range(1, 2 * lanes):
 
         @pl.when(third_ref[at] >= 0)
@@ -368,27 +366,79 @@
             arrive(at).wait()
             total[third_ref[at]] += late[at].astype(f32)
 
-    out_ref[...] = total[...].astype(out_ref.dtype)
-
-
-def land(rank, index, third_index, sums, back, home, thirds):
+
+def land_thirds(third_index, sums, back, thirds):
+    blocks = sums.shape[0]
+    lanes = len(thirds)
+    return pl.pallas_call(
+        functools.partial(land_thirds_kernel, blocks, lanes),
+        out_shape=jax.ShapeDtypeStruct(sums.shape, jnp.float32),
+        in_specs=[SMEM, VMEM, VMEM] + [ANY] * lanes,
+        out_specs=VMEM,
+        scratch_shapes=[
+            pltpu.VMEM((2 * lanes,) + back.shape, back.dtype),
+            pltpu.SemaphoreType.DMA((2 * lanes,)),
+        ],
+        compiler_params=params(),
+        cost_estimate=cost(sums.size * 2, 8 * sums.size),
+        name="land_thirds",
+    )(third_index, sums, back, *thirds)
+
+
+def land_kernel(
+    slots, blocks, rank_ref, index_ref, sums, home, out, total, late, low, sum_sems, home_sems, out_sems
+):
+    def read(n):
+        return pltpu.make_async_copy(sums.at[n], total.at[n], sum_sems.at[n])
+
+    def arrive(slot):
+        return pltpu.make_async_copy(home.at[slot], late.at[slot], home_sems.at[slot])
+
+    def write(n):
+        return pltpu.make_async_copy(low.at[n], out.at[n], out_sems.at[n])
+
+    start_all([read(n) for n in range(blocks)])
+    start_all([arrive(slot) for slot in range(slots)])
+    wait_all([read(n) for n in range(blocks)])
+
+    def one(slot, _):
+        arrive(slot).wait()
+
+        @pl.when(slot // 2 != rank_ref[0])
+        def _():
+            total[index_ref[slot]] += late[slot].astype(jnp.float32)
+
+    lax.fori_loop(0, slots, one, None)
+
+    def put(n, _):
+        low[n] = total[n].astype(low.dtype)
+        write(n).start()
+
+    lax.fori_loop(0, blocks, put, None)
+    wait_all([write(n) for n in range(blocks)])
+
+
+def land(rank, index, sums, home):
     slots = index.shape[0]
     blocks = sums.shape[0]
-    lanes = len(thirds)
-    return pl.pallas_call(
-        functools.partial(land_kernel, slots, blocks, lanes),
-        out_shape=jax.ShapeDtypeStruct(sums.shape, jnp.bfloat16),
-        in_specs=[SMEM, SMEM, SMEM, VMEM, VMEM, VMEM] + [ANY] * lanes,
-        out_specs=VMEM,
+    bf16 = jnp.bfloat16
+    return pl.pallas_call(
+        functools.partial(land_kernel, slots, blocks),
+        out_shape=jax.ShapeDtypeStruct(sums.shape, bf16),
+        in_specs=[SMEM, SMEM, ANY, ANY],
+        out_specs=ANY,
         scratch_shapes=[
             pltpu.VMEM(sums.shape, jnp.float32),
-            pltpu.VMEM((2 * lanes,) + home.shape[1:], home.dtype),
-            pltpu.SemaphoreType.DMA((2 * lanes,)),
+            pltpu.VMEM(home.shape, bf16),
+            pltpu.VMEM(sums.shape, bf16),
+            pltpu.SemaphoreType.DMA((blocks,)),
+            pltpu.SemaphoreType.DMA((slots,)),
+            pltpu.SemaphoreType.DMA((blocks,)),
         ],
         compiler_params=params(),
-        cost_estimate=cost(sums.size * 4, 6 * sums.size + 2 * home.size),
+        cost_estimate=cost(sums.size * 2, 6 * sums.size + 2 * home.size),
         name="land",
-    )(rank, index, third_index, sums, back, home, *thirds)
+    )(rank, index, sums, home)
 
 
 def plan(key_lists, blocks, ctx_count, lanes):
@@ -470,24 +520,24 @@
     qg = head_exchange(split_heads(queries, out_grad))
     thirds = along(pick_third(jnp.maximum(third_index, 0), kv), 1)
     edge = move(kv[blocks - 1], lambda i: (i + 1) % ctx_count)
-    to_send, qg, edge, thirds = lax.optimization_barrier(
-        (pick_blocks(send_main, kv), qg, edge, thirds)
+    cross = across(pick_cross(cross_steps, thirds))
+    to_send, qg, edge, cross = lax.optimization_barrier(
+        (pick_blocks(send_main, kv), qg, edge, cross)
     )
     main = ctx_exchange(to_send)
-    cross = across(pick_cross(cross_steps, thirds))
     out, main_grad, third_grad, edge_grad, sums = attend(
         my_slot, my_third, near_steps, qg, kv, edge, main, cross, thirds
     )
+    out = head_exchange(out)
     cross_grad = across(third_grad)
+    back = move(edge_grad, lambda i: (i - 1) % ctx_count)
+    main_grad, out, cross_grad, back = lax.optimization_barrier((main_grad, out, cross_grad, back))
     home = ctx_exchange(main_grad)
-    back = move(edge_grad, lambda i: (i - 1) % ctx_count)
     late = along(pick_back(near_steps, cross_steps, third_grad, cross_grad, lanes), -1)
-    out, home, back, late = lax.optimization_barrier((out, home, back, late))
+    sums = land_thirds(third_index, sums, back, late)
     rank = lax.axis_index("ctx").reshape(1)
-    attended, query_grad = join_heads(head_exchange(out))
-    key_grad, value_grad = join_heads(
-        head_exchange(land(rank, send_main, third_index, sums, back, home, late))
-    )
+    attended, query_grad = join_heads(out)
+    key_grad, value_grad = join_heads(head_exchange(land(rank, send_main, sums, home)))
     return attended, query_grad, key_grad, value_grad
 
 

time: 300 us -> 299 us (level)
  starting transfers between devices: 72.8 us -> 63.6 us
  Pallas kernels: 31.5 us -> 38 us
  waiting for transfers between devices: 177 us -> 183 us
  local copies, waits for them, and re-layouts: 13.7 us -> 9.59 us
    all_to_all x2, waiting for transfers between devices: 0.01 us -> 74.5 us  [ctx_exchange(): return lax.all_to_all(array, 'ctx', split_axis=0, concat_axis=0, tiled=True)]
    ppermute x18, waiting for transfers between devices: 112 us -> 47.5 us  [move(): lax.ppermute(array, 'ctx', [(i, target(i)) for i in range(ctx_count)])]
    ppermute x18, starting transfers between devices: 36.6 us -> 21.3 us  [move(): lax.ppermute(array, 'ctx', [(i, target(i)) for i in range(ctx_count)])]
    pallas_call x1 -> x2, Pallas kernels: 4.14 us -> 10.3 us  [the longest x1 9.02 us: land(): pl.pallas_call(functools.partial(land_kernel, slots, blocks), out_shape=j...]
    all_to_all x4, starting transfers between devices: 22.8 us -> 27.8 us  [head_exchange(): lax.all_to_all(array, 'head', split_axis=0, concat_axis=0, tiled=True)]
    unnamed x43 -> x23, local copies, waits for them, and re-layouts: 13 us -> 8.31 us
    all_to_all x4, waiting for transfers between devices: 64.9 us -> 61.4 us  [head_exchange(): lax.all_to_all(array, 'head', split_axis=0, concat_axis=0, tiled=True)]
  transfers between devices with their start and end apart: 24 -> 24, of which waited for: 10 -> 16; matrix products, arithmetic and copies ran while one was open for 1% -> 1% of each run, Pallas kernels for 4% -> 3%
where the time goes in v3:
time: 299 us; the launch traced here: 298 us
  waiting for transfers between devices  183 us (61%)
  starting transfers between devices  63.6 us (21%)
  Pallas kernels  38 us (13%)
  local copies, waits for them, and re-layouts  9.59 us (3%)
    all_to_all x2, waiting for transfers between devices, ctx_exchange(): return lax.all_to_all(array, 'ctx', split_axis=0, concat_axis=0, tiled=True)  74.5 us
    all_to_all x4, waiting for transfers between devices, head_exchange(): lax.all_to_all(array, 'head', split_axis=0, concat_axis=0, tiled=True)  61.4 us
    ppermute x18, waiting for transfers between devices, move(): lax.ppermute(array, 'ctx', [(i, target(i)) for i in range(ctx_count)])  47.5 us
    all_to_all x4, starting transfers between devices, head_exchange(): lax.all_to_all(array, 'head', split_axis=0, concat_axis=0, tiled=True)  27.8 us
    ppermute x18, starting transfers between devices, move(): lax.ppermute(array, 'ctx', [(i, target(i)) for i in range(ctx_count)])  21.3 us
    pallas_call x1, Pallas kernels, attend(): pl.pallas_call(functools.partial(attend_kernel, blocks, lanes), out_shape...  16.6 us
    all_to_all x2, starting transfers between devices, ctx_exchange(): return lax.all_to_all(array, 'ctx', split_axis=0, concat_axis=0, tiled=True)  14.5 us
    pallas_call x1, Pallas kernels, land(): pl.pallas_call(functools.partial(land_kernel, slots, blocks), out_shape=j...  9.02 us
  transfers between devices with their start and end apart: 24, of which 16 were waited for; matrix products, arithmetic and copies ran while one was open for 1% of the time, Pallas kernels for 3%

profile of v3, /device:TPU:56, one launch (start us, length us, event | category | flops | bytes accessed | tf_op | source)
XLA Modules:
  0.0 297.7 jit_solution(5279463455799019715)
XLA Ops:
  4.0 8.5 %all-to-all-start = ((bf16[16,2,128,128]{3,2,1,0:T(8,128)(2,1)}), bf16[16,2,128,128]{3,2,1,0:T(8,128)(2,1)S(1)}, u32[]{:S(2)}, u32[]{:S(2)}) async-start(bf16[16,2,128,128]{3,2,1,0:T(8,128)(2,1)} %split_heads.2), calls=%async_computation | async-start | bytes 2097152 | tf_op jit(solution)/shard_map/all_to_all | solution.py:502
  15.2 23.1 %all-to-all-done.in_ref.kv_ref = bf16[16,2,128,128]{3,2,1,0:T(8,128)(2,1)S(1)} async-done(((bf16[16,2,128,128]{3,2,1,0:T(8,128)(2,1)}), bf16[16,2,128,128]{3,2,1,0:T(8,128)(2,1)S(1)}, u32[]{:S(2)}, u32[]{:S(2)}) %all-to-all-start) | async-done | bytes 1048608 | tf_op jit(solution)/shard_map/all_to_all | solution.py:502
  38.2 5.2 %all-to-all-start.1 = ((bf16[16,2,128,128]{3,2,1,0:T(8,128)(2,1)}), bf16[16,2,128,128]{3,2,1,0:T(8,128)(2,1)S(1)}, u32[]{:S(2)}, u32[]{:S(2)}) async-start(bf16[16,2,128,128]{3,2,1,0:T(8,128)(2,1)} %split_heads.3), calls=%async_computation.1 | async-start | bytes 2097152 | tf_op jit(solution)/shard_map/all_to_all | solution.py:502
  47.1 2.6 collective-permute-start.3
  55.2 2.3 collective-permute-done.4.refs_4_
  57.5 2.5 collective-permute-done.5.refs_5_
  62.6 4.6 %collective-permute-start.8 = (bf16[2,2,128,128]{3,2,1,0:T(8,128)(2,1)S(1)}, bf16[2,2,128,128]{3,2,1,0:T(8,128)(2,1)S(1)}, u32[]{:S(2)}, u32[]{:S(2)}) collective-permute-start(bf16[2,2,128,128]{3,2,1,0:T(8,128)(2,1)S(1)} %pick_cross.1), channel_id=1, source_target_pairs={{0,128},{16,144},{32,160},{48,176},{64,192},{80,208},{96,224},{112... | collective-permute-start | bytes 393224 | tf_op jit(solution)/shard_map/ppermute | solution.py:508
  71.8 2.7 collective-permute-done.8.cross_ref
  74.5 10.0 %all-to-all-start.2 = ((bf16[32,2,128,128]{3,2,1,0:T(8,128)(2,1)}), bf16[32,2,128,128]{3,2,1,0:T(8,128)(2,1)}, u32[]{:S(2)}, u32[]{:S(2)}) async-start(bf16[32,2,128,128]{3,2,1,0:T(8,128)(2,1)} %pick_blocks.1), calls=%async_computation.2 | async-start | bytes 4194304 | tf_op jit(solution)/shard_map/all_to_all | solution.py:505
  84.6 51.3 %all-to-all-done.2.main_ref = bf16[32,2,128,128]{3,2,1,0:T(8,128)(2,1)} async-done(((bf16[32,2,128,128]{3,2,1,0:T(8,128)(2,1)}), bf16[32,2,128,128]{3,2,1,0:T(8,128)(2,1)}, u32[]{:S(2)}, u32[]{:S(2)}) %all-to-all-start.2) | async-done | bytes 2097184 | tf_op jit(solution)/shard_map/all_to_all | solution.py:505
  135.9 16.6 %attend.1 = (bf16[16,2,128,128]{3,2,1,0:T(8,128)(2,1)}, bf16[32,2,128,128]{3,2,1,0:T(8,128)(2,1)}, bf16[2,2,128,128]{3,2,1,0:T(8,128)(2,1)S(1)}, bf16[2,128,128]{2,1,0:T(8,128)(2,1)S(1)}, f32[16,2,128,128]{3,2,1,0:T(8,128)}) custom-call(s32[32]{0:T(128)S(1)} %select_reduce_fusion.4.slot_ref, s32[2]{0:T(128)S(1)} %get-tuple-element.74.third_ref, ...), custom_call_target="tpu_custom_call" | custom-call | flops 1342177280 | bytes 9437184 | tf_op jit(solution)/shard_map/attend/pallas_call | solution.py:317
  153.2 9.7 %all-to-all-start.3 = ((bf16[16,2,128,128]{3,2,1,0:T(8,128)(2,1)}), bf16[16,2,128,128]{3,2,1,0:T(8,128)(2,1)S(1)}, u32[]{:S(2)}, u32[]{:S(2)}) async-start(bf16[16,2,128,128]{3,2,1,0:T(8,128)(2,1)} %get-tuple-element.50), calls=%async_computation.3 | async-start | bytes 2097152 | tf_op jit(solution)/shard_map/all_to_all | solution.py:502
  165.3 15.5 %collective-permute-done.9.cross_in = bf16[2,2,128,128]{3,2,1,0:T(8,128)(2,1)S(1)} collective-permute-done((bf16[2,2,128,128]{3,2,1,0:T(8,128)(2,1)S(1)}, bf16[2,2,128,128]{3,2,1,0:T(8,128)(2,1)S(1)}, u32[]{:S(2)}, u32[]{:S(2)}) %collective-permute-start.9) | collective-permute-done | bytes 131104 | tf_op jit(solution)/shard_map/ppermute | solution.py:508
  180.8 13.5 %all-to-all-done.3.in_ref = bf16[16,2,128,128]{3,2,1,0:T(8,128)(2,1)S(1)} async-done(((bf16[16,2,128,128]{3,2,1,0:T(8,128)(2,1)}), bf16[16,2,128,128]{3,2,1,0:T(8,128)(2,1)S(1)}, u32[]{:S(2)}, u32[]{:S(2)}) %all-to-all-start.3) | async-done | bytes 1048608 | tf_op jit(solution)/shard_map/all_to_all | solution.py:502
  194.3 4.5 %all-to-all-start.4 = ((bf16[32,2,128,128]{3,2,1,0:T(8,128)(2,1)}), bf16[32,2,128,128]{3,2,1,0:T(8,128)(2,1)S(1)}, u32[]{:S(2)}, u32[]{:S(2)}) async-start(bf16[32,2,128,128]{3,2,1,0:T(8,128)(2,1)} %get-tuple-element.67), calls=%async_computation.4 | async-start | bytes 4194304 | tf_op jit(solution)/shard_map/all_to_all | solution.py:505
  201.6 2.7 collective-permute-start.14
  206.4 8.0 %collective-permute-done.11.refs_1_ = bf16[2,2,128,128]{3,2,1,0:T(8,128)(2,1)S(1)} collective-permute-done((bf16[2,2,128,128]{3,2,1,0:T(8,128)(2,1)S(1)}, bf16[2,2,128,128]{3,2,1,0:T(8,128)(2,1)S(1)}, u32[]{:S(2)}, u32[]{:S(2)}) %collective-permute-start.11) | collective-permute-done | bytes 131104 | tf_op jit(solution)/shard_map/ppermute | solution.py:508
  214.3 3.0 collective-permute-done.12.refs_2_
  217.3 2.6 collective-permute-done.13.refs_3_
  219.9 6.9 %collective-permute-done.14.refs_4_ = bf16[2,2,128,128]{3,2,1,0:T(8,128)(2,1)S(1)} collective-permute-done((bf16[2,2,128,128]{3,2,1,0:T(8,128)(2,1)S(1)}, bf16[2,2,128,128]{3,2,1,0:T(8,128)(2,1)S(1)}, u32[]{:S(2)}, u32[]{:S(2)}) %collective-permute-start.14) | collective-permute-done | bytes 131104 | tf_op jit(solution)/shard_map/ppermute | solution.py:508
  231.1 23.2 %all-to-all-done.4.home = bf16[32,2,128,128]{3,2,1,0:T(8,128)(2,1)S(1)} async-done(((bf16[32,2,128,128]{3,2,1,0:T(8,128)(2,1)}), bf16[32,2,128,128]{3,2,1,0:T(8,128)(2,1)S(1)}, u32[]{:S(2)}, u32[]{:S(2)}) %all-to-all-start.4) | async-done | bytes 2097184 | tf_op jit(solution)/shard_map/all_to_all | solution.py:505
  255.8 9.0 %land.1 = bf16[16,2,128,128]{3,2,1,0:T(8,128)(2,1)S(1)} custom-call(s32[1]{0:T(128)} %bitcast.1.rank_ref, s32[32]{0:T(128)S(1)} %reshape.201.index_ref, f32[16,2,128,128]{3,2,1,0:T(8,128)S(1)} %copy-done.1, bf16[32,2,128,128]{3,2,1,0:T(8,128)(2,1)S(1)} %all-to-all-done.4.home), custom_call_target="tpu_custom_call" | custom-call | flops 1048576 | bytes 5242880 | tf_op jit(solution)/shard_map/land/pallas_call | solution.py:425
  265.8 4.4 %all-to-all-start.5 = ((bf16[16,2,128,128]{3,2,1,0:T(8,128)(2,1)}), bf16[16,2,128,128]{3,2,1,0:T(8,128)(2,1)S(1)}, u32[]{:S(2)}, u32[]{:S(2)}) async-start(bf16[16,2,128,128]{3,2,1,0:T(8,128)(2,1)} %copy-done.2), calls=%async_computation.5 | async-start | bytes 2097152 | tf_op jit(solution)/shard_map/all_to_all | solution.py:502
  271.5 24.8 %all-to-all-done.5.in_ref = bf16[16,2,128,128]{3,2,1,0:T(8,128)(2,1)S(1)} async-done(((bf16[16,2,128,128]{3,2,1,0:T(8,128)(2,1)}), bf16[16,2,128,128]{3,2,1,0:T(8,128)(2,1)S(1)}, u32[]{:S(2)}, u32[]{:S(2)}) %all-to-all-start.5) | async-done | bytes 1048608 | tf_op jit(solution)/shard_map/all_to_all | solution.py:502
  (88 shorter events, 39.3 us)
Async XLA Ops:
  4.0 34.2 %all-to-all-start = ((bf16[16,2,128,128]{3,2,1,0:T(8,128)(2,1)}), bf16[16,2,128,128]{3,2,1,0:T(8,128)(2,1)S(1)}, u32[]{:S(2)}, u32[]{:S(2)}) async-start(bf16[16,2,128,128]{3,2,1,0:T(8,128)(2,1)} %split_heads.2), calls=%async_computation | async-start | bytes 2097152 | tf_op jit(solution)/shard_map/all_to_all | solution.py:502
  38.2 33.5 %all-to-all-start.1 = ((bf16[16,2,128,128]{3,2,1,0:T(8,128)(2,1)}), bf16[16,2,128,128]{3,2,1,0:T(8,128)(2,1)S(1)}, u32[]{:S(2)}, u32[]{:S(2)}) async-start(bf16[16,2,128,128]{3,2,1,0:T(8,128)(2,1)} %split_heads.3), calls=%async_computation.1 | async-start | bytes 2097152 | tf_op jit(solution)/shard_map/all_to_all | solution.py:502
  46.6 6.1 %collective-permute-start.1 = (bf16[2,2,128,128]{3,2,1,0:T(8,128)(2,1)S(1)}, bf16[2,2,128,128]{3,2,1,0:T(8,128)(2,1)S(1)}, u32[]{:S(2)}, u32[]{:S(2)}) collective-permute-start(bf16[2,2,128,128]{3,2,1,0:T(8,128)(2,1)S(1)} %get-tuple-element.38), channel_id=1, source_target_pairs={{0,16},{16,32},{32,48},{48,64},{64,80},{80,96},{96,112},{112,0},{1... | collective-permute-start | bytes 393224 | tf_op jit(solution)/shard_map/ppermute | solution.py:508
  46.7 6.4 %collective-permute-start.2 = (bf16[2,2,128,128]{3,2,1,0:T(8,128)(2,1)S(1)}, bf16[2,2,128,128]{3,2,1,0:T(8,128)(2,1)S(1)}, u32[]{:S(2)}, u32[]{:S(2)}) collective-permute-start(bf16[2,2,128,128]{3,2,1,0:T(8,128)(2,1)S(1)} %get-tuple-element.39), channel_id=1, source_target_pairs={{0,32},{16,48},{32,64},{48,80},{64,96},{80,112},{96,0},{112,16},{1... | collective-permute-start | bytes 393224 | tf_op jit(solution)/shard_map/ppermute | solution.py:508
  47.1 8.1 %collective-permute-start.3 = (bf16[2,2,128,128]{3,2,1,0:T(8,128)(2,1)S(1)}, bf16[2,2,128,128]{3,2,1,0:T(8,128)(2,1)S(1)}, u32[]{:S(2)}, u32[]{:S(2)}) collective-permute-start(bf16[2,2,128,128]{3,2,1,0:T(8,128)(2,1)S(1)} %get-tuple-element.40), channel_id=1, source_target_pairs={{0,48},{16,64},{32,80},{48,96},{64,112},{80,0},{96,16},{112,32},{1... | collective-permute-start | bytes 393224 | tf_op jit(solution)/shard_map/ppermute | solution.py:508
  49.7 7.8 %collective-permute-start.4 = (bf16[2,2,128,128]{3,2,1,0:T(8,128)(2,1)S(1)}, bf16[2,2,128,128]{3,2,1,0:T(8,128)(2,1)S(1)}, u32[]{:S(2)}, u32[]{:S(2)}) collective-permute-start(bf16[2,2,128,128]{3,2,1,0:T(8,128)(2,1)S(1)} %get-tuple-element.41), channel_id=1, source_target_pairs={{0,64},{16,80},{32,96},{48,112},{64,0},{80,16},{96,32},{112,48},{1... | collective-permute-start | bytes 393224 | tf_op jit(solution)/shard_map/ppermute | solution.py:508
  50.7 9.4 %collective-permute-start.5 = (bf16[2,2,128,128]{3,2,1,0:T(8,128)(2,1)S(1)}, bf16[2,2,128,128]{3,2,1,0:T(8,128)(2,1)S(1)}, u32[]{:S(2)}, u32[]{:S(2)}) collective-permute-start(bf16[2,2,128,128]{3,2,1,0:T(8,128)(2,1)S(1)} %get-tuple-element.42), channel_id=1, source_target_pairs={{0,80},{16,96},{32,112},{48,0},{64,16},{80,32},{96,48},{112,64},{1... | collective-permute-start | bytes 393224 | tf_op jit(solution)/shard_map/ppermute | solution.py:508
  52.7 9.1 %collective-permute-start.6 = (bf16[2,2,128,128]{3,2,1,0:T(8,128)(2,1)S(1)}, bf16[2,2,128,128]{3,2,1,0:T(8,128)(2,1)S(1)}, u32[]{:S(2)}, u32[]{:S(2)}) collective-permute-start(bf16[2,2,128,128]{3,2,1,0:T(8,128)(2,1)S(1)} %get-tuple-element.43), channel_id=1, source_target_pairs={{0,96},{16,112},{32,0},{48,16},{64,32},{80,48},{96,64},{112,80},{1... | collective-permute-start | bytes 393224 | tf_op jit(solution)/shard_map/ppermute | solution.py:508
  53.0 8.8 %collective-permute-start.7 = (bf16[2,2,128,128]{3,2,1,0:T(8,128)(2,1)S(1)}, bf16[2,2,128,128]{3,2,1,0:T(8,128)(2,1)S(1)}, u32[]{:S(2)}, u32[]{:S(2)}) collective-permute-start(bf16[2,2,128,128]{3,2,1,0:T(8,128)(2,1)S(1)} %get-tuple-element.44), channel_id=1, source_target_pairs={{0,112},{16,0},{32,16},{48,32},{64,48},{80,64},{96,80},{112,96},{1... | collective-permute-start | bytes 393224 | tf_op jit(solution)/shard_map/ppermute | solution.py:508
  62.6 11.9 %collective-permute-start.8 = (bf16[2,2,128,128]{3,2,1,0:T(8,128)(2,1)S(1)}, bf16[2,2,128,128]{3,2,1,0:T(8,128)(2,1)S(1)}, u32[]{:S(2)}, u32[]{:S(2)}) collective-permute-start(bf16[2,2,128,128]{3,2,1,0:T(8,128)(2,1)S(1)} %pick_cross.1), channel_id=1, source_target_pairs={{0,128},{16,144},{32,160},{48,176},{64,192},{80,208},{96,224},{112... | collective-permute-start | bytes 393224 | tf_op jit(solution)/shard_map/ppermute | solution.py:508
  67.8 4.0 %collective-permute-start = (bf16[2,128,128]{2,1,0:T(8,128)(2,1)}, bf16[2,128,128]{2,1,0:T(8,128)(2,1)S(1)}, u32[]{:S(2)}, u32[]{:S(2)}) collective-permute-start(bf16[2,128,128]{2,1,0:T(8,128)(2,1)} %slice_bitcast_fusion), channel_id=1, source_target_pairs={{0,16},{16,32},{32,48},{48,64},{64,80},{80,96},{96,112},{112,128},... | collective-permute-start | bytes 196616 | tf_op jit(solution)/shard_map/ppermute | solution.py:508
  74.5 61.4 %all-to-all-start.2 = ((bf16[32,2,128,128]{3,2,1,0:T(8,128)(2,1)}), bf16[32,2,128,128]{3,2,1,0:T(8,128)(2,1)}, u32[]{:S(2)}, u32[]{:S(2)}) async-start(bf16[32,2,128,128]{3,2,1,0:T(8,128)(2,1)} %pick_blocks.1), calls=%async_computation.2 | async-start | bytes 4194304 | tf_op jit(solution)/shard_map/all_to_all | solution.py:505
  153.2 41.2 %all-to-all-start.3 = ((bf16[16,2,128,128]{3,2,1,0:T(8,128)(2,1)}), bf16[16,2,128,128]{3,2,1,0:T(8,128)(2,1)S(1)}, u32[]{:S(2)}, u32[]{:S(2)}) async-start(bf16[16,2,128,128]{3,2,1,0:T(8,128)(2,1)} %get-tuple-element.50), calls=%async_computation.3 | async-start | bytes 2097152 | tf_op jit(solution)/shard_map/all_to_all | solution.py:502
  162.9 17.9 %collective-permute-start.9 = (bf16[2,2,128,128]{3,2,1,0:T(8,128)(2,1)S(1)}, bf16[2,2,128,128]{3,2,1,0:T(8,128)(2,1)S(1)}, u32[]{:S(2)}, u32[]{:S(2)}) collective-permute-start(bf16[2,2,128,128]{3,2,1,0:T(8,128)(2,1)S(1)} %get-tuple-element.51.own_in), channel_id=1, source_target_pairs={{0,128},{16,144},{32,160},{48,176},{64,192},{80,208},{96,224},{112... | collective-permute-start | bytes 393224 | tf_op jit(solution)/shard_map/ppermute | solution.py:508
  163.4 1.9 collective-permute-start.10
  194.3 59.9 %all-to-all-start.4 = ((bf16[32,2,128,128]{3,2,1,0:T(8,128)(2,1)}), bf16[32,2,128,128]{3,2,1,0:T(8,128)(2,1)S(1)}, u32[]{:S(2)}, u32[]{:S(2)}) async-start(bf16[32,2,128,128]{3,2,1,0:T(8,128)(2,1)} %get-tuple-element.67), calls=%async_computation.4 | async-start | bytes 4194304 | tf_op jit(solution)/shard_map/all_to_all | solution.py:505
  199.9 14.4 %collective-permute-start.11 = (bf16[2,2,128,128]{3,2,1,0:T(8,128)(2,1)S(1)}, bf16[2,2,128,128]{3,2,1,0:T(8,128)(2,1)S(1)}, u32[]{:S(2)}, u32[]{:S(2)}) collective-permute-start(bf16[2,2,128,128]{3,2,1,0:T(8,128)(2,1)S(1)} %get-tuple-element.60), channel_id=1, source_target_pairs={{0,112},{16,0},{32,16},{48,32},{64,48},{80,64},{96,80},{112,96},{1... | collective-permute-start | bytes 393224 | tf_op jit(solution)/shard_map/ppermute | solution.py:508
  200.4 16.8 %collective-permute-start.12 = (bf16[2,2,128,128]{3,2,1,0:T(8,128)(2,1)S(1)}, bf16[2,2,128,128]{3,2,1,0:T(8,128)(2,1)S(1)}, u32[]{:S(2)}, u32[]{:S(2)}) collective-permute-start(bf16[2,2,128,128]{3,2,1,0:T(8,128)(2,1)S(1)} %get-tuple-element.61), channel_id=1, source_target_pairs={{0,96},{16,112},{32,0},{48,16},{64,32},{80,48},{96,64},{112,80},{1... | collective-permute-start | bytes 393224 | tf_op jit(solution)/shard_map/ppermute | solution.py:508
  201.2 18.7 %collective-permute-start.13 = (bf16[2,2,128,128]{3,2,1,0:T(8,128)(2,1)S(1)}, bf16[2,2,128,128]{3,2,1,0:T(8,128)(2,1)S(1)}, u32[]{:S(2)}, u32[]{:S(2)}) collective-permute-start(bf16[2,2,128,128]{3,2,1,0:T(8,128)(2,1)S(1)} %get-tuple-element.62), channel_id=1, source_target_pairs={{0,80},{16,96},{32,112},{48,0},{64,16},{80,32},{96,48},{112,64},{1... | collective-permute-start | bytes 393224 | tf_op jit(solution)/shard_map/ppermute | solution.py:508
  201.6 25.3 %collective-permute-start.14 = (bf16[2,2,128,128]{3,2,1,0:T(8,128)(2,1)S(1)}, bf16[2,2,128,128]{3,2,1,0:T(8,128)(2,1)S(1)}, u32[]{:S(2)}, u32[]{:S(2)}) collective-permute-start(bf16[2,2,128,128]{3,2,1,0:T(8,128)(2,1)S(1)} %get-tuple-element.63), channel_id=1, source_target_pairs={{0,64},{16,80},{32,96},{48,112},{64,0},{80,16},{96,32},{112,48},{1... | collective-permute-start | bytes 393224 | tf_op jit(solution)/shard_map/ppermute | solution.py:508
  204.3 22.6 %collective-permute-start.15 = (bf16[2,2,128,128]{3,2,1,0:T(8,128)(2,1)S(1)}, bf16[2,2,128,128]{3,2,1,0:T(8,128)(2,1)S(1)}, u32[]{:S(2)}, u32[]{:S(2)}) collective-permute-start(bf16[2,2,128,128]{3,2,1,0:T(8,128)(2,1)S(1)} %get-tuple-element.64), channel_id=1, source_target_pairs={{0,48},{16,64},{32,80},{48,96},{64,112},{80,0},{96,16},{112,32},{1... | collective-permute-start | bytes 393224 | tf_op jit(solution)/shard_map/ppermute | solution.py:508
  214.3 12.5 %collective-permute-start.16 = (bf16[2,2,128,128]{3,2,1,0:T(8,128)(2,1)S(1)}, bf16[2,2,128,128]{3,2,1,0:T(8,128)(2,1)S(1)}, u32[]{:S(2)}, u32[]{:S(2)}) collective-permute-start(bf16[2,2,128,128]{3,2,1,0:T(8,128)(2,1)S(1)} %get-tuple-element.65), channel_id=1, source_target_pairs={{0,32},{16,48},{32,64},{48,80},{64,96},{80,112},{96,0},{112,16},{1... | collective-permute-start | bytes 393224 | tf_op jit(solution)/shard_map/ppermute | solution.py:508
  217.3 9.6 %collective-permute-start.17 = (bf16[2,2,128,128]{3,2,1,0:T(8,128)(2,1)S(1)}, bf16[2,2,128,128]{3,2,1,0:T(8,128)(2,1)S(1)}, u32[]{:S(2)}, u32[]{:S(2)}) collective-permute-start(bf16[2,2,128,128]{3,2,1,0:T(8,128)(2,1)S(1)} %get-tuple-element.66), channel_id=1, source_target_pairs={{0,16},{16,32},{32,48},{48,64},{64,80},{80,96},{96,112},{112,0},{1... | collective-permute-start | bytes 393224 | tf_op jit(solution)/shard_map/ppermute | solution.py:508
  265.8 30.5 %all-to-all-start.5 = ((bf16[16,2,128,128]{3,2,1,0:T(8,128)(2,1)}), bf16[16,2,128,128]{3,2,1,0:T(8,128)(2,1)S(1)}, u32[]{:S(2)}, u32[]{:S(2)}) async-start(bf16[16,2,128,128]{3,2,1,0:T(8,128)(2,1)} %copy-done.2), calls=%async_computation.5 | async-start | bytes 2097152 | tf_op jit(solution)/shard_map/all_to_all | solution.py:502
  (11 other events, 50.5 us)

commit v4 on v3

v4 whole, which is shorter than its diff:
```python
import functools

import jax
import jax.numpy as jnp
from jax import lax
from jax.experimental import pallas as pl
from jax.experimental.pallas import tpu as pltpu
from jax.sharding import PartitionSpec as P

HEAD_DIM = 128
BLOCK = 128
VMEM_LIMIT = 48 * 1024 * 1024
VMEM_ALL = 60 * 1024 * 1024
ANY = pl.BlockSpec(memory_space=pl.ANY)
VMEM = pl.BlockSpec(memory_space=pltpu.VMEM)
SMEM = pl.BlockSpec(memory_space=pltpu.SMEM)


def params(limit=VMEM_LIMIT):
    return pltpu.CompilerParams(vmem_limit_bytes=limit)


def cost(flops, nbytes):
    return pl.CostEstimate(flops=flops, bytes_accessed=nbytes, transcendentals=0)


def head_copies(heads, packed, arrays, sems, pack):
    copies = []
    for which, array in enumerate(arrays):
        for head in range(heads):
            flat = array.at[:, pl.ds(head * HEAD_DIM, HEAD_DIM)]
            block = packed.at[head, which]
            ends = (flat, block) if pack else (block, flat)
            copies.append(pltpu.make_async_copy(*ends, sems.at[which * heads + head]))
    return copies


def split_kernel(heads, count, *refs):
    copies = head_copies(heads, refs[count], refs[:count], refs[count + 1], True)
    start_all(copies)
    wait_all(copies)


def split_heads(*arrays):
    rows, features = arrays[0].shape
    heads, count = features // HEAD_DIM, len(arrays)
    return pl.pallas_call(
        functools.partial(split_kernel, heads, count),
        out_shape=jax.ShapeDtypeStruct((heads, count, rows, HEAD_DIM), arrays[0].dtype),
        in_specs=[ANY] * count,
        out_specs=ANY,
        scratch_shapes=[pltpu.SemaphoreType.DMA((count * heads,))],
        compiler_params=params(VMEM_ALL),
        cost_estimate=cost(0, 4 * arrays[0].size * count),
        name="split_heads",
    )(*arrays)


def join_kernel(heads, count, packed, *refs):
    copies = head_copies(heads, packed, refs[:count], refs[count], False)
    start_all(copies)
    wait_all(copies)


def join_heads(packed):
    heads, count, rows, depth = packed.shape
    shape = jax.ShapeDtypeStruct((rows, heads * depth), packed.dtype)
    return pl.pallas_call(
        functools.partial(join_kernel, heads, count),
        out_shape=(shape,) * count,
        in_specs=[ANY],
        out_specs=(ANY,) * count,
        scratch_shapes=[pltpu.SemaphoreType.DMA((count * heads,))],
        compiler_params=params(VMEM_ALL),
        cost_estimate=cost(0, 4 * packed.size),
        name="join_heads",
    )(packed)


def start_all(copies):
    for copy in copies:
        copy.start()


def wait_all(copies):
    for copy in copies:
        copy.wait()


def pick_kernel(slots, index_ref, in_ref, out_ref, sems):
    copies = [
        pltpu.make_async_copy(
            in_ref.at[index_ref[slot], pl.ds(0, 2)], out_ref.at[slot], sems.at[slot]
        )
        for slot in range(slots)
    ]
    start_all(copies)
    wait_all(copies)


def pick_blocks(index, blocks):
    slots = index.shape[0]
    return pl.pallas_call(
        functools.partial(pick_kernel, slots),
        out_shape=pltpu.HBM((slots, 2) + blocks.shape[2:], blocks.dtype),
        in_specs=[SMEM, VMEM],
        out_specs=ANY,
        scratch_shapes=[pltpu.SemaphoreType.DMA((slots,))],
        compiler_params=params(),
        cost_estimate=cost(0, 2 * slots * blocks[0].size),
        name="pick_blocks",
    )(index, blocks)


def pick_third_kernel(lanes, index_ref, in_ref, *refs):
    outs, sems = refs[:lanes], refs[lanes]

    def copy(at):
        step, half = divmod(at, 2)
        return pltpu.make_async_copy(
            in_ref.at[jnp.maximum(index_ref[at], 0), pl.ds(0, 2)], outs[step].at[half], sems.at[at]
        )

    for at in range(2 * lanes):

        @pl.when(index_ref[at] >= 0)
        def _():
            copy(at).start()

    for at in range(2 * lanes):

        @pl.when(index_ref[at] >= 0)
        def _():
            copy(at).wait()


def pick_third(index, blocks):
    lanes = index.shape[0] // 2
    shape = jax.ShapeDtypeStruct((2, 2) + blocks.shape[2:], blocks.dtype)
    return pl.pallas_call(
        functools.partial(pick_third_kernel, lanes),
        out_shape=(shape,) * lanes,
        in_specs=[SMEM, VMEM],
        out_specs=(ANY,) * lanes,
        scratch_shapes=[pltpu.SemaphoreType.DMA((2 * lanes,))],
        compiler_params=params(),
        cost_estimate=cost(0, 4 * blocks[0].size),
        name="pick_third",
    )(index, blocks)


def pick_cross_kernel(lanes, step_ref, *refs):
    ins, out_ref, sems = refs[:lanes], refs[lanes], refs[lanes + 1]
    for j in range(2):
        for step in range(lanes):

            @pl.when(step_ref[j] == step)
            def _():
                pltpu.make_async_copy(ins[step].at[1], out_ref.at[j], sems.at[j]).start()

    for j in range(2):

        @pl.when(step_ref[j] >= 0)
        def _():
            pltpu.make_async_copy(ins[0].at[1], out_ref.at[j], sems.at[j]).wait()


def pick_cross(steps, thirds):
    lanes = len(thirds)
    return pl.pallas_call(
        functools.partial(pick_cross_kernel, lanes),
        out_shape=jax.ShapeDtypeStruct(thirds[0].shape, thirds[0].dtype),
        in_specs=[SMEM] + [ANY] * lanes,
        out_specs=ANY,
        scratch_shapes=[pltpu.SemaphoreType.DMA((2,))],
        compiler_params=params(),
        cost_estimate=cost(0, 4 * thirds[0].size),
        name="pick_cross",
    )(steps, *thirds)


def pick_back_kernel(lanes, near_ref, cross_ref, own_in, cross_in, *refs):
    outs, sems = refs[:lanes], refs[lanes]
    plan = ((near_ref, own_in, 0), (cross_ref, cross_in, 1))
    for step_ref, ref, half in plan:
        for j in range(2):
            for step in range(lanes):

                @pl.when(step_ref[j] == step)
                def _():
                    pltpu.make_async_copy(
                        ref.at[j], outs[step].at[half], sems.at[2 * half + j]
                    ).start()

    for step_ref, ref, half in plan:
        for j in range(2):

            @pl.when(step_ref[j] >= 0)
            def _():
                pltpu.make_async_copy(ref.at[j], outs[0].at[half], sems.at[2 * half + j]).wait()


def pick_back(near_steps, cross_steps, own, crossed, lanes):
    shape = jax.ShapeDtypeStruct(own.shape, own.dtype)
    return pl.pallas_call(
        functools.partial(pick_back_kernel, lanes),
        out_shape=(shape,) * lanes,
        in_specs=[SMEM, SMEM, ANY, ANY],
        out_specs=(ANY,) * lanes,
        scratch_shapes=[pltpu.SemaphoreType.DMA((4,))],
        compiler_params=params(),
        cost_estimate=cost(0, 8 * own.size),
        name="pick_back",
    )(near_steps, cross_steps, own, crossed)


def dot(a, b, dims):
    return lax.dot_general(a, b, (dims, ((), ())), preferred_element_type=jnp.float32)


def attention(q, g, k, v):
    scale = HEAD_DIM ** (-0.5)
    s = dot(k, q, ((1,), (1,))) * scale
    dp = dot(v, g, ((1,), (1,)))
    w = jnp.exp(s - jnp.max(s, axis=0, keepdims=True))
    p = w * (1.0 / jnp.sum(w, axis=0, keepdims=True))
    p_low = p.astype(jnp.bfloat16)
    delta = jnp.sum(p_low.astype(jnp.float32) * dp, axis=0, keepdims=True)
    return p_low, (p * (dp - delta) * scale).astype(jnp.bfloat16)


def load_thirds(near_ref, cross_ref, thirds, extra, sems):
    for j in range(2):
        for step in range(1, len(thirds)):

            @pl.when(near_ref[j] == step)
            def _():
                pltpu.make_async_copy(thirds[step].at[0], extra.at[j], sems.at[j]).start()

        @pl.when(near_ref[j] < 0)
        def _():
            pltpu.make_async_copy(cross_ref.at[j], extra.at[j], sems.at[j]).start()

    for j in range(2):
        pltpu.make_async_copy(cross_ref.at[j], extra.at[j], sems.at[j]).wait()


def far_block(r, which, slot_ref, third_ref, main_ref, extra):
    slot = slot_ref[r]
    j = (third_ref[1] == r).astype(jnp.int32)
    return jnp.where(slot >= 0, main_ref[jnp.maximum(slot, 0), which], extra[j, which])


def attend_thirds_kernel(lanes, slot_ref, third_ref, near_ref, x_ref, edge_ref, main_ref, cross_ref, *refs):
    thirds, out_ref = refs[:lanes], refs[lanes]
    extra, sems = refs[lanes + 1 :]
    load_thirds(near_ref, cross_ref, thirds, extra, sems)
    for j in range(2):
        r = third_ref[j]
        n = r // 2
        listed = []
        for which in range(2):
            edge = edge_ref[which]
            before = jnp.where(n == 0, edge, x_ref[jnp.maximum(n - 1, 0), which])
            other = far_block(n * 4 + 1 - r, which, slot_ref, third_ref, main_ref, extra)
            listed.append(jnp.concatenate([extra[j, which], x_ref[n, which], before, other], axis=0))
        q, g = x_ref[n, 2], x_ref[n, 3]
        p_low, ds = attention(q, g, *listed)
        out_ref[j, 0] = dot(ds[:BLOCK], q, ((1,), (0,))).astype(out_ref.dtype)
        out_ref[j, 1] = dot(p_low[:BLOCK], g, ((1,), (0,))).astype(out_ref.dtype)


def attend_thirds(slot, third, near, x, edge, main, cross, thirds):
    lanes = len(thirds)
    return pl.pallas_call(
        functools.partial(attend_thirds_kernel, lanes),
        out_shape=jax.ShapeDtypeStruct(cross.shape, cross.dtype),
        in_specs=[SMEM, SMEM, SMEM, VMEM, VMEM, VMEM] + [ANY] * (1 + lanes),
        out_specs=VMEM,
        scratch_shapes=[pltpu.VMEM(cross.shape, cross.dtype), pltpu.SemaphoreType.DMA((2,))],
        compiler_params=params(),
        cost_estimate=cost(5 * 2 * 2 * 4 * BLOCK * BLOCK * HEAD_DIM, 8 * cross.size),
        name="attend_thirds",
    )(slot, third, near, x, edge, main, cross, *thirds)


def attend_kernel(
    blocks, lanes, slot_ref, third_ref, near_ref, x_ref, edge_ref, main_ref, cross_ref, *refs
):
    thirds = refs[:lanes]
    final, main_out, edge_out, sums = refs[lanes : lanes + 4]
    extra, far_out, out_ref, sum_ref, edge_low = refs[lanes + 4 : lanes + 9]
    sems, far_sems, out_sems, sum_sems, edge_sem = refs[lanes + 9 :]
    bf16 = jnp.bfloat16

    def leave(r, slot):
        return pltpu.make_async_copy(far_out.at[r], main_out.at[slot], far_sems.at[r])

    def finished(n):
        return pltpu.make_async_copy(out_ref.at[n], final.at[n, pl.ds(0, 2)], out_sems.at[n])

    def summed(n):
        return pltpu.make_async_copy(sum_ref.at[n], sums.at[n], sum_sems.at[n])

    edge_done = pltpu.make_async_copy(edge_low, edge_out, edge_sem)
    load_thirds(near_ref, cross_ref, thirds, extra, sems)

    def one(n, first):
        q, g = x_ref[n, 2], x_ref[n, 3]
        r2, r3 = 2 * n, 2 * n + 1
        listed = []
        for which in range(2):
            before = edge_ref[which] if first else x_ref[n - 1, which]
            far = [far_block(r, which, slot_ref, third_ref, main_ref, extra) for r in (r2, r3)]
            listed.append(jnp.concatenate([x_ref[n, which], before] + far, axis=0))
        k, v = listed
        p_low, ds = attention(q, g, k, v)
        out_ref[n, 0] = dot(p_low, v, ((0,), (0,))).astype(bf16)
        out_ref[n, 1] = dot(ds, k, ((0,), (0,))).astype(bf16)
        dk = dot(ds, q, ((1,), (0,)))
        dv = dot(p_low, g, ((1,), (0,)))
        for which, d in enumerate((dk, dv)):
            sum_ref[n, which] = d[:BLOCK]
            if first:
                edge_low[which] = d[BLOCK : 2 * BLOCK].astype(bf16)
            else:
                sum_ref[n - 1, which] += d[BLOCK : 2 * BLOCK]
            far_out[r2, which] = d[2 * BLOCK : 3 * BLOCK].astype(bf16)
            far_out[r3, which] = d[3 * BLOCK :].astype(bf16)
        finished(n).start()
        if first:
            edge_done.start()
        else:
            summed(n - 1).start()
        for r in (r2, r3):

            @pl.when(slot_ref[r] >= 0)
            def _():
                leave(r, slot_ref[r]).start()

    one(0, True)
    lax.fori_loop(1, blocks, lambda n, _: one(n, False), None, unroll=3)
    summed(blocks - 1).start()

    def finish(r, _):
        @pl.when(slot_ref[r] >= 0)
        def _():
            leave(r, 0).wait()

    lax.fori_loop(0, 2 * blocks, finish, None)
    lax.fori_loop(0, blocks, lambda n, _: finished(n).wait(), None)
    lax.fori_loop(0, blocks, lambda n, _: summed(n).wait(), None)
    edge_done.wait()


def attend(slot, third, near, x, edge, main, cross, thirds):
    blocks = x.shape[0]
    lanes = len(thirds)
    bf16 = jnp.bfloat16
    pair = (2,) + x.shape[2:]
    return pl.pallas_call(
        functools.partial(attend_kernel, blocks, lanes),
        out_shape=(
            pltpu.HBM(x.shape, bf16),
            pltpu.HBM(main.shape, bf16),
            pltpu.HBM(edge.shape, bf16),
            pltpu.HBM((blocks,) + pair, jnp.float32),
        ),
        in_specs=[SMEM, SMEM, SMEM, VMEM, VMEM, VMEM] + [ANY] * (1 + lanes),
        out_specs=(ANY, ANY, ANY, ANY),
        scratch_shapes=[
            pltpu.VMEM(cross.shape, bf16),
            pltpu.VMEM((2 * blocks,) + pair, bf16),
            pltpu.VMEM((blocks,) + pair, bf16),
            pltpu.VMEM((blocks,) + pair, jnp.float32),
            pltpu.VMEM(edge.shape, bf16),
            pltpu.SemaphoreType.DMA((2,)),
            pltpu.SemaphoreType.DMA((2 * blocks,)),
            pltpu.SemaphoreType.DMA((blocks,)),
            pltpu.SemaphoreType.DMA((blocks,)),
            pltpu.SemaphoreType.DMA,
        ],
        compiler_params=params(),
        cost_estimate=cost(
            5 * 2 * blocks * 4 * BLOCK * BLOCK * HEAD_DIM, 2 * (3 * x.size + 2 * main.size)
        ),
        name="attend",
    )(slot, third, near, x, edge, main, cross, *thirds)


def land_thirds_kernel(blocks, lanes, third_ref, sum_ref, back_ref, *refs):
    thirds, total = refs[:lanes], refs[lanes]
    late, sems = refs[lanes + 1 :]
    f32 = jnp.float32

    def arrive(at):
        step, half = divmod(at, 2)
        return pltpu.make_async_copy(thirds[step].at[half], late.at[at], sems.at[at])

    for at in range(1, 2 * lanes):

        @pl.when(third_ref[at] >= 0)
        def _():
            arrive(at).start()

    total[...] = sum_ref[...]
    total[blocks - 1] += back_ref[...].astype(f32)
    for at in range(1, 2 * lanes):

        @pl.when(third_ref[at] >= 0)
        def _():
            arrive(at).wait()
            total[third_ref[at]] += late[at].astype(f32)


def land_thirds(third_index, sums, back, thirds):
    blocks = sums.shape[0]
    lanes = len(thirds)
    return pl.pallas_call(
        functools.partial(land_thirds_kernel, blocks, lanes),
        out_shape=jax.ShapeDtypeStruct(sums.shape, jnp.float32),
        in_specs=[SMEM, VMEM, VMEM] + [ANY] * lanes,
        out_specs=VMEM,
        scratch_shapes=[
            pltpu.VMEM((2 * lanes,) + back.shape, back.dtype),
            pltpu.SemaphoreType.DMA((2 * lanes,)),
        ],
        compiler_params=params(),
        cost_estimate=cost(sums.size * 2, 8 * sums.size),
        name="land_thirds",
    )(third_index, sums, back, *thirds)


def land_kernel(
    slots, blocks, rank_ref, index_ref, sums, home, _, out, total, late, low, sum_sems, home_sems, out_sems
):
    def read(n):
        return pltpu.make_async_copy(sums.at[n], total.at[n], sum_sems.at[n])

    def arrive(slot):
        return pltpu.make_async_copy(home.at[slot], late.at[slot], home_sems.at[slot])

    def write(n):
        return pltpu.make_async_copy(low.at[n], out.at[n, pl.ds(2, 2)], out_sems.at[n])

    start_all([read(n) for n in range(blocks)])
    start_all([arrive(slot) for slot in range(slots)])
    wait_all([read(n) for n in range(blocks)])

    def one(slot, _):
        arrive(slot).wait()

        @pl.when(slot // 2 != rank_ref[0])
        def _():
            total[index_ref[slot]] += late[slot].astype(jnp.float32)

    lax.fori_loop(0, slots, one, None)

    def put(n, _):
        low[n] = total[n].astype(low.dtype)
        write(n).start()

    lax.fori_loop(0, blocks, put, None)
    wait_all([write(n) for n in range(blocks)])


def land(rank, index, sums, home, final):
    slots = index.shape[0]
    blocks = sums.shape[0]
    bf16 = jnp.bfloat16
    return pl.pallas_call(
        functools.partial(land_kernel, slots, blocks),
        out_shape=pltpu.HBM(final.shape, bf16),
        in_specs=[SMEM, SMEM, ANY, ANY, ANY],
        out_specs=ANY,
        scratch_shapes=[
            pltpu.VMEM(sums.shape, jnp.float32),
            pltpu.VMEM(home.shape, bf16),
            pltpu.VMEM(sums.shape, bf16),
            pltpu.SemaphoreType.DMA((blocks,)),
            pltpu.SemaphoreType.DMA((slots,)),
            pltpu.SemaphoreType.DMA((blocks,)),
        ],
        input_output_aliases={4: 0},
        compiler_params=params(VMEM_ALL),
        cost_estimate=cost(sums.size * 2, 6 * sums.size + 2 * home.size),
        name="land",
    )(rank, index, sums, home, final)


def plan(key_lists, blocks, ctx_count, lanes):
    i32 = jnp.int32
    me = lax.axis_index("ctx")
    half, lane = me // lanes, me % lanes
    requests = 2 * blocks
    far_all = key_lists[:, 2:].reshape(ctx_count, requests)
    source, inside = far_all // blocks, far_all % blocks
    earlier = (jnp.arange(requests)[None, :] < jnp.arange(requests)[:, None])[None]
    rank = jnp.sum(((source[:, None, :] == source[:, :, None]) & earlier).astype(i32), axis=2)
    is_third = rank == 2
    order = jnp.sum((is_third[:, None, :] & earlier).astype(i32), axis=2)

    pair = jnp.arange(2, dtype=i32)[None, :, None]
    wanted = (source[:, None, :] == me) & (rank[:, None, :] == pair)
    send_main = jnp.sum(jnp.where(wanted, inside[:, None, :], 0), axis=2).reshape(-1)

    from_me = is_third & (source == me)
    third_of = jnp.sum(jnp.where(from_me, inside + 1, 0), axis=1) - 1
    step = jnp.arange(lanes, dtype=i32)[:, None]
    side = jnp.arange(2, dtype=i32)[None, :]
    asker = jnp.where(side == 0, half, 1 - half) * lanes + (lane + step) % lanes
    hit = asker[:, :, None] == jnp.arange(ctx_count, dtype=i32)[None, None, :]
    third_index = jnp.sum(jnp.where(hit, third_of[None, None, :], 0), axis=2).reshape(-1)

    def row(of, array):
        at = jnp.arange(ctx_count, dtype=i32)[:, None] == of
        return jnp.sum(jnp.where(at, array, 0), axis=0)

    slot_of = jnp.where(is_third, -1, source * 2 + rank)
    my_slot = row(me, slot_of)
    is_jth = (is_third[:, None, :] & (order[:, None, :] == pair)).astype(i32)
    third_source = jnp.sum(is_jth * source[:, None, :], axis=2)
    third_request = jnp.sum(is_jth * jnp.arange(requests, dtype=i32), axis=2)

    def steps(of):
        slab = row(of, third_source)
        return jnp.where(slab // lanes == half, (lane - slab % lanes + lanes) % lanes, -1)

    partner = (me + lanes) % ctx_count
    return (
        send_main,
        third_index,
        my_slot,
        row(me, third_request),
        steps(me),
        steps(partner),
    )


def body(queries, keys, values, out_grad, key_lists):
    ctx_count = lax.axis_size("ctx")
    blocks = lax.axis_size("head")
    lanes = ctx_count // 2
    send_main, third_index, my_slot, my_third, near_steps, cross_steps = plan(
        key_lists, blocks, ctx_count, lanes
    )

    def head_exchange(array):
        return lax.all_to_all(array, "head", split_axis=0, concat_axis=0, tiled=True)

    def ctx_exchange(array):
        return lax.all_to_all(array, "ctx", split_axis=0, concat_axis=0, tiled=True)

    def move(array, target):
        return lax.ppermute(array, "ctx", [(i, target(i)) for i in range(ctx_count)])

    def across(array):
        return move(array, lambda i: (i + lanes) % ctx_count)

    def along(arrays, sign):
        def target(step):
            return lambda i: i // lanes * lanes + (i + sign * step) % lanes

        return [arrays[0]] + [move(arrays[s], target(s)) for s in range(1, lanes)]

    x = head_exchange(split_heads(keys, values, queries, out_grad))
    third_blocks = pick_third(third_index, x)
    send_main, third_blocks = lax.optimization_barrier((send_main, third_blocks))
    thirds = along(third_blocks, 1)
    edge = move(x[blocks - 1, :2], lambda i: (i + 1) % ctx_count)
    main = ctx_exchange(pick_blocks(send_main, x))
    cross = across(pick_cross(cross_steps, thirds))
    listed = (my_slot, my_third, near_steps, x, edge, main, cross)
    third_grad = attend_thirds(*listed, thirds)
    cross_grad = across(third_grad)
    my_slot, third_grad = lax.optimization_barrier((my_slot, third_grad))
    final, main_grad, edge_grad, sums = attend(my_slot, *listed[1:], thirds)
    main_grad, edge_grad, cross_grad = lax.optimization_barrier((main_grad, edge_grad, cross_grad))
    home = ctx_exchange(main_grad)
    back = move(edge_grad, lambda i: (i - 1) % ctx_count)
    late = along(pick_back(near_steps, cross_steps, third_grad, cross_grad, lanes), -1)
    sums = land_thirds(third_index, sums, back, late)
    rank = lax.axis_index("ctx").reshape(1)
    final = head_exchange(land(rank, send_main, sums, home, final))
    return join_heads(final)


def solution(mesh):
    tokens = P(("ctx", "head"), None)
    return jax.shard_map(
        body,
        mesh=mesh,
        in_specs=(tokens, tokens, tokens, tokens, P()),
        out_specs=(tokens, tokens, tokens, tokens),
        check_vma=False,
    )
```

time: 299 us -> 411 us (1.37)
  Pallas kernels: 38 us -> 159 us
  waiting for transfers between devices: 183 us -> 112 us
  blocking collectives: 0 us -> 52.2 us
  starting transfers between devices: 63.6 us -> 79 us
  local copies, waits for them, and re-layouts: 9.59 us -> 2.78 us
    pallas_call x6 -> x5, Pallas kernels: 16.1 us -> 141 us  [the longest x1 65.2 us: split_heads(): pl.pallas_call(functools.partial(split_kernel, heads, count), out_shape=j...]
    all_to_all x2, waiting for transfers between devices: 74.5 us -> 2.54 us  [ctx_exchange(): return lax.all_to_all(array, 'ctx', split_axis=0, concat_axis=0, tiled=True)]
    all_to_all x0 -> x1, blocking collectives: none -> 52.2 us  [head_exchange(): lax.all_to_all(array, 'head', split_axis=0, concat_axis=0, tiled=True)]
    ppermute x18, starting transfers between devices: 21.3 us -> 50.1 us  [move(): lax.ppermute(array, 'ctx', [(i, target(i)) for i in range(ctx_count)])]
    all_to_all x4 -> x1, starting transfers between devices: 27.8 us -> 8.49 us  [head_exchange(): lax.all_to_all(array, 'head', split_axis=0, concat_axis=0, tiled=True)]
    ppermute x18, waiting for transfers between devices: 47.5 us -> 65 us  [move(): lax.ppermute(array, 'ctx', [(i, target(i)) for i in range(ctx_count)])]
    all_to_all x4 -> x1, waiting for transfers between devices: 61.4 us -> 44.6 us  [head_exchange(): lax.all_to_all(array, 'head', split_axis=0, concat_axis=0, tiled=True)]
    unnamed x23 -> x19, local copies, waits for them, and re-layouts: 8.31 us -> 2.12 us
  transfers between devices with their start and end apart: 24 -> 21, of which waited for: 16 -> 10; matrix products, arithmetic and copies ran while one was open for 1% -> 1% of each run, Pallas kernels for 3% -> 4%
where the time goes in v4:
time: 411 us; the launch traced here: 409 us
  Pallas kernels  159 us (39%)
  waiting for transfers between devices  112 us (27%)
  starting transfers between devices  79 us (19%)
  blocking collectives  52.2 us (13%)
    pallas_call x1, Pallas kernels, split_heads(): pl.pallas_call(functools.partial(split_kernel, heads, count), out_shape=j...  65.2 us
    pallas_call x1, Pallas kernels, join_heads(): pl.pallas_call(functools.partial(join_kernel, heads, count), out_shape=(s...  65.2 us
    ppermute x18, waiting for transfers between devices, move(): lax.ppermute(array, 'ctx', [(i, target(i)) for i in range(ctx_count)])  65 us
    all_to_all x1, blocking collectives, head_exchange(): lax.all_to_all(array, 'head', split_axis=0, concat_axis=0, tiled=True)  52.2 us
    ppermute x18, starting transfers between devices, move(): lax.ppermute(array, 'ctx', [(i, target(i)) for i in range(ctx_count)])  50.1 us
    all_to_all x1, waiting for transfers between devices, head_exchange(): lax.all_to_all(array, 'head', split_axis=0, concat_axis=0, tiled=True)  44.6 us
    all_to_all x2, starting transfers between devices, ctx_exchange(): return lax.all_to_all(array, 'ctx', split_axis=0, concat_axis=0, tiled=True)  20.5 us
    pallas_call x1, Pallas kernels, attend(): pl.pallas_call(functools.partial(attend_kernel, blocks, lanes), out_shape...  13.4 us
  transfers between devices with their start and end apart: 21, of which 10 were waited for; matrix products, arithmetic and copies ran while one was open for 1% of the time, Pallas kernels for 4%

profile of v4, /device:TPU:56, one launch (start us, length us, event | category | flops | bytes accessed | tf_op | source)
XLA Modules:
  0.0 409.0 jit_solution(9039363379969296099)
XLA Ops:
  0.6 65.2 %split_heads.1 = bf16[16,4,128,128]{3,2,1,0:T(8,128)(2,1)} custom-call(bf16[128,2048]{1,0:T(8,128)(2,1)} %refs_0_.1, bf16[128,2048]{1,0:T(8,128)(2,1)} %refs_1_.1, bf16[128,2048]{1,0:T(8,128)(2,1)} %refs_2_.1, bf16[128,2048]{1,0:T(8,128)(2,1)} %refs_3_.1), custom_call_target="tpu_custom_call" | custom-call | bytes 4194304 | tf_op jit(solution)/shard_map/split_heads/pallas_call | solution.py:47
  65.9 8.5 %all-to-all-start = ((bf16[16,4,128,128]{3,2,1,0:T(8,128)(2,1)}), bf16[16,4,128,128]{3,2,1,0:T(8,128)(2,1)S(1)}, u32[]{:S(2)}, u32[]{:S(2)}) async-start(bf16[16,4,128,128]{3,2,1,0:T(8,128)(2,1)} %split_heads.1), calls=%async_computation | async-start | bytes 4194304 | tf_op jit(solution)/shard_map/all_to_all | solution.py:549
  77.0 44.6 %all-to-all-done.in_ref.x_ref = bf16[16,4,128,128]{3,2,1,0:T(8,128)(2,1)S(1)} async-done(((bf16[16,4,128,128]{3,2,1,0:T(8,128)(2,1)}), bf16[16,4,128,128]{3,2,1,0:T(8,128)(2,1)S(1)}, u32[]{:S(2)}, u32[]{:S(2)}) %all-to-all-start) | async-done | bytes 2097184 | tf_op jit(solution)/shard_map/all_to_all | solution.py:549
  123.1 2.2 pick_blocks.1
  125.3 8.1 %all-to-all-start.1 = ((bf16[32,2,128,128]{3,2,1,0:T(8,128)(2,1)}), bf16[32,2,128,128]{3,2,1,0:T(8,128)(2,1)}, u32[]{:S(2)}, u32[]{:S(2)}) async-start(bf16[32,2,128,128]{3,2,1,0:T(8,128)(2,1)} %pick_blocks.1), calls=%async_computation.1 | async-start | bytes 4194304 | tf_op jit(solution)/shard_map/all_to_all | solution.py:552
  134.1 2.5 collective-permute-start.3
  137.4 2.2 collective-permute-start.5
  139.7 9.6 %collective-permute-done.1.refs_1_ = bf16[2,2,128,128]{3,2,1,0:T(8,128)(2,1)S(1)} collective-permute-done((bf16[2,2,128,128]{3,2,1,0:T(8,128)(2,1)S(1)}, bf16[2,2,128,128]{3,2,1,0:T(8,128)(2,1)S(1)}, u32[]{:S(2)}, u32[]{:S(2)}) %collective-permute-start.1) | collective-permute-done | bytes 131104 | tf_op jit(solution)/shard_map/ppermute | solution.py:555
  152.4 3.6 collective-permute-done.6.refs_6_
  157.6 5.6 %collective-permute-start.8 = (bf16[2,2,128,128]{3,2,1,0:T(8,128)(2,1)S(1)}, bf16[2,2,128,128]{3,2,1,0:T(8,128)(2,1)S(1)}, u32[]{:S(2)}, u32[]{:S(2)}) collective-permute-start(bf16[2,2,128,128]{3,2,1,0:T(8,128)(2,1)S(1)} %pick_cross.1), channel_id=1, source_target_pairs={{0,128},{16,144},{32,160},{48,176},{64,192},{80,208},{96,224},{112... | collective-permute-start | bytes 393224 | tf_op jit(solution)/shard_map/ppermute | solution.py:555
  164.9 2.1 collective-permute-done.edge_ref
  166.9 20.9 %collective-permute-done.8.cross_ref = bf16[2,2,128,128]{3,2,1,0:T(8,128)(2,1)S(1)} collective-permute-done((bf16[2,2,128,128]{3,2,1,0:T(8,128)(2,1)S(1)}, bf16[2,2,128,128]{3,2,1,0:T(8,128)(2,1)S(1)}, u32[]{:S(2)}, u32[]{:S(2)}) %collective-permute-start.8) | collective-permute-done | bytes 131104 | tf_op jit(solution)/shard_map/ppermute | solution.py:555
  187.9 2.5 all-to-all-done.1.main_ref
  190.4 2.9 attend_thirds.1.own_in
  193.4 13.4 %attend.1 = (bf16[16,4,128,128]{3,2,1,0:T(8,128)(2,1)}, bf16[32,2,128,128]{3,2,1,0:T(8,128)(2,1)}, bf16[2,128,128]{2,1,0:T(8,128)(2,1)}, f32[16,2,128,128]{3,2,1,0:T(8,128)}) custom-call(s32[32]{0:T(128)S(1)} %select_reduce_fusion.3.slot_ref, s32[2]{0:T(128)S(1)} %get-tuple-element.76.third_ref, s32[2]{0:T(128)S(1)} %compare_select_fusion.7.near_ref, ...), custom_call_target="tpu_custom_call" | custom-call | flops 1342177280 | bytes 10485760 | tf_op jit(solution)/shard_map/attend/pallas_call | solution.py:361
  207.5 12.4 %all-to-all-start.2 = ((bf16[32,2,128,128]{3,2,1,0:T(8,128)(2,1)}), bf16[32,2,128,128]{3,2,1,0:T(8,128)(2,1)}, u32[]{:S(2)}, u32[]{:S(2)}) async-start(bf16[32,2,128,128]{3,2,1,0:T(8,128)(2,1)} %get-tuple-element.70), calls=%async_computation.2 | async-start | bytes 4194304 | tf_op jit(solution)/shard_map/all_to_all | solution.py:552
  222.5 3.2 collective-permute-start.13
  226.0 19.1 %collective-permute-done.10.back_ref = bf16[2,128,128]{2,1,0:T(8,128)(2,1)S(1)} collective-permute-done((bf16[2,128,128]{2,1,0:T(8,128)(2,1)S(1)}, bf16[2,128,128]{2,1,0:T(8,128)(2,1)S(1)}, u32[]{:S(2)}, u32[]{:S(2)}) %collective-permute-start.10) | collective-permute-done | bytes 65568 | tf_op jit(solution)/shard_map/ppermute | solution.py:555
  245.1 22.7 %collective-permute-start.16 = (bf16[2,2,128,128]{3,2,1,0:T(8,128)(2,1)S(1)}, bf16[2,2,128,128]{3,2,1,0:T(8,128)(2,1)S(1)}, u32[]{:S(2)}, u32[]{:S(2)}) collective-permute-start(bf16[2,2,128,128]{3,2,1,0:T(8,128)(2,1)S(1)} %get-tuple-element.68), channel_id=1, source_target_pairs={{0,32},{16,48},{32,64},{48,80},{64,96},{80,112},{96,0},{112,16},{1... | collective-permute-start | bytes 393224 | tf_op jit(solution)/shard_map/ppermute | solution.py:555
  267.8 7.4 %collective-permute-start.17 = (bf16[2,2,128,128]{3,2,1,0:T(8,128)(2,1)S(1)}, bf16[2,2,128,128]{3,2,1,0:T(8,128)(2,1)S(1)}, u32[]{:S(2)}, u32[]{:S(2)}) collective-permute-start(bf16[2,2,128,128]{3,2,1,0:T(8,128)(2,1)S(1)} %get-tuple-element.69), channel_id=1, source_target_pairs={{0,16},{16,32},{32,48},{48,64},{64,80},{80,96},{96,112},{112,0},{1... | collective-permute-start | bytes 393224 | tf_op jit(solution)/shard_map/ppermute | solution.py:555
  275.2 8.2 %collective-permute-done.16.refs_6_ = bf16[2,2,128,128]{3,2,1,0:T(8,128)(2,1)S(1)} collective-permute-done((bf16[2,2,128,128]{3,2,1,0:T(8,128)(2,1)S(1)}, bf16[2,2,128,128]{3,2,1,0:T(8,128)(2,1)S(1)}, u32[]{:S(2)}, u32[]{:S(2)}) %collective-permute-start.16) | collective-permute-done | bytes 131104 | tf_op jit(solution)/shard_map/ppermute | solution.py:555
  286.1 5.3 %land.1 = bf16[16,4,128,128]{3,2,1,0:T(8,128)(2,1)} custom-call(s32[1]{0:T(128)} %bitcast.rank_ref, s32[32]{0:T(128)} %copy-done.4, f32[16,2,128,128]{3,2,1,0:T(8,128)} %copy-done, bf16[32,2,128,128]{3,2,1,0:T(8,128)(2,1)} %all-to-all-done.2.home, bf16[16,4,128,128]{3,2,1,0:T(8,128)(2,1)} %get-tuple-element.71._), custom_call_target="tpu_custom_call", output_to_operand_aliasing={{}: (4, {})} | custom-call | flops 1048576 | bytes 5242880 | tf_op jit(solution)/shard_map/land/pallas_call | solution.py:471
  291.4 52.2 %all_to_all.20.packed = bf16[16,4,128,128]{3,2,1,0:T(8,128)(2,1)} all-to-all(bf16[16,4,128,128]{3,2,1,0:T(8,128)(2,1)} %land.1), channel_id=1, replica_groups=mesh['ctx'=16,'head'=16] {'head'}, dimensions={0} | all-to-all | bytes 4194304 | tf_op jit(solution)/shard_map/all_to_all | solution.py:549
  343.6 65.2 %join_heads.1 = (bf16[128,2048]{1,0:T(8,128)(2,1)}, bf16[128,2048]{1,0:T(8,128)(2,1)}, bf16[128,2048]{1,0:T(8,128)(2,1)}, bf16[128,2048]{1,0:T(8,128)(2,1)}) custom-call(bf16[16,4,128,128]{3,2,1,0:T(8,128)(2,1)} %all_to_all.20.packed), custom_call_target="tpu_custom_call" | custom-call | bytes 4194304 | tf_op jit(solution)/shard_map/join_heads/pallas_call | solution.py:68
  (77 shorter events, 18.2 us)
Async XLA Ops:
  65.9 55.8 %all-to-all-start = ((bf16[16,4,128,128]{3,2,1,0:T(8,128)(2,1)}), bf16[16,4,128,128]{3,2,1,0:T(8,128)(2,1)S(1)}, u32[]{:S(2)}, u32[]{:S(2)}) async-start(bf16[16,4,128,128]{3,2,1,0:T(8,128)(2,1)} %split_heads.1), calls=%async_computation | async-start | bytes 4194304 | tf_op jit(solution)/shard_map/all_to_all | solution.py:549
  77.0 48.3 %copy-start.4 = (s32[32]{0:T(128)}, s32[32]{0:T(128)S(1)}, u32[]{:S(2)}) copy-start(s32[32]{0:T(128)S(1)} %reshape.202.index_ref) | copy-start | bytes 388
  125.3 65.1 %all-to-all-start.1 = ((bf16[32,2,128,128]{3,2,1,0:T(8,128)(2,1)}), bf16[32,2,128,128]{3,2,1,0:T(8,128)(2,1)}, u32[]{:S(2)}, u32[]{:S(2)}) async-start(bf16[32,2,128,128]{3,2,1,0:T(8,128)(2,1)} %pick_blocks.1), calls=%async_computation.1 | async-start | bytes 4194304 | tf_op jit(solution)/shard_map/all_to_all | solution.py:552
  133.5 15.8 %collective-permute-start.1 = (bf16[2,2,128,128]{3,2,1,0:T(8,128)(2,1)S(1)}, bf16[2,2,128,128]{3,2,1,0:T(8,128)(2,1)S(1)}, u32[]{:S(2)}, u32[]{:S(2)}) collective-permute-start(bf16[2,2,128,128]{3,2,1,0:T(8,128)(2,1)S(1)} %get-tuple-element.48), channel_id=1, source_target_pairs={{0,16},{16,32},{32,48},{48,64},{64,80},{80,96},{96,112},{112,0},{1... | collective-permute-start | bytes 393224 | tf_op jit(solution)/shard_map/ppermute | solution.py:555
  133.7 16.6 %collective-permute-start.2 = (bf16[2,2,128,128]{3,2,1,0:T(8,128)(2,1)S(1)}, bf16[2,2,128,128]{3,2,1,0:T(8,128)(2,1)S(1)}, u32[]{:S(2)}, u32[]{:S(2)}) collective-permute-start(bf16[2,2,128,128]{3,2,1,0:T(8,128)(2,1)S(1)} %get-tuple-element.49), channel_id=1, source_target_pairs={{0,32},{16,48},{32,64},{48,80},{64,96},{80,112},{96,0},{112,16},{1... | collective-permute-start | bytes 393224 | tf_op jit(solution)/shard_map/ppermute | solution.py:555
  134.1 18.3 %collective-permute-start.3 = (bf16[2,2,128,128]{3,2,1,0:T(8,128)(2,1)}, bf16[2,2,128,128]{3,2,1,0:T(8,128)(2,1)S(1)}, u32[]{:S(2)}, u32[]{:S(2)}) collective-permute-start(bf16[2,2,128,128]{3,2,1,0:T(8,128)(2,1)} %get-tuple-element.50), channel_id=1, source_target_pairs={{0,48},{16,64},{32,80},{48,96},{64,112},{80,0},{96,16},{112,32},{1... | collective-permute-start | bytes 393224 | tf_op jit(solution)/shard_map/ppermute | solution.py:555
  136.6 15.8 %collective-permute-start.4 = (bf16[2,2,128,128]{3,2,1,0:T(8,128)(2,1)}, bf16[2,2,128,128]{3,2,1,0:T(8,128)(2,1)S(1)}, u32[]{:S(2)}, u32[]{:S(2)}) collective-permute-start(bf16[2,2,128,128]{3,2,1,0:T(8,128)(2,1)} %get-tuple-element.51), channel_id=1, source_target_pairs={{0,64},{16,80},{32,96},{48,112},{64,0},{80,16},{96,32},{112,48},{1... | collective-permute-start | bytes 393224 | tf_op jit(solution)/shard_map/ppermute | solution.py:555
  137.4 14.9 %collective-permute-start.5 = (bf16[2,2,128,128]{3,2,1,0:T(8,128)(2,1)}, bf16[2,2,128,128]{3,2,1,0:T(8,128)(2,1)S(1)}, u32[]{:S(2)}, u32[]{:S(2)}) collective-permute-start(bf16[2,2,128,128]{3,2,1,0:T(8,128)(2,1)} %get-tuple-element.52), channel_id=1, source_target_pairs={{0,80},{16,96},{32,112},{48,0},{64,16},{80,32},{96,48},{112,64},{1... | collective-permute-start | bytes 393224 | tf_op jit(solution)/shard_map/ppermute | solution.py:555
  149.3 6.7 %collective-permute-start.6 = (bf16[2,2,128,128]{3,2,1,0:T(8,128)(2,1)S(1)}, bf16[2,2,128,128]{3,2,1,0:T(8,128)(2,1)S(1)}, u32[]{:S(2)}, u32[]{:S(2)}) collective-permute-start(bf16[2,2,128,128]{3,2,1,0:T(8,128)(2,1)S(1)} %get-tuple-element.53), channel_id=1, source_target_pairs={{0,96},{16,112},{32,0},{48,16},{64,32},{80,48},{96,64},{112,80},{1... | collective-permute-start | bytes 393224 | tf_op jit(solution)/shard_map/ppermute | solution.py:555
  150.3 6.6 %collective-permute-start.7 = (bf16[2,2,128,128]{3,2,1,0:T(8,128)(2,1)S(1)}, bf16[2,2,128,128]{3,2,1,0:T(8,128)(2,1)S(1)}, u32[]{:S(2)}, u32[]{:S(2)}) collective-permute-start(bf16[2,2,128,128]{3,2,1,0:T(8,128)(2,1)S(1)} %get-tuple-element.54), channel_id=1, source_target_pairs={{0,112},{16,0},{32,16},{48,32},{64,48},{80,64},{96,80},{112,96},{1... | collective-permute-start | bytes 393224 | tf_op jit(solution)/shard_map/ppermute | solution.py:555
  157.6 30.3 %collective-permute-start.8 = (bf16[2,2,128,128]{3,2,1,0:T(8,128)(2,1)S(1)}, bf16[2,2,128,128]{3,2,1,0:T(8,128)(2,1)S(1)}, u32[]{:S(2)}, u32[]{:S(2)}) collective-permute-start(bf16[2,2,128,128]{3,2,1,0:T(8,128)(2,1)S(1)} %pick_cross.1), channel_id=1, source_target_pairs={{0,128},{16,144},{32,160},{48,176},{64,192},{80,208},{96,224},{112... | collective-permute-start | bytes 393224 | tf_op jit(solution)/shard_map/ppermute | solution.py:555
  163.2 3.7 collective-permute-start
  193.3 13.5 %collective-permute-start.9 = (bf16[2,2,128,128]{3,2,1,0:T(8,128)(2,1)S(1)}, bf16[2,2,128,128]{3,2,1,0:T(8,128)(2,1)S(1)}, u32[]{:S(2)}, u32[]{:S(2)}) collective-permute-start(bf16[2,2,128,128]{3,2,1,0:T(8,128)(2,1)S(1)} %attend_thirds.1.own_in), channel_id=1, source_target_pairs={{0,128},{16,144},{32,160},{48,176},{64,192},{80,208},{96,224},{112... | collective-permute-start | bytes 393224 | tf_op jit(solution)/shard_map/ppermute | solution.py:555
  207.5 14.8 %copy-start.8 = (bf16[2,128,128]{2,1,0:T(8,128)(2,1)S(1)}, bf16[2,128,128]{2,1,0:T(8,128)(2,1)}, u32[]{:S(2)}) copy-start(bf16[2,128,128]{2,1,0:T(8,128)(2,1)} %get-tuple-element.59) | copy-start | bytes 196612
  207.5 75.9 %copy-start.1 = (f32[16,2,128,128]{3,2,1,0:T(8,128)S(1)}, f32[16,2,128,128]{3,2,1,0:T(8,128)}, u32[]{:S(2)}) copy-start(f32[16,2,128,128]{3,2,1,0:T(8,128)} %get-tuple-element.56.sum_ref) | copy-start | bytes 6291460
  207.5 78.6 %all-to-all-start.2 = ((bf16[32,2,128,128]{3,2,1,0:T(8,128)(2,1)}), bf16[32,2,128,128]{3,2,1,0:T(8,128)(2,1)}, u32[]{:S(2)}, u32[]{:S(2)}) async-start(bf16[32,2,128,128]{3,2,1,0:T(8,128)(2,1)} %get-tuple-element.70), calls=%async_computation.2 | async-start | bytes 4194304 | tf_op jit(solution)/shard_map/all_to_all | solution.py:552
  221.1 23.9 %collective-permute-start.11 = (bf16[2,2,128,128]{3,2,1,0:T(8,128)(2,1)S(1)}, bf16[2,2,128,128]{3,2,1,0:T(8,128)(2,1)S(1)}, u32[]{:S(2)}, u32[]{:S(2)}) collective-permute-start(bf16[2,2,128,128]{3,2,1,0:T(8,128)(2,1)S(1)} %get-tuple-element.63), channel_id=1, source_target_pairs={{0,112},{16,0},{32,16},{48,32},{64,48},{80,64},{96,80},{112,96},{1... | collective-permute-start | bytes 393224 | tf_op jit(solution)/shard_map/ppermute | solution.py:555
  221.8 46.0 %collective-permute-start.12 = (bf16[2,2,128,128]{3,2,1,0:T(8,128)(2,1)S(1)}, bf16[2,2,128,128]{3,2,1,0:T(8,128)(2,1)S(1)}, u32[]{:S(2)}, u32[]{:S(2)}) collective-permute-start(bf16[2,2,128,128]{3,2,1,0:T(8,128)(2,1)S(1)} %get-tuple-element.64), channel_id=1, source_target_pairs={{0,96},{16,112},{32,0},{48,16},{64,32},{80,48},{96,64},{112,80},{1... | collective-permute-start | bytes 393224 | tf_op jit(solution)/shard_map/ppermute | solution.py:555
  222.3 22.7 %collective-permute-start.10 = (bf16[2,128,128]{2,1,0:T(8,128)(2,1)S(1)}, bf16[2,128,128]{2,1,0:T(8,128)(2,1)S(1)}, u32[]{:S(2)}, u32[]{:S(2)}) collective-permute-start(bf16[2,128,128]{2,1,0:T(8,128)(2,1)S(1)} %copy-done.8), channel_id=1, source_target_pairs={{0,240},{16,0},{32,16},{48,32},{64,48},{80,64},{96,80},{112,96},{1... | collective-permute-start | bytes 196616 | tf_op jit(solution)/shard_map/ppermute | solution.py:555
  222.5 52.7 %collective-permute-start.13 = (bf16[2,2,128,128]{3,2,1,0:T(8,128)(2,1)S(1)}, bf16[2,2,128,128]{3,2,1,0:T(8,128)(2,1)S(1)}, u32[]{:S(2)}, u32[]{:S(2)}) collective-permute-start(bf16[2,2,128,128]{3,2,1,0:T(8,128)(2,1)S(1)} %get-tuple-element.65), channel_id=1, source_target_pairs={{0,80},{16,96},{32,112},{48,0},{64,16},{80,32},{96,48},{112,64},{1... | collective-permute-start | bytes 393224 | tf_op jit(solution)/shard_map/ppermute | solution.py:555
  225.6 49.6 %collective-permute-start.14 = (bf16[2,2,128,128]{3,2,1,0:T(8,128)(2,1)S(1)}, bf16[2,2,128,128]{3,2,1,0:T(8,128)(2,1)S(1)}, u32[]{:S(2)}, u32[]{:S(2)}) collective-permute-start(bf16[2,2,128,128]{3,2,1,0:T(8,128)(2,1)S(1)} %get-tuple-element.66), channel_id=1, source_target_pairs={{0,64},{16,80},{32,96},{48,112},{64,0},{80,16},{96,32},{112,48},{1... | collective-permute-start | bytes 393224 | tf_op jit(solution)/shard_map/ppermute | solution.py:555
  245.0 30.1 %collective-permute-start.15 = (bf16[2,2,128,128]{3,2,1,0:T(8,128)(2,1)S(1)}, bf16[2,2,128,128]{3,2,1,0:T(8,128)(2,1)S(1)}, u32[]{:S(2)}, u32[]{:S(2)}) collective-permute-start(bf16[2,2,128,128]{3,2,1,0:T(8,128)(2,1)S(1)} %get-tuple-element.67), channel_id=1, source_target_pairs={{0,48},{16,64},{32,80},{48,96},{64,112},{80,0},{96,16},{112,32},{1... | collective-permute-start | bytes 393224 | tf_op jit(solution)/shard_map/ppermute | solution.py:555
  245.1 38.3 %collective-permute-start.16 = (bf16[2,2,128,128]{3,2,1,0:T(8,128)(2,1)S(1)}, bf16[2,2,128,128]{3,2,1,0:T(8,128)(2,1)S(1)}, u32[]{:S(2)}, u32[]{:S(2)}) collective-permute-start(bf16[2,2,128,128]{3,2,1,0:T(8,128)(2,1)S(1)} %get-tuple-element.68), channel_id=1, source_target_pairs={{0,32},{16,48},{32,64},{48,80},{64,96},{80,112},{96,0},{112,16},{1... | collective-permute-start | bytes 393224 | tf_op jit(solution)/shard_map/ppermute | solution.py:555
  267.8 15.6 %collective-permute-start.17 = (bf16[2,2,128,128]{3,2,1,0:T(8,128)(2,1)S(1)}, bf16[2,2,128,128]{3,2,1,0:T(8,128)(2,1)S(1)}, u32[]{:S(2)}, u32[]{:S(2)}) collective-permute-start(bf16[2,2,128,128]{3,2,1,0:T(8,128)(2,1)S(1)} %get-tuple-element.69), channel_id=1, source_target_pairs={{0,16},{16,32},{32,48},{48,64},{64,80},{80,96},{96,112},{112,0},{1... | collective-permute-start | bytes 393224 | tf_op jit(solution)/shard_map/ppermute | solution.py:555
  (6 other events, 27.0 us)
